TPU v7x, 128 devices: a whole 4x4x4 slice. The times are simulated.
128 devices in a mesh: slab: 32 (over z, y, x_lo), grid: 4 (over x_hi, core).
Axes of the slice: x: 4 (x_hi: 2, x_lo: 2; x = x_hi * 2 + x_lo), y: 4, z: 4, core: 2. Of those that a mesh axis runs over, the one named last changes fastest.
Arguments:
- eigvecs: float32 [2048, 65536], P('slab', 'grid'), may hold values from -6 to 6
- panel_one: bfloat16 [256, 65536], P('slab', 'grid'), may hold values from -0.0234375 to 0.0234375
- panel_two: bfloat16 [256, 65536], P('slab', 'grid'), may hold values from -0.0234375 to 0.0234375
- factor_one: float32 [256, 256], replicated
- factor_two: float32 [256, 256], replicated
- occupations: float32 [2048], P('slab'), may hold values from 0.3 to 3
- occupied_count: int32 [1], replicated, may hold values from 1024 to 2048
- row_offset: int32 [1], replicated, may hold values from 0 to 61440
Outputs:
- orbitals_out: float32 [2048, 65536], P('slab', 'grid')
- density: float32 [4096, 4, 16384], P('grid', None, 'slab')
All inputs are finite; a program needn't handle non-finite values.
Results may differ from a plain program's by a relative error of at most 0.01.
Values may be sent and summed in bfloat16 or wider, within the bound.
No kernel may reach another device: no remote copies, remote signals or barrier semaphores. Data moves between devices by JAX's collectives and lax.ppermute only.
A program may use at most 128 MiB of HBM per device.

v0:
```python
import math

import jax
import jax.numpy as jnp
from jax import lax
from jax.sharding import PartitionSpec as P

OCC = 2048
R = 4096


def right_transpose(left, right):
    return lax.dot_general(left, right, (((1,), (1,)), ((), ())), precision=lax.Precision.HIGHEST)


def split_three(values):
    high = values.astype(jnp.bfloat16)
    rest = values - high.astype(jnp.float32)
    middle = rest.astype(jnp.bfloat16)
    low = (rest - middle.astype(jnp.float32)).astype(jnp.bfloat16)
    return (high, middle, low)


def split_dot(values, vectors, numbers):
    total = None
    for piece in split_three(values):
        term = lax.dot_general(piece, vectors, numbers, preferred_element_type=jnp.float32)
        total = term if total is None else total + term
    return total


def project_on(orbs, vectors):
    return split_dot(orbs, vectors, (((1,), (1,)), ((), ())))


def expand_by(coeffs, vectors):
    return split_dot(coeffs, vectors, (((1,), (0,)), ((), ())))


def body(
    eigvecs, panel_one, panel_two, factor_one, factor_two, occupations, occupied_count, row_offset
):
    local_orbs = eigvecs.shape[0]
    local_basis = eigvecs.shape[1]
    orbs = eigvecs
    for panel, factor in ((panel_one, factor_one), (panel_two, factor_two)):
        vectors = lax.all_gather(panel, "slab", axis=0, tiled=True)
        partial_proj = project_on(orbs, vectors)
        project = lax.psum(partial_proj, "grid")
        coeffs = right_transpose(project, factor)
        orbs = orbs - expand_by(coeffs, vectors)
    orbital_index = lax.axis_index("slab") * local_orbs + jnp.arange(local_orbs, dtype=jnp.int32)
    weight = jnp.where(
        orbital_index < occupied_count[0], occupations / math.sqrt(OCC), jnp.float32(0.0)
    )
    orbitals = orbs.astype(jnp.bfloat16)
    weighted = (orbs * weight[:, None]).astype(jnp.bfloat16)
    padding = jnp.zeros((local_orbs, R), jnp.bfloat16)
    padded = jnp.concatenate([padding, orbitals, padding], axis=1)
    start = row_offset[0] - lax.axis_index("grid") * local_basis + R
    start = jnp.clip(start, 0, local_basis + R)
    window_piece = lax.dynamic_slice_in_dim(padded, start, R, 1)
    row_block = lax.all_to_all(weighted, "slab", split_axis=1, concat_axis=0, tiled=True)
    block_len = row_block.shape[1]
    window_all = lax.psum(window_piece.astype(jnp.float32).astype(jnp.bfloat16), "grid")
    tile = lax.dot_general(
        lax.all_gather(window_all, "slab", axis=0, tiled=True),
        row_block,
        (((0,), (0,)), ((), ())),
        preferred_element_type=jnp.float32,
    )
    density = lax.all_to_all(
        tile.reshape(R, 1, block_len), "grid", split_axis=0, concat_axis=1, tiled=True
    )
    return (orbs, density)


def solution(mesh):
    in_specs = (
        P("slab", "grid"),
        P("slab", "grid"),
        P("slab", "grid"),
        P(),
        P(),
        P("slab"),
        P(),
        P(),
    )
    out_specs = (P("slab", "grid"), P("grid", None, "slab"))
    return jax.shard_map(body, mesh=mesh, in_specs=in_specs, out_specs=out_specs, check_vma=False)
```

profile of v0, /device:TPU:1, one launch (start us, length us, event | category | flops | bytes accessed | tf_op | source)
XLA Modules:
  0.0 1090.2 jit_solution(8445762761695643908)
XLA Ops:
  7.2 0.0 copy-start
  7.2 0.0 all-gather.4.cloned.1.call-start
  7.2 0.7 all-gather.4.cloned.1.call-update
  7.9 0.0 all-reduce.4.cloned.1.call-start
  8.0 195.0 %all-gather.4.cloned.1.call-done = bf16[256,16384]{1,0:T(8,128)(2,1)} async-done(((bf16[8,16384]{1,0:T(8,128)(2,1)}), bf16[256,16384]{1,0:T(8,128)(2,1)}) %all-gather.4.cloned.1.call-update) | async-done | bytes 8388624 | tf_op jit(solution)/shard_map/all_gather | solution.py:47
  203.0 8.7 fusion.12
  211.7 0.7 copy-done.6
  212.4 2.7 fusion.5
  215.1 3.3 fusion.23
  218.4 0.0 all-reduce.4.cloned.1.call-update
  218.4 0.0 all-gather.6.cloned.1.call-start
  218.4 0.7 all-gather.6.cloned.1.call-update
  219.1 0.2 all-reduce.6.cloned.1.call-start
  220.0 36.6 %all-reduce.4.cloned.1.call-done = f32[64,256]{1,0:T(8,128)} async-done(((f32[64,256]{1,0:T(8,128)}), f32[64,256]{1,0:T(8,128)}) %all-reduce.4.cloned.1.call-update) | async-done | bytes 65552 | tf_op jit(solution)/shard_map/psum | solution.py:49
  256.7 1.2 fusion.36
  257.9 5.1 fusion.29
  263.0 0.0 copy-start.7
  263.0 5.1 convolution_add_fusion.3
  268.1 0.8 copy-done.7
  268.9 3.6 fusion
  272.5 174.9 %all-gather.6.cloned.1.call-done = bf16[256,16384]{1,0:T(8,128)(2,1)} async-done(((bf16[8,16384]{1,0:T(8,128)(2,1)}), bf16[256,16384]{1,0:T(8,128)(2,1)}) %all-gather.6.cloned.1.call-update) | async-done | bytes 8388624 | tf_op jit(solution)/shard_map/all_gather | solution.py:47
  447.5 8.7 fusion.13
  456.2 0.7 copy-done.4
  456.9 2.7 fusion.10
  459.6 0.0 copy-start.9
  459.6 0.0 copy-start.8
  459.6 3.3 fusion.17
  462.9 0.0 all-reduce.6.cloned.1.call-update
  462.9 0.3 all-reduce.8.cloned.1.call-start
  463.9 37.3 %all-reduce.6.cloned.1.call-done = f32[64,256]{1,0:T(8,128)} async-done(((f32[64,256]{1,0:T(8,128)}), f32[64,256]{1,0:T(8,128)}) %all-reduce.6.cloned.1.call-update) | async-done | bytes 65552 | tf_op jit(solution)/shard_map/psum | solution.py:49
  501.2 1.2 fusion.37
  502.4 5.1 fusion.33
  507.5 0.0 copy-start.5
  507.5 5.1 convolution_add_fusion.1
  512.6 0.7 copy-done.5
  513.4 4.3 multiply_convert_fusion
  517.7 1.4 fusion.27
  519.1 0.0 all-reduce.8.cloned.1.call-update
  519.2 0.0 all-gather.8.cloned.1.call-start
  519.2 41.7 %all-reduce.8.cloned.1.call-done = bf16[64,4096]{1,0:T(8,128)(2,1)} async-done(((bf16[64,4096]{1,0:T(8,128)(2,1)}), bf16[64,4096]{1,0:T(8,128)(2,1)}) %all-reduce.8.cloned.1.call-update) | async-done | bytes 524304 | tf_op jit(solution)/shard_map/psum | solution.py:65
  560.9 0.0 all-gather.8.cloned.1.call-update
  560.9 0.3 copy.20
  561.2 55.1 %all_to_all.37 = bf16[64,32,512]{2,0,1:T(8,128)(2,1)S(1)} all-to-all(bf16[64,32,512]{2,0,1:T(8,128)(2,1)S(1)} %bitcast.43), channel_id=1, replica_groups=mesh['slab'=32,'grid'=4] {'slab'}, dimensions={1} | all-to-all | bytes 4194304 | tf_op jit(solution)/shard_map/all_to_all | solution.py:63
  616.2 329.6 %all-gather.8.cloned.1.call-done = bf16[2048,4096]{1,0:T(8,128)(2,1)} async-done(((bf16[64,4096]{1,0:T(8,128)(2,1)}), bf16[2048,4096]{1,0:T(8,128)(2,1)}) %all-gather.8.cloned.1.call-update) | async-done | bytes 16777232 | tf_op jit(solution)/shard_map/all_gather | solution.py:67
  945.8 11.7 %convolution_bitcast_fusion = f32[4096,1,512]{2,0,1:T(8,128)S(1)} fusion(bf16[2048,4096]{1,0:T(8,128)(2,1)} %all-gather.8.cloned.1.call-done, bf16[2048,512]{1,0:T(8,128)(2,1)S(1)} %bitcast.45), kind=kOutput, calls=%fused_computation.7 | convolution fusion | flops 8589934592 | bytes 27262976 | tf_op jit(solution)/shard_map/dot_general | solution.py:66
  957.5 15.9 %copy.14 = f32[4096,1,512]{2,1,0:T(1,128)S(1)} copy(f32[4096,1,512]{2,0,1:T(8,128)S(1)} %convolution_bitcast_fusion) | data formatting | bytes 16777216 | tf_op jit(solution)/shard_map/reshape | solution.py:73
  973.3 97.8 %all_to_all.38 = f32[4096,1,512]{2,1,0:T(1,128)} all-to-all(f32[4096,1,512]{2,1,0:T(1,128)S(1)} %copy.14), channel_id=1, replica_groups=mesh['slab'=32,'grid'=4] {'grid'}, dimensions={0} | all-to-all | bytes 16777216 | tf_op jit(solution)/shard_map/all_to_all | solution.py:72
  1071.2 12.2 %copy.19 = f32[4,1024,1,512]{3,0,1,2:T(4,128)} copy(f32[4,1024,1,512]{3,2,1,0:T(1,128)} %bitcast.41) | data formatting | bytes 16777216 | tf_op jit(solution)/shard_map/all_to_all | solution.py:72
  (23 shorter events, 0.1 us)
Async XLA Ops:
  7.2 249.5 %copy-start = (f32[256,256]{1,0:T(8,128)S(1)}, f32[256,256]{1,0:T(8,128)}, u32[]{:S(2)}) copy-start(f32[256,256]{1,0:T(8,128)} %param.11) | copy-start | bytes 786436
  7.2 195.8 %all-gather.4.cloned.1.call-start = ((), (), s32[]{:S(2)}) async-start(), calls=%async_computation.2 | async-start | bytes 8650752 | tf_op jit(solution)/shard_map/all_gather | solution.py:47
  7.9 248.7 %all-reduce.4.cloned.1.call-start = ((), (), s32[]{:S(2)}) async-start(), calls=%async_computation.3 | async-start | bytes 131072 | tf_op jit(solution)/shard_map/psum | solution.py:49
  203.0 8.7 copy-start.3
  203.0 9.4 copy-start.6
  218.4 229.1 %all-gather.6.cloned.1.call-start = ((), (), s32[]{:S(2)}) async-start(), calls=%async_computation.4 | async-start | bytes 8650752 | tf_op jit(solution)/shard_map/all_gather | solution.py:47
  219.1 282.1 %all-reduce.6.cloned.1.call-start = ((), (), s32[]{:S(2)}) async-start(), calls=%async_computation.5 | async-start | bytes 131072 | tf_op jit(solution)/shard_map/psum | solution.py:49
  257.9 10.3 slice-start.2
  263.0 5.2 slice-start.3
  263.0 5.9 copy-start.7
  447.5 8.7 copy-start.2
  447.5 9.4 copy-start.4
  459.6 3.6 copy-start.9
  459.6 41.6 %copy-start.8 = (f32[256,256]{1,0:T(8,128)S(1)}, f32[256,256]{1,0:T(8,128)}, u32[]{:S(2)}) copy-start(f32[256,256]{1,0:T(8,128)} %param.12) | copy-start | bytes 786436
  462.9 98.0 %all-reduce.8.cloned.1.call-start = ((), (), s32[]{:S(2)}) async-start(), calls=%async_computation.6 | async-start | bytes 1048576 | tf_op jit(solution)/shard_map/psum | solution.py:65
  502.4 10.2 slice-start
  507.5 5.1 slice-start.1
  507.5 5.8 copy-start.5
  519.2 426.6 %all-gather.8.cloned.1.call-start = ((), (), s32[]{:S(2)}) async-start(), calls=%async_computation.7 | async-start | bytes 17301504 | tf_op jit(solution)/shard_map/all_gather | solution.py:67
  1071.2 12.2 %copy-start.1 = (f32[256,256]{1,0:T(8,128)S(1)}, f32[256,256]{1,0:T(8,128)}, u32[]{:S(2)}) copy-start(f32[256,256]{1,0:T(8,128)} %param.11) | copy-start | bytes 786436
Sparse Core Ops, SparseCore 0:
  9.7 193.2 all-gather.3
  218.5 38.0 all-reduce.3
  258.4 189.0 all-gather.5
  463.0 38.1 all-reduce.5
  519.3 41.5 all-reduce.7
  562.4 383.3 all-gather.7
where the time goes:
time: 1090 us
  waiting for transfers between devices  817 us (75%)
  blocking collectives  153 us (14%)
  matrix products  71.6 us (7%)
  local copies, waits for them, and re-layouts  31.4 us (3%)
  between operations  15.6 us (1%)
    all_gather x2, waiting for transfers between devices, body(): vectors = lax.all_gather(panel, 'slab', axis=0, tiled=True)  370 us
    all_gather x1, waiting for transfers between devices, body(): lax.all_gather(window_all, 'slab', axis=0, tiled=True)  330 us
    all_to_all x1, blocking collectives, body(): lax.all_to_all(tile.reshape(R, 1, block_len), 'grid', split_axis=0, conca...  97.8 us
    psum x2, waiting for transfers between devices, body(): project = lax.psum(partial_proj, 'grid')  74 us
    dot_general x12, matrix products, split_dot(): lax.dot_general(piece, vectors, numbers, preferred_element_type=jnp.float32)  57.6 us
    all_to_all x1, blocking collectives, body(): lax.all_to_all(weighted, 'slab', split_axis=1, concat_axis=0, tiled=True)  55.1 us
    psum x1, waiting for transfers between devices, body(): lax.psum(window_piece.astype(jnp.float32).astype(jnp.bfloat16), 'grid')  41.7 us
  transfers between devices with their start and end apart: 6, of which 6 were waited for; matrix products, arithmetic and copies ran while one was open for 1% of the time, Pallas kernels for 0%

commit v1 on v0

v1 whole, which is shorter than its diff:
```python
import math

import jax
import jax.numpy as jnp
from jax import lax
from jax.sharding import Mesh
from jax.sharding import PartitionSpec as P

OCC = 2048
R = 4096
ZY = ("z", "y")
TEAM = ("z", "y", "xh", "c")


def dot(left, right, dims, **kwargs):
    return lax.dot_general(
        left, right, (dims, ((), ())), preferred_element_type=jnp.float32, **kwargs
    )


def swap(values, axis):
    return lax.ppermute(values, axis, [(0, 1), (1, 0)])


def exchange(values, axes):
    return lax.all_to_all(values, axes, 0, 0, tiled=True)


def pick(first, second, flag):
    return jnp.where(flag == 0, first, second)


def body(
    eigvecs, panel_one, panel_two, factor_one, factor_two, occupations, occupied_count, row_offset
):
    bf16 = jnp.bfloat16
    xl, xh, c = (lax.axis_index(name) for name in ("xl", "xh", "c"))
    zy = lax.axis_index(ZY)
    n_orbs, n_basis = eigvecs.shape
    n_vec = panel_one.shape[0]
    chunk = n_basis // 16
    half = chunk // 2
    pw = factor_one.shape[0]
    rows = R // 4

    vecs = jnp.concatenate([panel_one, panel_two], axis=0)
    orbs16 = eigvecs.astype(bf16)

    with jax.named_scope("window_slice"):
        both = jnp.concatenate([orbs16, vecs], axis=0)
        pad = jnp.zeros((n_orbs + 2 * n_vec, R), bf16)
        padded = jnp.concatenate([pad, both, pad], axis=1)
        start = row_offset[0] - (xh * 2 + c) * n_basis + R

        def cut(part):
            at = jnp.clip(start, 0, n_basis + R) + part * 2 * rows
            return lax.dynamic_slice_in_dim(padded, at, 2 * rows, 1)

        sent = swap(cut(1 - xh), "xh")
        kept = cut(xh)

    with jax.named_scope("vectors"):
        occ_high = occupations.astype(bf16)
        rest = occupations - occ_high.astype(jnp.float32)
        occ_mid = rest.astype(bf16)
        occ_low = (rest - occ_mid.astype(jnp.float32)).astype(bf16)
        extra = jnp.zeros((2 * n_vec, 128), bf16)
        extra = extra.at[:3, :n_orbs].set(jnp.stack([occ_high, occ_mid, occ_low]))
        packed = vecs.reshape(2 * n_vec, 16, chunk).transpose(1, 0, 2)
        packed = jnp.concatenate(
            [packed, jnp.broadcast_to(extra[None], (16, 2 * n_vec, 128))], axis=2
        )
        got = exchange(packed, ZY)
        own = got[:, :, :chunk]
        occ = got[:, :3, chunk : chunk + n_orbs].astype(jnp.float32).sum(1).reshape(16 * n_orbs)
        other = swap(own, "xl")

        def order(own, other, width):
            shape = (16, 2, n_vec, width)
            own, other = own.reshape(shape), other.reshape(shape)
            pair = jnp.stack([pick(own, other, xl), pick(other, own, xl)], axis=1)
            return pair.transpose(2, 0, 1, 3, 4).reshape(2 * pw, width)

    with jax.named_scope("window_core"):
        four = kept + sent
        four = four.reshape(n_orbs + 2 * n_vec, 2, rows)
        mine = lax.dynamic_index_in_dim(four, c, 1, keepdims=False)
        mine = mine + swap(lax.dynamic_index_in_dim(four, 1 - c, 1, keepdims=False), "c")
        mine_x = swap(mine, "xl")

    with jax.named_scope("transpose_in"):
        orbs_t = exchange(orbs16.reshape(n_orbs, 16, chunk).transpose(1, 0, 2), ZY)
        orbs_t = orbs_t.reshape(16 * n_orbs, chunk)
        vec_t = order(own, other, chunk)

    with jax.named_scope("window_gather"):
        window = lax.all_gather(jnp.stack([mine, mine_x]), ZY, axis=0)

    with jax.named_scope("project"):
        proj = dot(orbs_t, vec_t, ((1,), (1,))).astype(bf16)
        cross = dot(vec_t[:pw], vec_t[pw:], ((1,), (1,))).astype(bf16)
        n_own = 16 * n_orbs // 64
        lanes = pw * pw // (64 * n_own)
        parts = jnp.concatenate(
            [proj.reshape(64, n_own, 2 * pw), cross.reshape(64, n_own, lanes)], axis=2
        )
        summed = exchange(parts, TEAM).astype(jnp.float32).sum(0)
        high = lax.Precision.HIGHEST
        first = dot(summed[:, :pw], factor_one, ((1,), (1,)), precision=high)
        second = dot(summed[:, pw : 2 * pw], factor_two, ((1,), (1,)), precision=high)
        share = jnp.concatenate([first, second, summed[:, 2 * pw :]], axis=1).astype(bf16)
        every = exchange(jnp.broadcast_to(share[None], (64,) + share.shape), TEAM)
        cross = every[:, :, 2 * pw :].reshape(pw, pw)
        first = every[:, :, :pw].reshape(16 * n_orbs, pw)
        second = every[:, :, pw : 2 * pw].reshape(16 * n_orbs, pw)
        mixed = dot(cross.astype(jnp.float32), factor_two, ((1,), (1,)), precision=high)
        second = second.astype(jnp.float32) - dot(first, mixed.astype(bf16), ((1,), (0,)))
        coeffs = jnp.concatenate([first, second.astype(bf16)], axis=1)

    with jax.named_scope("update"):
        update = dot(coeffs, vec_t, ((1,), (0,)))
        index = (
            (jnp.arange(16, dtype=jnp.int32)[:, None] * 2 + xl) * n_orbs
            + jnp.arange(n_orbs, dtype=jnp.int32)[None]
        ).reshape(16 * n_orbs)
        weight = jnp.where(index < occupied_count[0], occ / math.sqrt(OCC), jnp.float32(0.0))
        new_t = orbs_t.astype(jnp.float32) - update
        weighted = (new_t * weight[:, None]).astype(bf16)
        update16 = update.astype(bf16)

    with jax.named_scope("spread"):
        left, right = weighted[:, :half], weighted[:, half:]
        keep, give = pick(left, right, xl), pick(right, left, xl)
        flat = ("xl", "xh")
        w_same_oth = swap(give, "xl")
        w_diff_oth = lax.ppermute(give, flat, [(i, 3 - i) for i in range(4)])
        w_diff_own = swap(keep, "xh")
        coeffs_half = lax.dynamic_slice_in_dim(coeffs, c * 8 * n_orbs, 8 * n_orbs, 0)
        coeffs_x = swap(coeffs_half, "xl")
        coeffs_y = swap(coeffs_x, "c")
        coeffs_o = jnp.concatenate(
            [pick(coeffs_x, coeffs_y, c), pick(coeffs_y, coeffs_x, c)], axis=0
        )

    with jax.named_scope("transpose_out"):
        back = exchange(update16.reshape(16, n_orbs, chunk), ZY)
        out = eigvecs - back.transpose(1, 0, 2).reshape(n_orbs, n_basis).astype(jnp.float32)

    with jax.named_scope("window_rows"):
        win_vec = order(window[:, 0, n_orbs:], window[:, 1, n_orbs:], rows)

        def rotate(piece, factors):
            piece = piece.reshape(16 * n_orbs, rows).astype(jnp.float32)
            return (piece - dot(factors, win_vec, ((1,), (0,)))).astype(bf16)

        win_own = rotate(window[:, 0, :n_orbs], coeffs)
        win_oth = rotate(window[:, 1, :n_orbs], coeffs_o)

    with jax.named_scope("density"):
        pieces = []
        for one, two in ((keep, w_same_oth), (w_diff_own, w_diff_oth)):
            one_c, two_c = swap(one, "c"), swap(two, "c")
            a = dot(win_own, one, ((0,), (0,))) + dot(win_oth, two, ((0,), (0,)))
            b = dot(win_own, one_c, ((0,), (0,))) + dot(win_oth, two_c, ((0,), (0,)))
            pieces.append((pick(a, b, c), pick(b, a, c)))
        (s0, s1), (d0, d1) = pieces
        density = jnp.stack(
            [pick(s0, d0, xh), pick(s1, d1, xh), pick(d0, s0, xh), pick(d1, s1, xh)], axis=1
        )
    return (out, density)


def solution(mesh):
    mesh = Mesh(mesh.devices.reshape(4, 4, 2, 2, 2), ("z", "y", "xl", "xh", "c"))
    slab, grid = ("z", "y", "xl"), ("xh", "c")
    both = P(slab, grid)
    in_specs = (both, both, both, P(), P(), P(slab), P(), P())
    out_specs = (both, P(grid, None, slab))
    return jax.shard_map(body, mesh=mesh, in_specs=in_specs, out_specs=out_specs, check_vma=False)
```

time: 1090 us -> 296 us (0.27)
  waiting for transfers between devices: 817 us -> 119 us
  blocking collectives: 153 us -> 31.2 us
  starting transfers between devices: 0.64 us -> 39.6 us
  matrix products: 71.6 us -> 33.4 us
  other arithmetic: 1.44 us -> 22.8 us
    all_gather x3 -> x1, waiting for transfers between devices: 700 us -> 0.01 us  [body(): window = lax.all_gather(jnp.stack([mine, mine_x]), ZY, axis=0)]
    all_to_all x2 -> x1, blocking collectives: 153 us -> 31.2 us  [exchange(): return lax.all_to_all(values, axes, 0, 0, tiled=True)]
    psum x3 -> x0, waiting for transfers between devices: 116 us -> none  [the longest x2 74 us: body(): project = lax.psum(partial_proj, 'grid')]
    ppermute x0 -> x13, waiting for transfers between devices: none -> 64.9 us  [the longest x12 33.3 us: swap(): return lax.ppermute(values, axis, [(0, 1), (1, 0)])]
    all_to_all x0 -> x4, waiting for transfers between devices: none -> 53.6 us  [exchange(): return lax.all_to_all(values, axes, 0, 0, tiled=True)]
    dot_general x15 -> x17, matrix products: 71.6 us -> 33.4 us  [dot(): lax.dot_general(left, right, (dims, ((), ())), preferred_element_type=jnp...]
    all_to_all x0 -> x4, starting transfers between devices: none -> 23.8 us  [exchange(): return lax.all_to_all(values, axes, 0, 0, tiled=True)]
    unnamed x28 -> x35, local copies, waits for them, and re-layouts: 3.03 us -> 18.8 us
  transfers between devices with their start and end apart: 6 -> 18, of which waited for: 6 -> 10; matrix products, arithmetic and copies ran while one was open for 1% -> 19% of each run, Pallas kernels for 0% -> 0%
where the time goes in v1:
time: 296 us; the launch traced here: 295 us
  waiting for transfers between devices  119 us (40%)
  starting transfers between devices  39.6 us (13%)
  local copies, waits for them, and re-layouts  33.4 us (11%)
  matrix products  33.4 us (11%)
  blocking collectives  31.2 us (11%)
  other arithmetic  22.8 us (8%)
  between operations  16 us (5%)
    all_to_all x4, waiting for transfers between devices, exchange(): return lax.all_to_all(values, axes, 0, 0, tiled=True)  53.6 us
    dot_general x17, matrix products, dot(): lax.dot_general(left, right, (dims, ((), ())), preferred_element_type=jnp...  33.4 us
    ppermute x12, waiting for transfers between devices, swap(): return lax.ppermute(values, axis, [(0, 1), (1, 0)])  33.3 us
    ppermute x1, waiting for transfers between devices, body(): w_diff_oth = lax.ppermute(give, flat, [(i, 3 - i) for i in range(4)])  31.6 us
    all_to_all x1, blocking collectives, exchange(): return lax.all_to_all(values, axes, 0, 0, tiled=True)  31.2 us
    all_to_all x4, starting transfers between devices, exchange(): return lax.all_to_all(values, axes, 0, 0, tiled=True)  23.8 us
    unnamed x35, local copies, waits for them, and re-layouts  18.8 us
    ppermute x12, starting transfers between devices, swap(): return lax.ppermute(values, axis, [(0, 1), (1, 0)])  15.8 us
  transfers between devices with their start and end apart: 18, of which 10 were waited for; matrix products, arithmetic and copies ran while one was open for 19% of the time, Pallas kernels for 0%

profile of v1, /device:TPU:1, one launch (start us, length us, event | category | flops | bytes accessed | tf_op | source)
XLA Modules:
  0.0 295.0 jit_solution(933901895561901494)
XLA Ops:
  7.9 2.5 convert_element_type.92
  10.4 3.1 %pad_maximum_fusion.1 = bf16[80,24576]{1,0:T(8,128)(2,1)S(1)} fusion(bf16[80,4096]{1,0:T(8,128)(2,1)S(1)} %broadcast_in_dim.11, bf16[8,16384]{1,0:T(8,128)(2,1)S(1)} %copy-done.10, bf16[8,16384]{1,0:T(8,128)(2,1)S(1)} %copy-done.11, bf16[64,16384]{1,0:T(8,128)(2,1)S(1)} %convert_element_type.92), kind=kLoop, calls=%fused_computation.7 | loop fusion | flops 19660800 | bytes 7208960 | tf_op jit(solution)/shard_map/window_slice/concatenate | solution.py:52
  13.5 1.9 copy-done.3
  16.3 3.6 %collective-permute-start.1 = (bf16[80,2048]{1,0:T(8,128)(2,1)}, bf16[80,2048]{1,0:T(8,128)(2,1)}, u32[]{:S(2)}, u32[]{:S(2)}) collective-permute-start(bf16[80,2048]{1,0:T(8,128)(2,1)} %constant_dynamic-slice_fusion.2), channel_id=1, source_target_pairs={{0,2},{2,0},{1,3},{3,1},{4,6},{6,4},{5,7},{7,5},{8,10},{10,8},{9,1... | collective-permute-start | bytes 983048 | tf_op jit(solution)/shard_map/window_slice/ppermute | solution.py:22
  20.0 7.2 %collective-permute-done.1 = bf16[80,2048]{1,0:T(8,128)(2,1)} collective-permute-done((bf16[80,2048]{1,0:T(8,128)(2,1)}, bf16[80,2048]{1,0:T(8,128)(2,1)}, u32[]{:S(2)}, u32[]{:S(2)}) %collective-permute-start.1) | collective-permute-done | bytes 327712 | tf_op jit(solution)/shard_map/window_slice/ppermute | solution.py:22
  29.4 1.8 collective-permute-start.2
  32.3 1.5 collective-permute-start.3
  34.8 7.8 %all-to-all-start = ((bf16[16,16,1152]{2,1,0:T(8,128)(2,1)}), bf16[16,16,1152]{2,1,0:T(8,128)(2,1)S(1)}, u32[]{:S(2)}, u32[]{:S(2)}) async-start(bf16[16,16,1152]{2,1,0:T(8,128)(2,1)} %copy.47), calls=%async_computation | async-start | bytes 1179648 | tf_op jit(solution)/shard_map/vectors/all_to_all | solution.py:26
  43.4 1.6 copy.68
  45.0 8.7 %all-to-all-done = bf16[16,16,1152]{2,1,0:T(8,128)(2,1)S(1)} async-done(((bf16[16,16,1152]{2,1,0:T(8,128)(2,1)}), bf16[16,16,1152]{2,1,0:T(8,128)(2,1)S(1)}, u32[]{:S(2)}, u32[]{:S(2)}) %all-to-all-start) | async-done | bytes 589856 | tf_op jit(solution)/shard_map/vectors/all_to_all | solution.py:26
  53.7 3.7 %all-to-all-start.1 = ((bf16[16,64,1024]{2,1,0:T(8,128)(2,1)}), bf16[16,64,1024]{2,1,0:T(8,128)(2,1)S(1)}, u32[]{:S(2)}, u32[]{:S(2)}) async-start(bf16[16,64,1024]{2,1,0:T(8,128)(2,1)} %bitcast.102), calls=%async_computation.1 | async-start | bytes 4194304 | tf_op jit(solution)/shard_map/transpose_in/all_to_all | solution.py:26
  58.5 11.4 %collective-permute-done = bf16[16,16,1024]{2,1,0:T(8,128)(2,1)S(1)} collective-permute-done((bf16[16,16,1024]{2,1,0:T(8,128)(2,1)}, bf16[16,16,1024]{2,1,0:T(8,128)(2,1)S(1)}, u32[]{:S(2)}, u32[]{:S(2)}) %collective-permute-start) | collective-permute-done | bytes 524320 | tf_op jit(solution)/shard_map/vectors/ppermute | solution.py:22
  71.9 23.2 %all-to-all-done.1 = bf16[16,64,1024]{2,1,0:T(8,128)(2,1)S(1)} async-done(((bf16[16,64,1024]{2,1,0:T(8,128)(2,1)}), bf16[16,64,1024]{2,1,0:T(8,128)(2,1)S(1)}, u32[]{:S(2)}, u32[]{:S(2)}) %all-to-all-start.1) | async-done | bytes 2097184 | tf_op jit(solution)/shard_map/transpose_in/all_to_all | solution.py:26
  95.0 1.3 copy-done.6
  96.4 3.5 %fusion.2 = bf16[1024,512]{0,1:T(8,128)(2,1)} fusion(bf16[512,1024]{1,0:T(8,128)(2,1)} %bitcast.116, bf16[1024,1024]{1,0:T(8,128)(2,1)S(1)} %bitcast.108), kind=kOutput, calls=%fused_computation.19 | convolution fusion | flops 1074266112 | bytes 4194304 | tf_op jit(solution)/shard_map/project/dot_general | solution.py:16
  99.8 1.5 copy.50
  101.5 31.2 %all_to_all.25 = bf16[64,16,576]{2,1,0:T(8,128)(2,1)S(1)} all-to-all(bf16[64,16,576]{2,1,0:T(8,128)(2,1)S(1)} %pad_maximum_fusion.2), channel_id=1, replica_groups=mesh['z'=4,'y'=4,'xl'=2,'xh'=2,'c'=2] {'z','y','xh','c'}, dimensions={0} | all-to-all | bytes 2359296 | tf_op jit(solution)/shard_map/project/all_to_all | solution.py:26
  134.8 8.4 %all-to-all-start.3 = ((bf16[64,16,576]{2,1,0:T(8,128)(2,1)}), bf16[64,16,576]{2,1,0:T(8,128)(2,1)S(1)}, u32[]{:S(2)}, u32[]{:S(2)}) async-start(bf16[64,16,576]{2,1,0:T(8,128)(2,1)} %broadcast_in_dim.10), calls=%async_computation.3 | async-start | bytes 2621440 | tf_op jit(solution)/shard_map/project/all_to_all | solution.py:26
  144.1 21.8 %all-to-all-done.3 = bf16[64,16,576]{2,1,0:T(8,128)(2,1)S(1)} async-done(((bf16[64,16,576]{2,1,0:T(8,128)(2,1)}), bf16[64,16,576]{2,1,0:T(8,128)(2,1)S(1)}, u32[]{:S(2)}, u32[]{:S(2)}) %all-to-all-start.3) | async-done | bytes 1179680 | tf_op jit(solution)/shard_map/project/all_to_all | solution.py:26
  167.0 1.6 copy.53
  170.8 4.8 %multiply_convert_fusion = (bf16[1024,1024]{1,0:T(8,128)(2,1)}, bf16[1024,1024]{1,0:T(8,128)(2,1)}) fusion(f32[1024]{0:T(1024)S(1)} %select_n.169, bf16[16,64,1024]{2,1,0:T(8,128)(2,1)S(1)} %copy-done.7, bf16[512,1024]{1,0:T(8,128)(2,1)} %bitcast.117, bf16[1024,256]{0,1:T(8,128)(2,1)S(1)} %fusion.3, bf16[1024,256]{0,1:T(8,128)(2,1)S(1)} %copy.54), kind=kOutput, calls=%fused_computation.6 | convolution fusion | flops 1081081856 | bytes 8392704 | tf_op jit(solution)/shard_map/update/dot_general | solution.py:16
  175.7 3.9 %all-to-all-start.4 = ((bf16[16,64,1024]{2,1,0:T(8,128)(2,1)}), bf16[16,64,1024]{2,1,0:T(8,128)(2,1)S(1)}, u32[]{:S(2)}, u32[]{:S(2)}) async-start(bf16[16,64,1024]{2,1,0:T(8,128)(2,1)} %bitcast.109), calls=%async_computation.4 | async-start | bytes 4194304 | tf_op jit(solution)/shard_map/transpose_out/all_to_all | solution.py:26
  179.7 3.0 %broadcast_select_fusion = (bf16[1024,512]{1,0:T(8,128)(2,1)}, bf16[1024,512]{1,0:T(8,128)(2,1)}) fusion(pred[]{:T(512)S(6)} %eq.6, bf16[1024,1024]{1,0:T(8,128)(2,1)} %get-tuple-element.32), kind=kLoop, calls=%fused_computation.35 | loop fusion | flops 1048576 | bytes 4194305 | tf_op jit(solution)/shard_map/spread/jit(_where)/select_n | solution.py:30
  182.8 3.2 %collective-permute-start.9 = (bf16[1024,512]{1,0:T(8,128)(2,1)}, bf16[1024,512]{1,0:T(8,128)(2,1)}, u32[]{:S(2)}, u32[]{:S(2)}) collective-permute-start(bf16[1024,512]{1,0:T(8,128)(2,1)} %get-tuple-element.35), channel_id=1, source_target_pairs={{0,2},{2,0},{1,3},{3,1},{4,6},{6,4},{5,7},{7,5},{8,10},{10,8},{9,1... | collective-permute-start | bytes 3145736 | tf_op jit(solution)/shard_map/spread/ppermute | solution.py:22
  186.0 6.7 %collective-permute-done.4 = bf16[512,512]{0,1:T(8,128)(2,1)} collective-permute-done((bf16[512,512]{0,1:T(8,128)(2,1)S(1)}, bf16[512,512]{0,1:T(8,128)(2,1)}, u32[]{:S(2)}, u32[]{:S(2)}) %collective-permute-start.4) | collective-permute-done | bytes 524320 | tf_op jit(solution)/shard_map/spread/ppermute | solution.py:22
  192.7 2.5 collective-permute-start.5
  195.2 1.9 collective-permute-done.5
  197.1 2.2 broadcast_select_fusion.7
  199.3 31.6 %collective-permute-done.10 = bf16[1024,512]{1,0:T(8,128)(2,1)} collective-permute-done((bf16[1024,512]{1,0:T(8,128)(2,1)}, bf16[1024,512]{1,0:T(8,128)(2,1)}, u32[]{:S(2)}, u32[]{:S(2)}) %collective-permute-start.10) | collective-permute-done | bytes 1048608 | tf_op jit(solution)/shard_map/spread/ppermute | solution.py:136
  230.9 1.4 collective-permute-start.12
  232.3 5.4 %collective-permute-done.6 = bf16[1024,512]{1,0:T(8,128)(2,1)} collective-permute-done((bf16[1024,512]{1,0:T(8,128)(2,1)}, bf16[1024,512]{1,0:T(8,128)(2,1)}, u32[]{:S(2)}, u32[]{:S(2)}) %collective-permute-start.6) | collective-permute-done | bytes 1048608 | tf_op jit(solution)/shard_map/spread/ppermute | solution.py:22
  237.7 1.4 collective-permute-start.8
  239.9 1.9 copy-done.2
  241.8 2.4 sub.33
  244.3 1.3 select_bitcast_fusion.5
  245.5 2.7 fusion.23
  248.5 1.4 fusion.1
  249.9 1.3 fusion
  251.2 2.5 fusion.26
  253.7 2.5 fusion.28
  256.2 2.5 convolution_add_fusion.1
  258.8 2.5 fusion.27
  261.3 2.5 fusion.29
  263.8 2.5 convolution_add_fusion.3
  266.3 2.5 convolution_add_fusion
  268.9 3.3 %select_bitcast_fusion.3 = (f32[1024,1,512]{2,0,1:T(8,128)S(1)}, f32[1024,1,512]{2,0,1:T(8,128)S(1)}, f32[1024,1,512]{2,0,1:T(8,128)S(1)}, f32[1024,1,512]{2,0,1:T(8,128)S(1)}) fusion(pred[]{:T(512)S(6)} %eq.7, f32[1024,512]{1,0:T(8,128)S(1)} %convolution_add_fusion.3, pred[]{:T(512)S(6)} %eq.8, f32[1024,512]{1,0:T(8,128)S(1)} %convolution_add_fusion.1, ...), kind=kOutput, calls=%fused_computation.13 | convolution fusion | flops 1078460416 | bytes 19922946 | tf_op jit(solution)/shard_map/density/dot_general | solution.py:16
  272.1 3.8 %pad_maximum_fusion = f32[1024,4,512]{2,0,1:T(8,128)} fusion(f32[1024,1,512]{2,0,1:T(8,128)S(1)} %get-tuple-element.27, f32[1024,1,512]{2,0,1:T(8,128)S(1)} %get-tuple-element.26, f32[1024,1,512]{2,0,1:T(8,128)S(1)} %get-tuple-element.25, f32[1024,1,512]{2,0,1:T(8,128)S(1)} %get-tuple-element.24), kind=kLoop, calls=%fused_computation | loop fusion | flops 6291456 | bytes 16777216 | tf_op jit(solution)/shard_map/density/stack | solution.py:167
  275.9 12.2 %copy.58 = f32[1024,4,512]{2,1,0:T(4,128)} copy(f32[1024,4,512]{2,0,1:T(8,128)} %pad_maximum_fusion) | data formatting | bytes 16777216
  (93 shorter events, 16.0 us)
Async XLA Ops:
  7.2 125.8 %copy-start = (f32[256,256]{1,0:T(8,128)S(1)}, f32[256,256]{1,0:T(8,128)}, u32[]{:S(2)}) copy-start(f32[256,256]{1,0:T(8,128)} %param.14) | copy-start | bytes 786436
  7.9 2.5 copy-start.10
  7.9 2.5 copy-start.11
  13.5 1.9 copy-start.3
  16.3 14.9 %copy-start.15 = (f32[64]{0:T(128)S(1)}, f32[64]{0:T(128)}, u32[]{:S(2)}) copy-start(f32[64]{0:T(128)} %param.15) | copy-start | bytes 772
  16.3 10.8 %collective-permute-start.1 = (bf16[80,2048]{1,0:T(8,128)(2,1)}, bf16[80,2048]{1,0:T(8,128)(2,1)}, u32[]{:S(2)}, u32[]{:S(2)}) collective-permute-start(bf16[80,2048]{1,0:T(8,128)(2,1)} %constant_dynamic-slice_fusion.2), channel_id=1, source_target_pairs={{0,2},{2,0},{1,3},{3,1},{4,6},{6,4},{5,7},{7,5},{8,10},{10,8},{9,1... | collective-permute-start | bytes 983048 | tf_op jit(solution)/shard_map/window_slice/ppermute | solution.py:22
  29.4 2.8 collective-permute-start.2
  32.3 10.3 %collective-permute-start.3 = (bf16[80,1024]{1,0:T(8,128)(2,1)S(1)}, bf16[80,1024]{1,0:T(8,128)(2,1)S(1)}, u32[]{:S(2)}, u32[]{:S(2)}) collective-permute-start(bf16[80,1024]{1,0:T(8,128)(2,1)S(1)} %bitcast_add_fusion), channel_id=1, source_target_pairs={{0,4},{4,0},{1,5},{5,1},{2,6},{6,2},{3,7},{7,3},{8,12},{12,8},{9,1... | collective-permute-start | bytes 491528 | tf_op jit(solution)/shard_map/window_core/ppermute | solution.py:22
  34.8 18.9 %all-to-all-start = ((bf16[16,16,1152]{2,1,0:T(8,128)(2,1)}), bf16[16,16,1152]{2,1,0:T(8,128)(2,1)S(1)}, u32[]{:S(2)}, u32[]{:S(2)}) async-start(bf16[16,16,1152]{2,1,0:T(8,128)(2,1)} %copy.47), calls=%async_computation | async-start | bytes 1179648 | tf_op jit(solution)/shard_map/vectors/all_to_all | solution.py:26
  42.6 201.7 %all-gather.3.cloned.1.call-start = ((), (), s32[]{:S(2)}) async-start(), calls=%async_computation.5 | async-start | bytes 5570560 | tf_op jit(solution)/shard_map/window_gather/all_gather | solution.py:97
  53.7 41.4 %all-to-all-start.1 = ((bf16[16,64,1024]{2,1,0:T(8,128)(2,1)}), bf16[16,64,1024]{2,1,0:T(8,128)(2,1)S(1)}, u32[]{:S(2)}, u32[]{:S(2)}) async-start(bf16[16,64,1024]{2,1,0:T(8,128)(2,1)} %bitcast.102), calls=%async_computation.1 | async-start | bytes 4194304 | tf_op jit(solution)/shard_map/transpose_in/all_to_all | solution.py:26
  58.3 11.7 %collective-permute-start = (bf16[16,16,1024]{2,1,0:T(8,128)(2,1)}, bf16[16,16,1024]{2,1,0:T(8,128)(2,1)S(1)}, u32[]{:S(2)}, u32[]{:S(2)}) collective-permute-start(bf16[16,16,1024]{2,1,0:T(8,128)(2,1)} %slice.93), channel_id=1, source_target_pairs={{0,4},{4,0},{1,5},{5,1},{2,6},{6,2},{3,7},{7,3},{8,12},{12,8},{9,1... | collective-permute-start | bytes 1572872 | tf_op jit(solution)/shard_map/vectors/ppermute | solution.py:22
  95.0 1.3 copy-start.6
  101.5 31.8 %copy-start.14 = (f32[256,256]{1,0:T(8,128)S(1)}, f32[256,256]{1,0:T(8,128)}, u32[]{:S(2)}) copy-start(f32[256,256]{1,0:T(8,128)} %param.13) | copy-start | bytes 786436
  134.8 31.1 %all-to-all-start.3 = ((bf16[64,16,576]{2,1,0:T(8,128)(2,1)}), bf16[64,16,576]{2,1,0:T(8,128)(2,1)S(1)}, u32[]{:S(2)}, u32[]{:S(2)}) async-start(bf16[64,16,576]{2,1,0:T(8,128)(2,1)} %broadcast_in_dim.10), calls=%async_computation.3 | async-start | bytes 2621440 | tf_op jit(solution)/shard_map/project/all_to_all | solution.py:26
  169.0 6.6 %copy-start.8 = (bf16[1024,256]{0,1:T(8,128)(2,1)}, bf16[1024,256]{0,1:T(8,128)(2,1)S(1)}, u32[]{:S(2)}) copy-start(bf16[1024,256]{0,1:T(8,128)(2,1)S(1)} %copy.54) | copy-start | bytes 1572868
  169.1 1.8 copy-start.7
  170.8 4.8 %copy-start.4 = (bf16[1024,256]{0,1:T(8,128)(2,1)}, bf16[1024,256]{0,1:T(8,128)(2,1)S(1)}, u32[]{:S(2)}) copy-start(bf16[1024,256]{0,1:T(8,128)(2,1)S(1)} %fusion.3) | copy-start | bytes 1572868
  175.7 3.9 %copy-start.5 = (bf16[1024,256]{0,1:T(8,128)(2,1)S(1)}, bf16[1024,256]{0,1:T(8,128)(2,1)}, u32[]{:S(2)}) copy-start(bf16[1024,256]{0,1:T(8,128)(2,1)} %copy-done.4) | copy-start | bytes 1572868
  175.7 3.9 %copy-start.9 = (bf16[1024,256]{0,1:T(8,128)(2,1)S(1)}, bf16[1024,256]{0,1:T(8,128)(2,1)}, u32[]{:S(2)}) copy-start(bf16[1024,256]{0,1:T(8,128)(2,1)} %copy-done.8) | copy-start | bytes 1572868
  175.7 63.5 %all-to-all-start.4 = ((bf16[16,64,1024]{2,1,0:T(8,128)(2,1)}), bf16[16,64,1024]{2,1,0:T(8,128)(2,1)S(1)}, u32[]{:S(2)}, u32[]{:S(2)}) async-start(bf16[16,64,1024]{2,1,0:T(8,128)(2,1)} %bitcast.109), calls=%async_computation.4 | async-start | bytes 4194304 | tf_op jit(solution)/shard_map/transpose_out/all_to_all | solution.py:26
  179.6 13.1 %collective-permute-start.4 = (bf16[512,512]{0,1:T(8,128)(2,1)S(1)}, bf16[512,512]{0,1:T(8,128)(2,1)}, u32[]{:S(2)}, u32[]{:S(2)}) collective-permute-start(bf16[512,512]{0,1:T(8,128)(2,1)S(1)} %fusion.8), channel_id=1, source_target_pairs={{0,4},{4,0},{1,5},{5,1},{2,6},{6,2},{3,7},{7,3},{8,12},{12,8},{9,1... | collective-permute-start | bytes 1572872 | tf_op jit(solution)/shard_map/spread/ppermute | solution.py:22
  182.7 48.1 %collective-permute-start.10 = (bf16[1024,512]{1,0:T(8,128)(2,1)}, bf16[1024,512]{1,0:T(8,128)(2,1)}, u32[]{:S(2)}, u32[]{:S(2)}) collective-permute-start(bf16[1024,512]{1,0:T(8,128)(2,1)} %get-tuple-element.34), channel_id=1, source_target_pairs={{0,6},{2,4},{4,2},{6,0},{1,7},{3,5},{5,3},{7,1},{8,14},{10,12},{12... | collective-permute-start | bytes 3145736 | tf_op jit(solution)/shard_map/spread/ppermute | solution.py:136
  182.8 49.5 %collective-permute-start.9 = (bf16[1024,512]{1,0:T(8,128)(2,1)}, bf16[1024,512]{1,0:T(8,128)(2,1)}, u32[]{:S(2)}, u32[]{:S(2)}) collective-permute-start(bf16[1024,512]{1,0:T(8,128)(2,1)} %get-tuple-element.35), channel_id=1, source_target_pairs={{0,2},{2,0},{1,3},{3,1},{4,6},{6,4},{5,7},{7,5},{8,10},{10,8},{9,1... | collective-permute-start | bytes 3145736 | tf_op jit(solution)/shard_map/spread/ppermute | solution.py:22
  186.0 51.7 %collective-permute-start.6 = (bf16[1024,512]{1,0:T(8,128)(2,1)}, bf16[1024,512]{1,0:T(8,128)(2,1)}, u32[]{:S(2)}, u32[]{:S(2)}) collective-permute-start(bf16[1024,512]{1,0:T(8,128)(2,1)} %get-tuple-element.34), channel_id=1, source_target_pairs={{0,4},{4,0},{1,5},{5,1},{2,6},{6,2},{3,7},{7,3},{8,12},{12,8},{9,1... | collective-permute-start | bytes 3145736 | tf_op jit(solution)/shard_map/spread/ppermute | solution.py:22
  192.7 4.3 %collective-permute-start.5 = (bf16[512,512]{0,1:T(8,128)(2,1)}, bf16[512,512]{0,1:T(8,128)(2,1)}, u32[]{:S(2)}, u32[]{:S(2)}) collective-permute-start(bf16[512,512]{0,1:T(8,128)(2,1)} %collective-permute-done.4), channel_id=1, source_target_pairs={{0,1},{1,0},{2,3},{3,2},{4,5},{5,4},{6,7},{7,6},{8,9},{9,8},{10,11... | collective-permute-start | bytes 1572872 | tf_op jit(solution)/shard_map/spread/ppermute | solution.py:22
  195.2 63.6 %collective-permute-start.7 = (bf16[1024,512]{1,0:T(8,128)(2,1)}, bf16[1024,512]{1,0:T(8,128)(2,1)}, u32[]{:S(2)}, u32[]{:S(2)}) collective-permute-start(bf16[1024,512]{1,0:T(8,128)(2,1)} %get-tuple-element.35), channel_id=1, source_target_pairs={{0,1},{1,0},{2,3},{3,2},{4,5},{5,4},{6,7},{7,6},{8,9},{9,8},{10,11... | collective-permute-start | bytes 3145736 | tf_op jit(solution)/shard_map/density/ppermute | solution.py:22
  230.9 30.4 %collective-permute-start.12 = (bf16[1024,512]{1,0:T(8,128)(2,1)}, bf16[1024,512]{1,0:T(8,128)(2,1)}, u32[]{:S(2)}, u32[]{:S(2)}) collective-permute-start(bf16[1024,512]{1,0:T(8,128)(2,1)} %collective-permute-done.10), channel_id=1, source_target_pairs={{0,1},{1,0},{2,3},{3,2},{4,5},{5,4},{6,7},{7,6},{8,9},{9,8},{10,11... | collective-permute-start | bytes 3145736 | tf_op jit(solution)/shard_map/density/ppermute | solution.py:22
  232.3 34.0 %collective-permute-start.11 = (bf16[1024,512]{1,0:T(8,128)(2,1)}, bf16[1024,512]{1,0:T(8,128)(2,1)}, u32[]{:S(2)}, u32[]{:S(2)}) collective-permute-start(bf16[1024,512]{1,0:T(8,128)(2,1)} %collective-permute-done.9), channel_id=1, source_target_pairs={{0,1},{1,0},{2,3},{3,2},{4,5},{5,4},{6,7},{7,6},{8,9},{9,8},{10,11... | collective-permute-start | bytes 3145736 | tf_op jit(solution)/shard_map/density/ppermute | solution.py:22
  237.7 31.1 %collective-permute-start.8 = (bf16[1024,512]{1,0:T(8,128)(2,1)}, bf16[1024,512]{1,0:T(8,128)(2,1)}, u32[]{:S(2)}, u32[]{:S(2)}) collective-permute-start(bf16[1024,512]{1,0:T(8,128)(2,1)} %collective-permute-done.6), channel_id=1, source_target_pairs={{0,1},{1,0},{2,3},{3,2},{4,5},{5,4},{6,7},{7,6},{8,9},{9,8},{10,11... | collective-permute-start | bytes 3145736 | tf_op jit(solution)/shard_map/density/ppermute | solution.py:22
  239.6 2.2 copy-start.2
  248.5 1.4 copy-start.12
  248.5 1.4 copy-start.13
  275.9 12.2 %copy-start.1 = (f32[256,256]{1,0:T(8,128)S(1)}, f32[256,256]{1,0:T(8,128)}, u32[]{:S(2)}) copy-start(f32[256,256]{1,0:T(8,128)} %param.14) | copy-start | bytes 786436
Sparse Core Ops, SparseCore 0:
  45.5 91.1 all-gather.2

commit v2 on v1

v2 whole, which is shorter than its diff:
```python
import math

import jax
import jax.numpy as jnp
from jax import lax
from jax.experimental import pallas as pl
from jax.experimental.pallas import tpu as pltpu
from jax.sharding import Mesh
from jax.sharding import PartitionSpec as P

OCC = 2048
R = 4096
ZY = ("z", "y")
ZYC = ("z", "y", "c")
TILE = 256


def dot(left, right, dims, **kwargs):
    return lax.dot_general(
        left, right, (dims, ((), ())), preferred_element_type=jnp.float32, **kwargs
    )


def swap(values, axis):
    return lax.ppermute(values, axis, [(0, 1), (1, 0)])


def exchange(values, axes):
    return lax.all_to_all(values, axes, 0, 0, tiled=True)


def pick(first, second, flag):
    return jnp.where(flag == 0, first, second)


def body(
    eigvecs, panel_one, panel_two, factor_one, factor_two, occupations, occupied_count, row_offset
):
    bf16 = jnp.bfloat16
    xl, xh, c = (lax.axis_index(name) for name in ("xl", "xh", "c"))
    zy = lax.axis_index(ZY)
    n_orbs, n_basis = eigvecs.shape
    n_vec = panel_one.shape[0]
    chunk = n_basis // 16
    half = chunk // 2
    pw = factor_one.shape[0]
    rows = R // 4

    vecs = jnp.concatenate([panel_one, panel_two], axis=0)

    with jax.named_scope("vectors"):
        occ_high = occupations.astype(bf16)
        rest = occupations - occ_high.astype(jnp.float32)
        occ_mid = rest.astype(bf16)
        occ_low = (rest - occ_mid.astype(jnp.float32)).astype(bf16)
        extra = jnp.zeros((2 * n_vec, 128), bf16)
        extra = extra.at[:3, :n_orbs].set(jnp.stack([occ_high, occ_mid, occ_low]))
        packed = vecs.reshape(2 * n_vec, 16, chunk).transpose(1, 0, 2)
        packed = jnp.concatenate(
            [packed, jnp.broadcast_to(extra[None], (16, 2 * n_vec, 128))], axis=2
        )
        own = exchange(packed, ZY)
        other = swap(own, "xl")

        def order(own, other, width):
            shape = (16, 2, n_vec, width)
            own, other = own.reshape(shape), other.reshape(shape)
            pair = jnp.stack([pick(own, other, xl), pick(other, own, xl)], axis=1)
            return pair.transpose(2, 0, 1, 3, 4).reshape(2 * pw, width)

        def weight_of(got, side):
            occ = got[:, :3, chunk : chunk + n_orbs].astype(jnp.float32)
            occ = (occ[:, 0] + occ[:, 1]) + occ[:, 2]
            index = (jnp.arange(16, dtype=jnp.int32)[:, None] * 2 + side) * n_orbs
            index = index + jnp.arange(n_orbs, dtype=jnp.int32)[None]
            occ = jnp.where(index < occupied_count[0], occ / math.sqrt(OCC), jnp.float32(0.0))
            return occ.reshape(16 * n_orbs, 1)

        weight_own, weight_oth = weight_of(own, xl), weight_of(other, 1 - xl)
        vec_t = order(own[:, :, :chunk], other[:, :, :chunk], chunk)
        vec_half = lax.dynamic_slice_in_dim(vec_t, xl * half, half, 1)
        vec_half_x = swap(vec_half, "xh")
        vec_sides = [vec_half, swap(vec_half, "c"), vec_half_x, swap(vec_half_x, "c")]

    with jax.named_scope("window_exchange"):
        held, _ = lax.optimization_barrier((eigvecs, own))
        both = jnp.concatenate([held.astype(bf16), vecs], axis=0)
        pad = jnp.zeros((n_orbs + 2 * n_vec, R), bf16)
        padded = jnp.concatenate([pad, both, pad], axis=1)
        start = row_offset[0] - (xh * 2 + c) * n_basis + R

        def cut(part):
            at = jnp.clip(start, 0, n_basis + R) + part * 2 * rows
            return lax.dynamic_slice_in_dim(padded, at, 2 * rows, 1)

        four = cut(xh) + swap(cut(1 - xh), "xh")
        four = four.reshape(n_orbs + 2 * n_vec, 2, rows)
        mine = lax.dynamic_index_in_dim(four, c, 1, keepdims=False)
        mine = mine + swap(lax.dynamic_index_in_dim(four, 1 - c, 1, keepdims=False), "c")
        mine_x = swap(mine, "xl")

    with jax.named_scope("transpose_in"):
        orbs_t = exchange(eigvecs.astype(bf16).reshape(n_orbs, 16, chunk).transpose(1, 0, 2), ZY)
        orbs_t = orbs_t.reshape(16 * n_orbs, chunk)

    with jax.named_scope("spread"):
        left, right = orbs_t[:, :half], orbs_t[:, half:]
        keep, give = pick(left, right, xl), pick(right, left, xl)
        same_oth = swap(give, "xl")
        diff_oth = lax.ppermute(give, ("xl", "xh"), [(i, 3 - i) for i in range(4)])

    with jax.named_scope("window_gather"):
        window = lax.all_gather(jnp.stack([mine, mine_x]), ZY, axis=0)

    with jax.named_scope("project"):
        proj = dot(orbs_t, vec_t, ((1,), (1,))).astype(bf16)
        cross = dot(vec_t[:pw], vec_t[pw:], ((1,), (1,))).astype(bf16)
        n_own = 16 * n_orbs // 32
        lanes = pw * pw // (32 * n_own)
        parts = jnp.concatenate(
            [proj.reshape(32, n_own, 2 * pw), cross.reshape(32, n_own, lanes)], axis=2
        )
        summed = exchange(parts, ZYC).astype(jnp.float32).sum(0)
        summed = summed + swap(summed, "xh")

    with jax.named_scope("spread_late"):
        keep, summed = lax.optimization_barrier((keep, summed))
        diff_own = swap(keep, "xh")
        sides = [(keep, same_oth), None, (diff_own, diff_oth), None]
        sides[1] = tuple(swap(part, "c") for part in sides[0])
        sides[3] = tuple(swap(part, "c") for part in sides[2])

    with jax.named_scope("coefficients"):
        high = lax.Precision.HIGHEST
        first = dot(summed[:, :pw], factor_one, ((1,), (1,)), precision=high)
        second = dot(summed[:, pw : 2 * pw], factor_two, ((1,), (1,)), precision=high)
        share = jnp.concatenate([first, second, summed[:, 2 * pw :]], axis=1).astype(bf16)
        every = exchange(jnp.broadcast_to(share[None], (32,) + share.shape), ZYC)
        cross = every[:, :, 2 * pw :].reshape(pw, pw)
        first = every[:, :, :pw].reshape(16 * n_orbs, pw)
        second = every[:, :, pw : 2 * pw].reshape(16 * n_orbs, pw)
        mixed = dot(cross.astype(jnp.float32), factor_two, ((1,), (1,)), precision=high)
        second = second.astype(jnp.float32) - dot(first, mixed.astype(bf16), ((1,), (0,)))
        coeffs = jnp.concatenate([first, second.astype(bf16)], axis=1)
        coeffs_half = lax.dynamic_slice_in_dim(coeffs, c * 8 * n_orbs, 8 * n_orbs, 0)
        coeffs_x = swap(coeffs_half, "xl")
        coeffs_y = swap(coeffs_x, "c")
        coeffs_o = jnp.concatenate(
            [pick(coeffs_x, coeffs_y, c), pick(coeffs_y, coeffs_x, c)], axis=0
        )

    with jax.named_scope("transpose_out"):
        update = dot(coeffs, vec_t, ((1,), (0,))).astype(bf16)
        back = exchange(update.reshape(16, n_orbs, chunk), ZY)
        out = eigvecs - back.transpose(1, 0, 2).reshape(n_orbs, n_basis).astype(jnp.float32)

    with jax.named_scope("window_rows"):
        win_vec = order(window[:, 0, n_orbs:], window[:, 1, n_orbs:], rows)

        def rotate(piece, factors):
            piece = piece.reshape(16 * n_orbs, rows).T.astype(jnp.float32)
            return (piece - dot(win_vec, factors, ((0,), (1,)))).astype(bf16)

        win_own = rotate(window[:, 0, :n_orbs], coeffs)
        win_oth = rotate(window[:, 1, :n_orbs], coeffs_o)

    with jax.named_scope("density"):
        place = (xh * 2 + c).astype(jnp.int32).reshape(1)
        density = density_of(
            place, win_own, win_oth, coeffs, coeffs_o, weight_own, weight_oth, sides, vec_sides
        )
    return (out, density)


def density_kernel(place, win_own, win_oth, coeffs, coeffs_o, weight_own, weight_oth, *rest):
    orbs, vecs, out, weighted = rest[:8], rest[8:12], rest[12], rest[13]
    n_half = coeffs.shape[0]

    @pl.when(pl.program_id(0) == 0)
    def _():
        for side in range(4):
            for part, (factor, weight) in enumerate(
                ((coeffs, weight_own), (coeffs_o, weight_oth))
            ):

                @pl.loop(0, n_half // TILE)
                def _(step):
                    at = pl.ds(pl.multiple_of(step * TILE, TILE), TILE)
                    update = dot(factor[at, :], vecs[side][...], ((1,), (0,)))
                    new = orbs[2 * side + part][at, :].astype(jnp.float32) - update
                    new = (new * weight[at, :]).astype(jnp.bfloat16)
                    to = pl.ds(pl.multiple_of(part * n_half + step * TILE, TILE), TILE)
                    weighted[side, to, :] = new

    for block in range(4):
        side = jnp.bitwise_xor(place[0], block)
        total = dot(win_own[...], weighted[side, :n_half, :], ((1,), (0,)))
        total = total + dot(win_oth[...], weighted[side, n_half:, :], ((1,), (0,)))
        out[:, block, :] = total


def density_of(place, win_own, win_oth, coeffs, coeffs_o, weight_own, weight_oth, sides, vecs):
    rows, n_half = win_own.shape
    width = vecs[0].shape[1]
    operands = [coeffs, coeffs_o, weight_own, weight_oth]
    operands += [part for side in sides for part in side] + list(vecs)
    whole = [
        pl.BlockSpec(value.shape, lambda i, _: (0, 0), pipeline_mode=pl.Buffered(1))
        for value in operands
    ]
    tile = pl.BlockSpec((TILE, n_half), lambda i, _: (i, 0))
    return pl.pallas_call(
        density_kernel,
        out_shape=jax.ShapeDtypeStruct((rows, 4, width), jnp.float32),
        grid_spec=pltpu.PrefetchScalarGridSpec(
            num_scalar_prefetch=1,
            grid=(rows // TILE,),
            in_specs=[tile, tile] + whole,
            out_specs=pl.BlockSpec((TILE, 4, width), lambda i, _: (i, 0, 0)),
            scratch_shapes=[pltpu.VMEM((4, 2 * n_half, width), jnp.bfloat16)],
        ),
        compiler_params=pltpu.CompilerParams(vmem_limit_bytes=48 * 2**20),
        cost_estimate=pl.CostEstimate(
            flops=2 * rows * 2 * n_half * 4 * width + 16 * n_half * 512 * width,
            bytes_accessed=28 * 2**20,
            transcendentals=0,
        ),
        name="density",
    )(place, win_own, win_oth, *operands)


def solution(mesh):
    mesh = Mesh(mesh.devices.reshape(4, 4, 2, 2, 2), ("z", "y", "xl", "xh", "c"))
    slab, grid = ("z", "y", "xl"), ("xh", "c")
    both = P(slab, grid)
    in_specs = (both, both, both, P(), P(), P(slab), P(), P())
    out_specs = (both, P(grid, None, slab))
    return jax.shard_map(body, mesh=mesh, in_specs=in_specs, out_specs=out_specs, check_vma=False)
```

time: 296 us -> 312 us (1.054)
  Pallas kernels: 0 us -> 25.6 us
  waiting for transfers between devices: 119 us -> 99.1 us
  matrix products: 33.4 us -> 17.7 us
  starting transfers between devices: 39.6 us -> 50.7 us
  other arithmetic: 22.8 us -> 30.9 us
  blocking collectives: 31.2 us -> 39 us
    ppermute x1, waiting for transfers between devices: 31.6 us -> 0.01 us  [body(): diff_oth = lax.ppermute(give, ('xl', 'xh'), [(i, 3 - i) for i in range(4)])]
    pallas_call x0 -> x1, Pallas kernels: none -> 25.6 us  [density_of(): pl.pallas_call(density_kernel, out_shape=jax.ShapeDtypeStruct((rows, 4, w...]
    ppermute x12 -> x16, waiting for transfers between devices: 33.3 us -> 52.1 us  [swap(): return lax.ppermute(values, axis, [(0, 1), (1, 0)])]
    dot_general x17 -> x9, matrix products: 33.4 us -> 17.7 us  [dot(): lax.dot_general(left, right, (dims, ((), ())), preferred_element_type=jnp...]
    unnamed x35 -> x38, local copies, waits for them, and re-layouts: 18.8 us -> 6.33 us
    ppermute x12 -> x16, starting transfers between devices: 15.8 us -> 26 us  [swap(): return lax.ppermute(values, axis, [(0, 1), (1, 0)])]
    convert_element_type x1 -> x2, local copies, waits for them, and re-layouts: 1.55 us -> 10.7 us  [rotate(): piece = piece.reshape(16 * n_orbs, rows).T.astype(jnp.float32)]
    convert_element_type x2 -> x6, other arithmetic: 3.53 us -> 11.8 us  [the longest x2 5.23 us: rotate(): piece = piece.reshape(16 * n_orbs, rows).T.astype(jnp.float32)]
  transfers between devices with their start and end apart: 18 -> 22, of which waited for: 10 -> 10; matrix products, arithmetic and copies ran while one was open for 19% -> 20% of each run, Pallas kernels for 0% -> 0%
where the time goes in v2:
time: 312 us; the launch traced here: 311 us
  waiting for transfers between devices  99.1 us (32%)
  starting transfers between devices  50.7 us (16%)
  blocking collectives  39 us (12%)
  local copies, waits for them, and re-layouts  32.5 us (10%)
  other arithmetic  30.9 us (10%)
  Pallas kernels  25.6 us (8%)
  matrix products  17.7 us (6%)
  between operations  15.9 us (5%)
    ppermute x16, waiting for transfers between devices, swap(): return lax.ppermute(values, axis, [(0, 1), (1, 0)])  52.1 us
    all_to_all x4, waiting for transfers between devices, exchange(): return lax.all_to_all(values, axes, 0, 0, tiled=True)  46.9 us
    all_to_all x1, blocking collectives, exchange(): return lax.all_to_all(values, axes, 0, 0, tiled=True)  39 us
    ppermute x16, starting transfers between devices, swap(): return lax.ppermute(values, axis, [(0, 1), (1, 0)])  26 us
    pallas_call x1, Pallas kernels, density_of(): pl.pallas_call(density_kernel, out_shape=jax.ShapeDtypeStruct((rows, 4, w...  25.6 us
    all_to_all x4, starting transfers between devices, exchange(): return lax.all_to_all(values, axes, 0, 0, tiled=True)  22.3 us
    dot_general x9, matrix products, dot(): lax.dot_general(left, right, (dims, ((), ())), preferred_element_type=jnp...  17.7 us
    convert_element_type x2, local copies, waits for them, and re-layouts, rotate(): piece = piece.reshape(16 * n_orbs, rows).T.astype(jnp.float32)  10.7 us
  transfers between devices with their start and end apart: 22, of which 10 were waited for; matrix products, arithmetic and copies ran while one was open for 20% of the time, Pallas kernels for 0%

profile of v2, /device:TPU:1, one launch (start us, length us, event | category | flops | bytes accessed | tf_op | source)
XLA Modules:
  0.0 311.4 jit_solution(8859717784210983146)
XLA Ops:
  10.3 8.6 %all-to-all-start.1 = ((bf16[16,16,1152]{2,1,0:T(8,128)(2,1)}), bf16[16,16,1152]{2,1,0:T(8,128)(2,1)S(1)}, u32[]{:S(2)}, u32[]{:S(2)}) async-start(bf16[16,16,1152]{2,1,0:T(8,128)(2,1)} %copy.43), calls=%async_computation.1 | async-start | bytes 1179648 | tf_op jit(solution)/shard_map/vectors/all_to_all | solution.py:29
  19.6 10.3 %all-to-all-done.1 = bf16[16,16,1152]{2,1,0:T(8,128)(2,1)S(1)} async-done(((bf16[16,16,1152]{2,1,0:T(8,128)(2,1)}), bf16[16,16,1152]{2,1,0:T(8,128)(2,1)S(1)}, u32[]{:S(2)}, u32[]{:S(2)}) %all-to-all-start.1) | async-done | bytes 589856 | tf_op jit(solution)/shard_map/vectors/all_to_all | solution.py:29
  30.0 2.6 convert_element_type.111
  32.7 3.1 pad_maximum_fusion
  35.8 1.9 copy-done.7
  37.8 2.8 collective-permute-start.2
  40.7 5.8 %collective-permute-done.2 = bf16[80,2048]{1,0:T(8,128)(2,1)S(1)} collective-permute-done((bf16[80,2048]{1,0:T(8,128)(2,1)S(1)}, bf16[80,2048]{1,0:T(8,128)(2,1)S(1)}, u32[]{:S(2)}, u32[]{:S(2)}) %collective-permute-start.2) | collective-permute-done | bytes 327712 | tf_op jit(solution)/shard_map/window_exchange/ppermute | solution.py:25
  46.5 1.1 dynamic-slice_add_fusion
  48.6 3.1 %collective-permute-start.3 = (bf16[80,1024]{1,0:T(8,128)(2,1)S(1)}, bf16[80,1024]{1,0:T(8,128)(2,1)S(1)}, u32[]{:S(2)}, u32[]{:S(2)}) collective-permute-start(bf16[80,1024]{1,0:T(8,128)(2,1)S(1)} %bitcast.111), channel_id=1, source_target_pairs={{0,1},{1,0},{2,3},{3,2},{4,5},{5,4},{6,7},{7,6},{8,9},{9,8},{10,11... | collective-permute-start | bytes 491528 | tf_op jit(solution)/shard_map/window_exchange/ppermute | solution.py:25
  52.8 1.3 collective-permute-start.4
  54.1 4.2 %collective-permute-done.4 = bf16[80,1024]{1,0:T(8,128)(2,1)S(1)} collective-permute-done((bf16[80,1024]{1,0:T(8,128)(2,1)S(1)}, bf16[80,1024]{1,0:T(8,128)(2,1)S(1)}, u32[]{:S(2)}, u32[]{:S(2)}) %collective-permute-start.4) | collective-permute-done | bytes 163872 | tf_op jit(solution)/shard_map/window_exchange/ppermute | solution.py:25
  59.1 2.4 convert_element_type.93
  61.5 1.6 copy.66
  63.1 3.7 %all-to-all-start = ((bf16[16,64,1024]{2,1,0:T(8,128)(2,1)}), bf16[16,64,1024]{2,1,0:T(8,128)(2,1)S(1)}, u32[]{:S(2)}, u32[]{:S(2)}) async-start(bf16[16,64,1024]{2,1,0:T(8,128)(2,1)} %bitcast.97), calls=%async_computation | async-start | bytes 4194304 | tf_op jit(solution)/shard_map/transpose_in/all_to_all | solution.py:29
  66.8 1.3 collective-permute-start
  68.1 12.3 %collective-permute-done = bf16[16,16,1152]{2,1,0:T(8,128)(2,1)S(1)} collective-permute-done((bf16[16,16,1152]{2,1,0:T(8,128)(2,1)S(1)}, bf16[16,16,1152]{2,1,0:T(8,128)(2,1)S(1)}, u32[]{:S(2)}, u32[]{:S(2)}) %collective-permute-start) | collective-permute-done | bytes 589856 | tf_op jit(solution)/shard_map/vectors/ppermute | solution.py:25
  82.9 18.7 %all-to-all-done = bf16[16,64,1024]{2,1,0:T(8,128)(2,1)S(1)} async-done(((bf16[16,64,1024]{2,1,0:T(8,128)(2,1)}), bf16[16,64,1024]{2,1,0:T(8,128)(2,1)S(1)}, u32[]{:S(2)}, u32[]{:S(2)}) %all-to-all-start) | async-done | bytes 2097184 | tf_op jit(solution)/shard_map/transpose_in/all_to_all | solution.py:29
  101.6 2.3 fusion.2
  103.9 1.5 copy.45
  106.4 39.0 %all_to_all.25 = bf16[32,32,576]{2,1,0:T(8,128)(2,1)S(1)} all-to-all(bf16[32,32,576]{2,1,0:T(8,128)(2,1)S(1)} %pad_maximum_fusion.1), channel_id=1, replica_groups=mesh['z'=4,'y'=4,'xl'=2,'xh'=2,'c'=2] {'z','y','c'}, dimensions={0} | all-to-all | bytes 2359296 | tf_op jit(solution)/shard_map/project/all_to_all | solution.py:29
  145.6 2.6 collective-permute-start.1
  148.2 1.5 broadcast_select_fusion
  151.3 1.2 broadcast_in_dim.12
  152.4 5.6 %all-to-all-start.3 = ((bf16[32,32,576]{2,1,0:T(8,128)(2,1)}), bf16[32,32,576]{2,1,0:T(8,128)(2,1)S(1)}, u32[]{:S(2)}, u32[]{:S(2)}) async-start(bf16[32,32,576]{2,1,0:T(8,128)(2,1)} %broadcast_in_dim.12), calls=%async_computation.3 | async-start | bytes 2621440 | tf_op jit(solution)/shard_map/coefficients/all_to_all | solution.py:29
  159.3 17.9 %all-to-all-done.3 = bf16[32,32,576]{2,1,0:T(8,128)(2,1)S(1)} async-done(((bf16[32,32,576]{2,1,0:T(8,128)(2,1)}), bf16[32,32,576]{2,1,0:T(8,128)(2,1)S(1)}, u32[]{:S(2)}, u32[]{:S(2)}) %all-to-all-start.3) | async-done | bytes 1179680 | tf_op jit(solution)/shard_map/coefficients/all_to_all | solution.py:29
  178.7 2.6 convolution_convert_fusion
  181.2 4.4 %all-to-all-start.4 = ((bf16[16,64,1024]{2,1,0:T(8,128)(2,1)}), bf16[16,64,1024]{2,1,0:T(8,128)(2,1)}, u32[]{:S(2)}, u32[]{:S(2)}) async-start(bf16[16,64,1024]{2,1,0:T(8,128)(2,1)} %bitcast.16), calls=%async_computation.4 | async-start | bytes 4194304 | tf_op jit(solution)/shard_map/transpose_out/all_to_all | solution.py:29
  186.3 2.4 collective-permute-start.11
  189.5 1.5 collective-permute-start.5
  193.1 3.1 collective-permute-start.14
  197.0 25.7 %collective-permute-done.5 = bf16[512,512]{1,0:T(8,128)(2,1)} collective-permute-done((bf16[512,512]{1,0:T(8,128)(2,1)}, bf16[512,512]{1,0:T(8,128)(2,1)}, u32[]{:S(2)}, u32[]{:S(2)}) %collective-permute-start.5) | collective-permute-done | bytes 524320 | tf_op jit(solution)/shard_map/coefficients/ppermute | solution.py:25
  222.7 5.9 %collective-permute-start.6 = (bf16[512,512]{1,0:T(8,128)(2,1)}, bf16[512,512]{1,0:T(8,128)(2,1)}, u32[]{:S(2)}, u32[]{:S(2)}) collective-permute-start(bf16[512,512]{1,0:T(8,128)(2,1)} %collective-permute-done.5), channel_id=1, source_target_pairs={{0,1},{1,0},{2,3},{3,2},{4,5},{5,4},{6,7},{7,6},{8,9},{9,8},{10,11... | collective-permute-start | bytes 1572872 | tf_op jit(solution)/shard_map/coefficients/ppermute | solution.py:25
  231.4 1.3 broadcast_select_fusion.3
  233.7 2.0 convert_bitcast_fusion
  236.1 1.9 copy-done.3
  238.0 2.4 sub.33
  240.4 4.2 %fusion.20 = (bf16[16,1,64,1024]{3,2,1,0:T(8,128)(2,1)S(1)}, bf16[16,1,64,1024]{3,2,1,0:T(8,128)(2,1)}) fusion(bf16[16,2,80,1024]{3,2,1,0:T(8,128)(2,1)} %bitcast.98), kind=kLoop, calls=%fused_computation.81 | loop fusion | bytes 8388608 | tf_op jit(solution)/shard_map/window_rows/slice | solution.py:165
  244.6 1.3 select_bitcast_fusion.1
  245.9 2.6 bitcast_convert_fusion
  248.6 1.1 copy.51
  249.7 5.3 %copy.52 = f32[1024,1024]{0,1:T(8,128)} copy(f32[1024,1024]{1,0:T(8,128)} %bitcast_convert_fusion) | data formatting | bytes 8388608 | tf_op jit(solution)/shard_map/window_rows/convert_element_type | solution.py:161
  255.5 2.2 collective-permute-done.10.rest_4_
  257.7 1.9 collective-permute-start.12
  259.6 5.6 %fusion.win_oth = bf16[1024,1024]{1,0:T(8,128)(2,1)} fusion(f32[1024,1024]{0,1:T(8,128)} %copy.52, bf16[512,1024]{1,0:T(8,128)(2,1)} %bitcast.92, bf16[512,512]{1,0:T(8,128)(2,1)} %copy-done.9, bf16[512,512]{1,0:T(8,128)(2,1)} %copy-done.8), kind=kOutput, calls=%fused_computation.1 | convolution fusion | flops 1077936128 | bytes 8388608 | tf_op jit(solution)/shard_map/window_rows/dot_general | solution.py:19
  265.3 2.6 bitcast_convert_fusion.1
  267.9 5.3 %copy.50 = f32[1024,1024]{0,1:T(8,128)} copy(f32[1024,1024]{1,0:T(8,128)} %bitcast_convert_fusion.1) | data formatting | bytes 8388608 | tf_op jit(solution)/shard_map/window_rows/convert_element_type | solution.py:161
  273.3 5.6 %fusion.1.win_own = bf16[1024,1024]{1,0:T(8,128)(2,1)} fusion(f32[1024,1024]{0,1:T(8,128)} %copy.50, bf16[512,1024]{1,0:T(8,128)(2,1)} %bitcast.93, bf16[1024,256]{1,0:T(8,128)(2,1)} %copy-done.6, bf16[1024,256]{1,0:T(8,128)(2,1)} %bitcast.91), kind=kOutput, calls=%fused_computation.3 | convolution fusion | flops 1077936128 | bytes 8388608 | tf_op jit(solution)/shard_map/window_rows/dot_general | solution.py:19
  278.9 25.6 %density.1 = f32[1024,4,512]{2,1,0:T(4,128)} custom-call(s32[1]{0:T(128)} %bitcast.18.place, bf16[1024,1024]{1,0:T(8,128)(2,1)} %fusion.1.win_own, bf16[1024,1024]{1,0:T(8,128)(2,1)} %fusion.win_oth, bf16[1024,512]{1,0:T(8,128)(2,1)S(1)} %pad_maximum_fusion.2.coeffs, bf16[1024,512]{1,0:T(8,128)(2,1)S(1)} %pad_maximum_fusion.3.coeffs_o, ...), custom_call_target="tpu_custom_call" | custom-call | flops 12884901888 | bytes 29360128 | tf_op jit(solution)/shard_map/density/density/pallas_call | solution.py:212
  (110 shorter events, 22.5 us)
Async XLA Ops:
  7.2 143.4 %copy-start = (f32[256,256]{1,0:T(8,128)S(1)}, f32[256,256]{1,0:T(8,128)}, u32[]{:S(2)}) copy-start(f32[256,256]{1,0:T(8,128)} %param.14) | copy-start | bytes 786436
  10.3 19.7 %all-to-all-start.1 = ((bf16[16,16,1152]{2,1,0:T(8,128)(2,1)}), bf16[16,16,1152]{2,1,0:T(8,128)(2,1)S(1)}, u32[]{:S(2)}, u32[]{:S(2)}) async-start(bf16[16,16,1152]{2,1,0:T(8,128)(2,1)} %copy.43), calls=%async_computation.1 | async-start | bytes 1179648 | tf_op jit(solution)/shard_map/vectors/all_to_all | solution.py:29
  18.9 221.5 %all-gather.3.cloned.1.call-start = ((), (), s32[]{:S(2)}) async-start(), calls=%async_computation.5 | async-start | bytes 5570560 | tf_op jit(solution)/shard_map/window_gather/all_gather | solution.py:113
  19.6 13.0 %copy-start.14 = (bf16[8,16384]{1,0:T(8,128)(2,1)S(1)}, bf16[8,16384]{1,0:T(8,128)(2,1)}, u32[]{:S(2)}) copy-start(bf16[8,16384]{1,0:T(8,128)(2,1)} %param.12) | copy-start | bytes 786436
  19.6 13.0 %copy-start.15 = (bf16[8,16384]{1,0:T(8,128)(2,1)S(1)}, bf16[8,16384]{1,0:T(8,128)(2,1)}, u32[]{:S(2)}) copy-start(bf16[8,16384]{1,0:T(8,128)(2,1)} %param.11) | copy-start | bytes 786436
  30.0 50.5 %copy-start.13 = (bf16[16,16,1152]{2,1,0:T(8,128)(2,1)}, bf16[16,16,1152]{2,1,0:T(8,128)(2,1)S(1)}, u32[]{:S(2)}) copy-start(bf16[16,16,1152]{2,1,0:T(8,128)(2,1)S(1)} %all-to-all-done.1) | copy-start | bytes 1769476
  35.7 1.9 copy-start.7
  37.8 8.7 %collective-permute-start.2 = (bf16[80,2048]{1,0:T(8,128)(2,1)S(1)}, bf16[80,2048]{1,0:T(8,128)(2,1)S(1)}, u32[]{:S(2)}, u32[]{:S(2)}) collective-permute-start(bf16[80,2048]{1,0:T(8,128)(2,1)S(1)} %constant_dynamic-slice_fusion.3), channel_id=1, source_target_pairs={{0,2},{2,0},{1,3},{3,1},{4,6},{6,4},{5,7},{7,5},{8,10},{10,8},{9,1... | collective-permute-start | bytes 983048 | tf_op jit(solution)/shard_map/window_exchange/ppermute | solution.py:25
  48.6 4.2 %collective-permute-start.3 = (bf16[80,1024]{1,0:T(8,128)(2,1)S(1)}, bf16[80,1024]{1,0:T(8,128)(2,1)S(1)}, u32[]{:S(2)}, u32[]{:S(2)}) collective-permute-start(bf16[80,1024]{1,0:T(8,128)(2,1)S(1)} %bitcast.111), channel_id=1, source_target_pairs={{0,1},{1,0},{2,3},{3,2},{4,5},{5,4},{6,7},{7,6},{8,9},{9,8},{10,11... | collective-permute-start | bytes 491528 | tf_op jit(solution)/shard_map/window_exchange/ppermute | solution.py:25
  52.8 5.5 %collective-permute-start.4 = (bf16[80,1024]{1,0:T(8,128)(2,1)S(1)}, bf16[80,1024]{1,0:T(8,128)(2,1)S(1)}, u32[]{:S(2)}, u32[]{:S(2)}) collective-permute-start(bf16[80,1024]{1,0:T(8,128)(2,1)S(1)} %bitcast_add_fusion), channel_id=1, source_target_pairs={{0,4},{4,0},{1,5},{5,1},{2,6},{6,2},{3,7},{7,3},{8,12},{12,8},{9,1... | collective-permute-start | bytes 491528 | tf_op jit(solution)/shard_map/window_exchange/ppermute | solution.py:25
  63.1 38.5 %all-to-all-start = ((bf16[16,64,1024]{2,1,0:T(8,128)(2,1)}), bf16[16,64,1024]{2,1,0:T(8,128)(2,1)S(1)}, u32[]{:S(2)}, u32[]{:S(2)}) async-start(bf16[16,64,1024]{2,1,0:T(8,128)(2,1)} %bitcast.97), calls=%async_computation | async-start | bytes 4194304 | tf_op jit(solution)/shard_map/transpose_in/all_to_all | solution.py:29
  66.8 13.6 %collective-permute-start = (bf16[16,16,1152]{2,1,0:T(8,128)(2,1)S(1)}, bf16[16,16,1152]{2,1,0:T(8,128)(2,1)S(1)}, u32[]{:S(2)}, u32[]{:S(2)}) collective-permute-start(bf16[16,16,1152]{2,1,0:T(8,128)(2,1)S(1)} %all-to-all-done.1), channel_id=1, source_target_pairs={{0,4},{4,0},{1,5},{5,1},{2,6},{6,2},{3,7},{7,3},{8,12},{12,8},{9,1... | collective-permute-start | bytes 1769480 | tf_op jit(solution)/shard_map/vectors/ppermute | solution.py:25
  80.5 0.8 copy-start.16
  81.5 20.1 %copy-start.10 = (bf16[2,16,2,8,1024]{4,3,2,1,0:T(8,128)(2,1)}, bf16[2,16,2,8,1024]{4,3,2,1,0:T(8,128)(2,1)S(1)}, u32[]{:S(2)}) copy-start(bf16[2,16,2,8,1024]{4,3,2,1,0:T(8,128)(2,1)S(1)} %copy.44) | copy-start | bytes 3145732
  145.6 5.3 %copy-start.17 = (f32[256,256]{1,0:T(8,128)S(1)}, f32[256,256]{1,0:T(8,128)}, u32[]{:S(2)}) copy-start(f32[256,256]{1,0:T(8,128)} %param.13) | copy-start | bytes 786436
  145.6 4.9 %collective-permute-start.1 = (f32[32,576]{1,0:T(8,128)S(1)}, f32[32,576]{1,0:T(8,128)S(1)}, u32[]{:S(2)}, u32[]{:S(2)}) collective-permute-start(f32[32,576]{1,0:T(8,128)S(1)} %convert_reduce_fusion), channel_id=1, source_target_pairs={{0,2},{2,0},{1,3},{3,1},{4,6},{6,4},{5,7},{7,5},{8,10},{10,8},{9,1... | collective-permute-start | bytes 221192 | tf_op jit(solution)/shard_map/project/ppermute | solution.py:25
  152.4 24.8 %all-to-all-start.3 = ((bf16[32,32,576]{2,1,0:T(8,128)(2,1)}), bf16[32,32,576]{2,1,0:T(8,128)(2,1)S(1)}, u32[]{:S(2)}, u32[]{:S(2)}) async-start(bf16[32,32,576]{2,1,0:T(8,128)(2,1)} %broadcast_in_dim.12), calls=%async_computation.3 | async-start | bytes 2621440 | tf_op jit(solution)/shard_map/coefficients/all_to_all | solution.py:29
  177.4 1.2 copy-start.11
  177.9 52.6 %copy-start.4 = (bf16[32,32,256]{2,1,0:T(8,128)(2,1)}, bf16[32,32,256]{2,1,0:T(8,128)(2,1)S(1)}, u32[]{:S(2)}) copy-start(bf16[32,32,256]{2,1,0:T(8,128)(2,1)S(1)} %get-tuple-element.27) | copy-start | bytes 1572868
  178.7 51.9 %copy-start.6 = (bf16[1024,256]{1,0:T(8,128)(2,1)}, bf16[1024,256]{1,0:T(8,128)(2,1)S(1)}, u32[]{:S(2)}) copy-start(bf16[1024,256]{1,0:T(8,128)(2,1)S(1)} %fusion.3) | copy-start | bytes 1572868
  181.2 52.5 %all-to-all-start.4 = ((bf16[16,64,1024]{2,1,0:T(8,128)(2,1)}), bf16[16,64,1024]{2,1,0:T(8,128)(2,1)}, u32[]{:S(2)}, u32[]{:S(2)}) async-start(bf16[16,64,1024]{2,1,0:T(8,128)(2,1)} %bitcast.16), calls=%async_computation.4 | async-start | bytes 4194304 | tf_op jit(solution)/shard_map/transpose_out/all_to_all | solution.py:29
  185.7 6.6 %copy-start.12 = (bf16[2,16,2,8,1024]{4,3,2,1,0:T(8,128)(2,1)S(1)}, bf16[2,16,2,8,1024]{4,3,2,1,0:T(8,128)(2,1)}, u32[]{:S(2)}) copy-start(bf16[2,16,2,8,1024]{4,3,2,1,0:T(8,128)(2,1)} %copy-done.10) | copy-start | bytes 3145732
  186.3 43.7 %collective-permute-start.11 = (bf16[1024,512]{1,0:T(8,128)(2,1)}, bf16[1024,512]{1,0:T(8,128)(2,1)}, u32[]{:S(2)}, u32[]{:S(2)}) collective-permute-start(bf16[1024,512]{1,0:T(8,128)(2,1)} %get-tuple-element.24), channel_id=1, source_target_pairs={{0,6},{2,4},{4,2},{6,0},{1,7},{3,5},{5,3},{7,1},{8,14},{10,12},{12... | collective-permute-start | bytes 3145736 | tf_op jit(solution)/shard_map/spread/ppermute | solution.py:110
  188.7 41.3 %collective-permute-start.7 = (bf16[1024,512]{1,0:T(8,128)(2,1)}, bf16[1024,512]{1,0:T(8,128)(2,1)}, u32[]{:S(2)}, u32[]{:S(2)}) collective-permute-start(bf16[1024,512]{1,0:T(8,128)(2,1)} %get-tuple-element.24), channel_id=1, source_target_pairs={{0,4},{4,0},{1,5},{5,1},{2,6},{6,2},{3,7},{7,3},{8,12},{12,8},{9,1... | collective-permute-start | bytes 3145736 | tf_op jit(solution)/shard_map/spread/ppermute | solution.py:25
  189.5 33.1 %collective-permute-start.5 = (bf16[512,512]{1,0:T(8,128)(2,1)}, bf16[512,512]{1,0:T(8,128)(2,1)}, u32[]{:S(2)}, u32[]{:S(2)}) collective-permute-start(bf16[512,512]{1,0:T(8,128)(2,1)} %fusion.4), channel_id=1, source_target_pairs={{0,4},{4,0},{1,5},{5,1},{2,6},{6,2},{3,7},{7,3},{8,12},{12,8},{9,1... | collective-permute-start | bytes 1572872 | tf_op jit(solution)/shard_map/coefficients/ppermute | solution.py:25
  192.3 62.7 %collective-permute-start.15 = (bf16[512,512]{1,0:T(8,128)(2,1)S(1)}, bf16[512,512]{1,0:T(8,128)(2,1)}, u32[]{:S(2)}, u32[]{:S(2)}) collective-permute-start(bf16[512,512]{1,0:T(8,128)(2,1)S(1)} %constant_dynamic-slice_fusion.rest_8_), channel_id=1, source_target_pairs={{0,2},{2,0},{1,3},{3,1},{4,6},{6,4},{5,7},{7,5},{8,10},{10,8},{9,1... | collective-permute-start | bytes 1572872 | tf_op jit(solution)/shard_map/vectors/ppermute | solution.py:25
  193.1 72.2 %collective-permute-start.14 = (bf16[512,512]{1,0:T(8,128)(2,1)S(1)}, bf16[512,512]{1,0:T(8,128)(2,1)}, u32[]{:S(2)}, u32[]{:S(2)}) collective-permute-start(bf16[512,512]{1,0:T(8,128)(2,1)S(1)} %constant_dynamic-slice_fusion.rest_8_), channel_id=1, source_target_pairs={{0,1},{1,0},{2,3},{3,2},{4,5},{5,4},{6,7},{7,6},{8,9},{9,8},{10,11... | collective-permute-start | bytes 1572872 | tf_op jit(solution)/shard_map/vectors/ppermute | solution.py:25
  222.7 7.9 %collective-permute-start.6 = (bf16[512,512]{1,0:T(8,128)(2,1)}, bf16[512,512]{1,0:T(8,128)(2,1)}, u32[]{:S(2)}, u32[]{:S(2)}) collective-permute-start(bf16[512,512]{1,0:T(8,128)(2,1)} %collective-permute-done.5), channel_id=1, source_target_pairs={{0,1},{1,0},{2,3},{3,2},{4,5},{5,4},{6,7},{7,6},{8,9},{9,8},{10,11... | collective-permute-start | bytes 1572872 | tf_op jit(solution)/shard_map/coefficients/ppermute | solution.py:25
  230.0 48.9 %collective-permute-start.13 = (bf16[1024,512]{1,0:T(8,128)(2,1)}, bf16[1024,512]{1,0:T(8,128)(2,1)}, u32[]{:S(2)}, u32[]{:S(2)}) collective-permute-start(bf16[1024,512]{1,0:T(8,128)(2,1)} %collective-permute-done.11.rest_5_), channel_id=1, source_target_pairs={{0,1},{1,0},{2,3},{3,2},{4,5},{5,4},{6,7},{7,6},{8,9},{9,8},{10,11... | collective-permute-start | bytes 3145736 | tf_op jit(solution)/shard_map/spread_late/ppermute | solution.py:25
  230.0 48.9 %collective-permute-start.9 = (bf16[1024,512]{1,0:T(8,128)(2,1)}, bf16[1024,512]{1,0:T(8,128)(2,1)}, u32[]{:S(2)}, u32[]{:S(2)}) collective-permute-start(bf16[1024,512]{1,0:T(8,128)(2,1)} %collective-permute-done.7.rest_1_), channel_id=1, source_target_pairs={{0,1},{1,0},{2,3},{3,2},{4,5},{5,4},{6,7},{7,6},{8,9},{9,8},{10,11... | collective-permute-start | bytes 3145736 | tf_op jit(solution)/shard_map/spread_late/ppermute | solution.py:25
  230.6 27.1 %collective-permute-start.10 = (bf16[1024,512]{1,0:T(8,128)(2,1)}, bf16[1024,512]{1,0:T(8,128)(2,1)}, u32[]{:S(2)}, u32[]{:S(2)}) collective-permute-start(bf16[1024,512]{1,0:T(8,128)(2,1)} %get-tuple-element.19.rest_0_), channel_id=1, source_target_pairs={{0,2},{2,0},{1,3},{3,1},{4,6},{6,4},{5,7},{7,5},{8,10},{10,8},{9,1... | collective-permute-start | bytes 3145736 | tf_op jit(solution)/shard_map/spread_late/ppermute | solution.py:25
  232.7 0.8 copy-start.8
  232.7 1.0 copy-start.9
  235.8 2.2 copy-start.3
  255.1 23.8 %collective-permute-start.8 = (bf16[1024,512]{1,0:T(8,128)(2,1)}, bf16[1024,512]{1,0:T(8,128)(2,1)}, u32[]{:S(2)}, u32[]{:S(2)}) collective-permute-start(bf16[1024,512]{1,0:T(8,128)(2,1)} %get-tuple-element.19.rest_0_), channel_id=1, source_target_pairs={{0,1},{1,0},{2,3},{3,2},{4,5},{5,4},{6,7},{7,6},{8,9},{9,8},{10,11... | collective-permute-start | bytes 3145736 | tf_op jit(solution)/shard_map/spread_late/ppermute | solution.py:25
  257.7 21.1 %collective-permute-start.12 = (bf16[1024,512]{1,0:T(8,128)(2,1)}, bf16[1024,512]{1,0:T(8,128)(2,1)}, u32[]{:S(2)}, u32[]{:S(2)}) collective-permute-start(bf16[1024,512]{1,0:T(8,128)(2,1)} %collective-permute-done.10.rest_4_), channel_id=1, source_target_pairs={{0,1},{1,0},{2,3},{3,2},{4,5},{5,4},{6,7},{7,6},{8,9},{9,8},{10,11... | collective-permute-start | bytes 3145736 | tf_op jit(solution)/shard_map/spread_late/ppermute | solution.py:25
  259.6 5.7 %copy-start.5 = (bf16[16,1,64,1024]{3,2,1,0:T(8,128)(2,1)S(1)}, bf16[16,1,64,1024]{3,2,1,0:T(8,128)(2,1)}, u32[]{:S(2)}) copy-start(bf16[16,1,64,1024]{3,2,1,0:T(8,128)(2,1)} %get-tuple-element.21) | copy-start | bytes 6291460
  265.3 13.6 %collective-permute-start.16 = (bf16[512,512]{1,0:T(8,128)(2,1)}, bf16[512,512]{1,0:T(8,128)(2,1)}, u32[]{:S(2)}, u32[]{:S(2)}) collective-permute-start(bf16[512,512]{1,0:T(8,128)(2,1)} %collective-permute-done.15.rest_10_), channel_id=1, source_target_pairs={{0,1},{1,0},{2,3},{3,2},{4,5},{5,4},{6,7},{7,6},{8,9},{9,8},{10,11... | collective-permute-start | bytes 1572872 | tf_op jit(solution)/shard_map/vectors/ppermute | solution.py:25
  273.3 5.6 %copy-start.2 = (f32[1024,1]{1,0:T(8,128)S(1)}, f32[1024,1]{1,0:T(8,128)}, u32[]{:S(2)}) copy-start(f32[1024,1]{1,0:T(8,128)} %get-tuple-element.40.weight_own) | copy-start | bytes 12292
  278.9 25.6 %copy-start.1 = (f32[256,256]{1,0:T(8,128)S(1)}, f32[256,256]{1,0:T(8,128)}, u32[]{:S(2)}) copy-start(f32[256,256]{1,0:T(8,128)} %param.14) | copy-start | bytes 786436
Sparse Core Ops, SparseCore 0:
  59.3 87.5 all-gather.2

commit v3 on v2

v3 whole, which is shorter than its diff:
```python
import functools
import math

import jax
import jax.numpy as jnp
from jax import lax
from jax.experimental import pallas as pl
from jax.experimental.pallas import tpu as pltpu
from jax.sharding import Mesh
from jax.sharding import PartitionSpec as P

OCC = 2048
R = 4096
ZY = ("z", "y")
ZYC = ("z", "y", "c")
TILE = 256


def dot(left, right, dims, **kwargs):
    return lax.dot_general(
        left, right, (dims, ((), ())), preferred_element_type=jnp.float32, **kwargs
    )


def swap(values, axis):
    return lax.ppermute(values, axis, [(0, 1), (1, 0)])


def exchange(values, axes):
    return lax.all_to_all(values, axes, 0, 0, tiled=True)


def tie(*values):
    return lax.optimization_barrier(values)


def pick(first, second, flag):
    return jnp.where(flag == 0, first, second)


def body(
    eigvecs, panel_one, panel_two, factor_one, factor_two, occupations, occupied_count, row_offset
):
    bf16 = jnp.bfloat16
    xl, xh, c = (lax.axis_index(name) for name in ("xl", "xh", "c"))
    zy = lax.axis_index(ZY)
    n_orbs, n_basis = eigvecs.shape
    n_vec = panel_one.shape[0]
    chunk = n_basis // 16
    half = chunk // 2
    pw = factor_one.shape[0]
    rows = R // 4

    n_all = 2 * n_vec
    side_xl = xl.astype(jnp.int32).reshape(1)
    place = jnp.stack([xh * 2 + c, c]).astype(jnp.int32)

    with jax.named_scope("pack"):
        occ_high = occupations.astype(bf16)
        rest = occupations - occ_high.astype(jnp.float32)
        occ_mid = rest.astype(bf16)
        occ_low = (rest - occ_mid.astype(jnp.float32)).astype(bf16)
        extra = jnp.zeros((16, half), bf16)
        extra = extra.at[:3, :n_orbs].set(jnp.stack([occ_high, occ_mid, occ_low]))
        give_p, keep_p = pack(side_xl, eigvecs, panel_one, panel_two, extra, chunk)

    with jax.named_scope("transpose_give"):
        got = exchange(give_p, ZY)

    with jax.named_scope("window_exchange"):
        start = row_offset[0] - (xh * 2 + c) * n_basis
        held, _ = tie(eigvecs, give_p)

        def cut(part):
            first = start + part * rows
            at = jnp.clip(first, 0, n_basis - rows)
            pieces = (held, panel_one, panel_two)
            pieces = [lax.dynamic_slice_in_dim(v, at, rows, 1).astype(bf16) for v in pieces]
            piece = jnp.concatenate(pieces)
            zeros = jnp.zeros_like(piece)
            piece = jnp.concatenate([zeros, piece, zeros], axis=1)
            shift = jnp.clip(first - at, -rows, rows)
            return lax.dynamic_slice_in_dim(piece, rows + shift, rows, 1)

        both_flip = [(i, 3 - i) for i in range(4)]
        from_xh = swap(cut((1 - xh) * 2 + c), "xh")
        from_both = lax.ppermute(cut((1 - xh) * 2 + 1 - c), ("xh", "c"), both_flip)
        from_c = swap(cut(xh * 2 + 1 - c), "c")
        mine = (cut(xh * 2 + c) + from_c) + (from_xh + from_both)
        mine_x = swap(mine, "xl")

        def by_xl(own, other, axis):
            return jnp.stack([pick(own, other, xl), pick(other, own, xl)], axis=axis)

        win_vecs = by_xl(mine[n_orbs:], mine_x[n_orbs:], 0).reshape(2 * n_all, rows)
        window = jnp.concatenate([mine[:n_orbs], mine_x[:n_orbs], win_vecs], axis=0)
        got, keep_p, window = tie(got, keep_p, window)
        window = lax.all_gather(window, ZY, axis=0)

    with jax.named_scope("transpose_keep"):
        keep = exchange(keep_p, ZY)
        give = got[:, :n_orbs].reshape(16 * n_orbs, half)
        vec_own = got[:, n_orbs : n_orbs + 2 * n_all]
        occ_own = got[:, n_orbs + 2 * n_all :, :128]
        vec_oth = swap(vec_own, "xl")
        occ_oth = swap(occ_own, "xl")
        quarter = 8 * n_orbs
        give_a, give_b = give[:quarter], give[quarter:]
        same_a = swap(give_a, "xl")
        diff_a = lax.ppermute(give_a, ("xl", "xh"), both_flip)
        count, factor_one, factor_two, vec_oth = tie(
            occupied_count, factor_one, factor_two, vec_oth
        )

        def weight_of(occ, side):
            occ = occ[:, :3, :n_orbs].astype(jnp.float32)
            occ = (occ[:, 0] + occ[:, 1]) + occ[:, 2]
            index = (jnp.arange(16, dtype=jnp.int32)[:, None] * 2 + side) * n_orbs
            index = index + jnp.arange(n_orbs, dtype=jnp.int32)[None]
            occ = jnp.where(index < count[0], occ / math.sqrt(OCC), jnp.float32(0.0))
            return occ.reshape(16 * n_orbs, 1)

        weight_own, weight_oth = weight_of(occ_own, xl), weight_of(occ_oth, 1 - xl)
        vecs = by_xl(vec_own.reshape(16, 2, n_all, half), vec_oth.reshape(16, 2, n_all, half), 2)
        vecs = vecs.transpose(1, 0, 2, 3, 4)
        vec_two = vecs.reshape(2, 32, 2, n_vec, half)[:, :, 1].reshape(2, pw, half)
        vecs = vecs.reshape(2, 2 * pw, half)
        vec_keep = lax.dynamic_index_in_dim(vecs, xl, 0, keepdims=False)
        vec_give = lax.dynamic_index_in_dim(vecs, 1 - xl, 0, keepdims=False)

        high = lax.Precision.HIGHEST
        at_v = jnp.arange(pw, dtype=jnp.int32)[:, None]
        at_q = jnp.arange(2 * pw, dtype=jnp.int32)[None]
        factor = jnp.zeros((2 * pw, 2 * pw), jnp.float32)
        for panel, one in enumerate((factor_one, factor_two)):
            spot = (at_v // n_vec) * 2 * n_vec + panel * n_vec + at_v % n_vec
            place_of = (at_q == spot).astype(jnp.float32)
            wide = dot(one, place_of, ((0,), (0,)), precision=high)
            factor = factor + dot(place_of, wide, ((0,), (0,)), precision=high)
        wide_high = wide.astype(bf16)
        wide_low = (wide - wide_high.astype(jnp.float32)).astype(bf16)
        vec_keep_x = lax.ppermute(vec_give, ("xl", "xh"), both_flip)
        keep, same_a, diff_a, vecs, vec_two, vec_keep = tie(
            keep, same_a, diff_a, vecs, vec_two, vec_keep
        )
        keep, weight_own, weight_oth, factor, wide_high, wide_low = tie(
            keep, weight_own, weight_oth, factor, wide_high, wide_low
        )
        keep = keep.reshape(16 * n_orbs, half)

    with jax.named_scope("project"):
        cross_a = swap(keep[:quarter], "xh")
        parts = project(side_xl, give, keep, vecs, vec_two)
        summed = exchange(parts, ZYC)
        keep_c, same_a_c, diff_a_c, vec_keep_c = (
            swap(v, "c") for v in (keep, same_a, diff_a, vec_keep)
        )
        summed, cross_a, keep_c, same_a_c, diff_a_c, vec_keep_c, vec_keep_x = tie(
            summed, cross_a, keep_c, same_a_c, diff_a_c, vec_keep_c, vec_keep_x
        )
        summed = summed.astype(jnp.float32).sum(0)
        summed = summed + swap(summed, "xh")
        summed, late = tie(summed, keep)

    with jax.named_scope("coefficients"):
        share = dot(summed[:, : 2 * pw], factor, ((1,), (0,)), precision=high)
        share = jnp.concatenate([share, summed[:, 2 * pw :]], axis=1).astype(bf16)
        every = exchange(jnp.broadcast_to(share[None], (32,) + share.shape), ZYC)
        cross_b = swap(late[quarter:], "xh")
        cross_a_c, vec_keep_xc = swap(cross_a, "c"), swap(vec_keep_x, "c")
        every, cross_b, cross_a_c, vec_keep_xc, give_b = tie(
            every, cross_b, cross_a_c, vec_keep_xc, give_b
        )
        coeffs, coeffs_half, update = expand(place, every, wide_high, wide_low, vecs, n_orbs)

    with jax.named_scope("transpose_out"):
        back = exchange(update, ZY)

    with jax.named_scope("density"):
        coeffs_x = swap(coeffs_half, "xl")
        cross_b_c = swap(cross_b, "c")
        give_b, coeffs_half = tie(give_b, coeffs_half)
        same_b = swap(give_b, "xl")
        diff_b = lax.ppermute(give_b, ("xl", "xh"), both_flip)
        vec_sides = [vec_keep, vec_keep_c, vec_keep_x, vec_keep_xc]
        first = density_part(
            0,
            place,
            window,
            [coeffs],
            weight_own,
            [[keep], [keep_c], [cross_a, cross_b], [cross_a_c, cross_b_c]],
            vec_sides,
        )
        first, coeffs_x, same_b, diff_b = tie(first, coeffs_x, same_b, diff_b)
        coeffs_y = swap(coeffs_x, "c")
        same_b_c, diff_b_c = swap(same_b, "c"), swap(diff_b, "c")
        density = density_part(
            1,
            place,
            window,
            [coeffs_x, coeffs_y],
            weight_oth,
            [[same_a, same_b], [same_a_c, same_b_c], [diff_a, diff_b], [diff_a_c, diff_b_c]],
            vec_sides,
            first,
        )

    with jax.named_scope("subtract"):
        back, density = tie(back, density)
        out = subtract(eigvecs, back)
    return (out, density)


def cost(flops, bytes_accessed):
    return pl.CostEstimate(flops=flops, bytes_accessed=bytes_accessed, transcendentals=0)


def pack_kernel(side, orbs, panel_one, panel_two, extra, give, keep):
    parts, n_orbs, half = keep.shape
    n_all = 2 * panel_one.shape[0]
    vecs = jnp.concatenate([panel_one[...], panel_two[...]], axis=0)
    for part in range(parts):
        for out, which in ((keep, side[0]), (give, 1 - side[0])):
            at = pl.multiple_of((2 * part + which) * half, half)
            out[part, :n_orbs, :] = orbs[:, pl.ds(at, half)].astype(jnp.bfloat16)
        for which in range(2):
            at = (2 * part + which) * half
            rows = pl.ds(n_orbs + which * n_all, n_all)
            give[part, rows, :] = vecs[:, at : at + half]
        give[part, pl.ds(n_orbs + 2 * n_all, 16), :] = extra[...]


def pack(side, orbs, panel_one, panel_two, extra, chunk):
    n_orbs, n_basis = orbs.shape
    n_vec = panel_one.shape[0]
    parts, half = n_basis // chunk, chunk // 2
    step = 4

    def split(value):
        return pl.BlockSpec((value.shape[0], step * chunk), lambda i, _: (0, i))

    n_give = n_orbs + 4 * n_vec + 16
    return pl.pallas_call(
        pack_kernel,
        out_shape=(
            jax.ShapeDtypeStruct((parts, n_give, half), jnp.bfloat16),
            jax.ShapeDtypeStruct((parts, n_orbs, half), jnp.bfloat16),
        ),
        grid_spec=pltpu.PrefetchScalarGridSpec(
            num_scalar_prefetch=1,
            grid=(parts // step,),
            in_specs=[split(orbs), split(panel_one), split(panel_two)]
            + [pl.BlockSpec(extra.shape, lambda i, _: (0, 0))],
            out_specs=(
                pl.BlockSpec((step, n_give, half), lambda i, _: (i, 0, 0)),
                pl.BlockSpec((step, n_orbs, half), lambda i, _: (i, 0, 0)),
            ),
        ),
        compiler_params=pltpu.CompilerParams(vmem_limit_bytes=60 * 2**20),
        cost_estimate=cost(0, 7 * n_orbs * n_basis),
        name="pack",
    )(side, orbs, panel_one, panel_two, extra)


def subtract_kernel(orbs, update, out):
    parts, _, chunk = update.shape
    for part in range(parts):
        at = pl.ds(part * chunk, chunk)
        out[:, at] = orbs[:, at] - update[part].astype(jnp.float32)


def subtract(orbs, update):
    n_orbs, n_basis = orbs.shape
    parts, _, chunk = update.shape
    step = 4
    block = pl.BlockSpec((n_orbs, step * chunk), lambda i: (0, i))
    return pl.pallas_call(
        subtract_kernel,
        out_shape=jax.ShapeDtypeStruct(orbs.shape, jnp.float32),
        grid=(parts // step,),
        in_specs=[block, pl.BlockSpec((step, n_orbs, chunk), lambda i: (i, 0, 0))],
        out_specs=block,
        compiler_params=pltpu.CompilerParams(vmem_limit_bytes=60 * 2**20),
        cost_estimate=cost(n_orbs * n_basis, 10 * n_orbs * n_basis),
        name="subtract_update",
    )(orbs, update)


def project_kernel(side, give, keep, vecs, vec_two, out):
    blocks, n_own, lanes = out.shape
    width = vecs.shape[1]
    proj = dot(give[...], vecs[1 - side[0]], ((1,), (1,)))
    proj = proj + dot(keep[...], vecs[side[0]], ((1,), (1,)))
    out[:, :, :width] = proj.astype(jnp.bfloat16).reshape(blocks, n_own, width)
    cross = dot(vecs[0], vec_two[0], ((1,), (1,)))
    cross = cross + dot(vecs[1], vec_two[1], ((1,), (1,)))
    out[:, :, width:] = cross.astype(jnp.bfloat16).reshape(blocks, n_own, lanes - width)


def project(side, give, keep, vecs, vec_two):
    n_orbs, half = give.shape
    width, n_two = vecs.shape[1], vec_two.shape[1]
    tile, lanes = n_orbs // 2, n_two // 2
    return pl.pallas_call(
        project_kernel,
        out_shape=jax.ShapeDtypeStruct((32, n_orbs // 32, width + lanes), jnp.bfloat16),
        grid_spec=pltpu.PrefetchScalarGridSpec(
            num_scalar_prefetch=1,
            grid=(2,),
            in_specs=[
                pl.BlockSpec((tile, half), lambda i, _: (i, 0)),
                pl.BlockSpec((tile, half), lambda i, _: (i, 0)),
                pl.BlockSpec(vecs.shape, lambda i, _: (0, 0, 0)),
                pl.BlockSpec((2, lanes, half), lambda i, _: (0, i, 0)),
            ],
            out_specs=pl.BlockSpec((16, n_orbs // 32, width + lanes), lambda i, _: (i, 0, 0)),
        ),
        compiler_params=pltpu.CompilerParams(vmem_limit_bytes=18 * 2**20),
        cost_estimate=cost(4 * n_orbs * width * half, 6 * 2**20),
        name="project",
    )(side, give, keep, vecs, vec_two)


def expand_kernel(place, every, wide_high, wide_low, vecs, coeffs, mine, update, mixed):
    width, half = vecs.shape[1:]
    step = pl.program_id(0)
    blocks, n_own = every.shape[0] // 2, every.shape[1]

    @pl.when(step == 0)
    def _():
        lanes = every.shape[2] - width
        total = None
        for part in range(2):
            cross = every[part * blocks : (part + 1) * blocks, :, width:].reshape(width, lanes)
            at = pl.ds(part * lanes, lanes)
            for wide in (wide_high, wide_low):
                term = dot(cross, wide[at, :], ((1,), (0,)))
                total = term if total is None else total + term
        row = lax.broadcasted_iota(jnp.int32, total.shape, 0)
        first = jnp.bitwise_and(lax.shift_right_logical(row, 3), 1) == 0
        mixed[...] = jnp.where(first, total, 0.0).astype(jnp.bfloat16)

    base = every[pl.ds(step * blocks, blocks), :, :width].reshape(blocks * n_own, width)
    fixed = base.astype(jnp.float32) - dot(base, mixed[...], ((1,), (0,)))
    fixed = fixed.astype(jnp.bfloat16)
    coeffs[...] = fixed

    @pl.when(step == place[1])
    def _():
        mine[...] = fixed

    for part in range(2):
        new = dot(fixed, vecs[part], ((1,), (0,))).astype(jnp.bfloat16)
        update[:, :, part * half : (part + 1) * half] = new.reshape(update.shape[:2] + (half,))


def expand(place, every, wide_high, wide_low, vecs, n_orbs):
    _, width, half = vecs.shape
    total = every.shape[0] * every.shape[1]

    def whole(value):
        zeros = (0,) * value.ndim
        return pl.BlockSpec(value.shape, lambda i, _: zeros, pipeline_mode=pl.Buffered(1))

    return pl.pallas_call(
        expand_kernel,
        out_shape=(
            jax.ShapeDtypeStruct((total, width), jnp.bfloat16),
            jax.ShapeDtypeStruct((total // 2, width), jnp.bfloat16),
            jax.ShapeDtypeStruct((16, n_orbs, 2 * half), jnp.bfloat16),
        ),
        grid_spec=pltpu.PrefetchScalarGridSpec(
            num_scalar_prefetch=1,
            grid=(2,),
            in_specs=[whole(value) for value in (every, wide_high, wide_low, vecs)],
            out_specs=(
                pl.BlockSpec((total // 2, width), lambda i, _: (i, 0)),
                pl.BlockSpec((total // 2, width), lambda i, _: (0, 0)),
                pl.BlockSpec((8, n_orbs, 2 * half), lambda i, _: (i, 0, 0)),
            ),
            scratch_shapes=[pltpu.VMEM((width, width), jnp.bfloat16)],
        ),
        compiler_params=pltpu.CompilerParams(vmem_limit_bytes=18 * 2**20),
        cost_estimate=cost(2 * total * width * (width + 2 * half), 6 * 2**20),
        name="expand",
    )(place, every, wide_high, wide_low, vecs)


def density_kernel(n_factors, counts, place, win_orbs, win_vecs, *refs):
    factors, refs = refs[:n_factors], refs[n_factors:]
    weight, refs = refs[0], refs[1:]
    orbs = []
    for n in counts:
        orbs.append(refs[:n])
        refs = refs[n:]
    vecs, refs = refs[:4], refs[4:]
    so_far = refs[0] if n_factors == 2 else None
    out, weighted, coeffs = refs[-3:]
    n_half, width = coeffs.shape
    tile = win_orbs.shape[2]

    @pl.when(pl.program_id(0) == 0)
    def _():
        if n_factors == 1:
            coeffs[...] = factors[0][...]
        else:
            for core, factor in ((place[1], factors[0]), (1 - place[1], factors[1])):
                to = pl.multiple_of(core * (n_half // 2), n_half // 2)
                coeffs[pl.ds(to, n_half // 2), :] = factor[...]
        for side in range(4):
            rows = n_half // len(orbs[side])
            for i, piece in enumerate(orbs[side]):
                at = pl.ds(i * rows, rows)
                update = dot(coeffs[at, :], vecs[side][...], ((1,), (0,)))
                new = piece[...].astype(jnp.float32) - update
                weighted[side, at, :] = (new * weight[at, :]).astype(jnp.bfloat16)

    update = dot(coeffs[...], win_vecs[...].reshape(width, tile), ((1,), (0,)))
    turned = win_orbs[...].reshape(n_half, tile).astype(jnp.float32) - update
    turned = turned.astype(jnp.bfloat16).T
    for block in range(4):
        side = jnp.bitwise_xor(place[0], block)
        total = dot(turned, weighted[side], ((1,), (0,)))
        if so_far is not None:
            total = total + so_far[:, block, :]
        out[:, block, :] = total


def density_part(part, place, window, factors, weight, orbs, vecs, so_far=None):
    rows = window.shape[2]
    n_half, width = weight.shape[0], vecs[0].shape[1]
    n_vec, n_orbs = vecs[0].shape[0] // 16, n_half // 16
    flat = [piece for side in orbs for piece in side]
    operands = [*factors, weight, *flat, *vecs]
    specs = [
        pl.BlockSpec((16, n_orbs, TILE), lambda i, _: (0, part, i)),
        pl.BlockSpec((16, n_vec, TILE), lambda i, _: (0, 2 * n_orbs // n_vec, i)),
    ]
    specs += [
        pl.BlockSpec(value.shape, lambda i, _: (0, 0), pipeline_mode=pl.Buffered(1))
        for value in operands
    ]
    block = pl.BlockSpec((TILE, 4, width), lambda i, _: (i, 0, 0))
    aliases = {}
    if so_far is not None:
        specs.append(block)
        operands.append(so_far)
        aliases = {2 + len(operands): 0}
    kernel = functools.partial(density_kernel, len(factors), [len(side) for side in orbs])
    return pl.pallas_call(
        kernel,
        out_shape=jax.ShapeDtypeStruct((rows, 4, width), jnp.float32),
        grid_spec=pltpu.PrefetchScalarGridSpec(
            num_scalar_prefetch=1,
            grid=(rows // TILE,),
            in_specs=specs,
            out_specs=block,
            scratch_shapes=[
                pltpu.VMEM((4, n_half, width), jnp.bfloat16),
                pltpu.VMEM((n_half, vecs[0].shape[0]), jnp.bfloat16),
            ],
        ),
        input_output_aliases=aliases,
        compiler_params=pltpu.CompilerParams(vmem_limit_bytes=60 * 2**20),
        cost_estimate=cost(2 * rows * n_half * (4 * width + 1024), 20 * 2**20),
        name="density_own" if part == 0 else "density_other",
    )(place, window, window, *operands)


def solution(mesh):
    mesh = Mesh(mesh.devices.reshape(4, 4, 2, 2, 2), ("z", "y", "xl", "xh", "c"))
    slab, grid = ("z", "y", "xl"), ("xh", "c")
    both = P(slab, grid)
    in_specs = (both, both, both, P(), P(), P(slab), P(), P())
    out_specs = (both, P(grid, None, slab))
    return jax.shard_map(body, mesh=mesh, in_specs=in_specs, out_specs=out_specs, check_vma=False)
```

time: 312 us -> 246 us (0.79)
  blocking collectives: 39 us -> 0 us
  Pallas kernels: 25.6 us -> 51.4 us
  other arithmetic: 30.9 us -> 11.7 us
  waiting for transfers between devices: 99.1 us -> 82.8 us
  matrix products: 17.7 us -> 6.06 us
  local copies, waits for them, and re-layouts: 32.5 us -> 22.1 us
  starting transfers between devices: 50.7 us -> 54.8 us
    all_to_all x4 -> x5, waiting for transfers between devices: 46.9 us -> 5.23 us  [exchange(): return lax.all_to_all(values, axes, 0, 0, tiled=True)]
    all_to_all x1 -> x0, blocking collectives: 39 us -> none  [exchange(): return lax.all_to_all(values, axes, 0, 0, tiled=True)]
    pallas_call x1 -> x6, Pallas kernels: 25.6 us -> 51.4 us  [the longest x2 34.6 us: density_part(): pl.pallas_call(kernel, out_shape=jax.ShapeDtypeStruct((rows, 4, width), j...]
    ppermute x1 -> x4, waiting for transfers between devices: 0.01 us -> 16.7 us  [the longest x1 12.1 us: body(): vec_keep_x = lax.ppermute(vec_give, ('xl', 'xh'), both_flip)]
    ppermute x16 -> x21, starting transfers between devices: 26 us -> 10.7 us  [swap(): return lax.ppermute(values, axis, [(0, 1), (1, 0)])]
    all_to_all x4 -> x5, starting transfers between devices: 22.3 us -> 35.4 us  [exchange(): return lax.all_to_all(values, axes, 0, 0, tiled=True)]
    dot_general x9 -> x5, matrix products: 17.7 us -> 6.06 us  [dot(): lax.dot_general(left, right, (dims, ((), ())), preferred_element_type=jnp...]
    convert_element_type x4 -> x1, local copies, waits for them, and re-layouts: 12.5 us -> 1.45 us  [cut(): lax.dynamic_slice_in_dim(v, at, rows, 1).astype(bf16)]
  transfers between devices with their start and end apart: 22 -> 31, of which waited for: 10 -> 16; matrix products, arithmetic and copies ran while one was open for 20% -> 11% of each run, Pallas kernels for 0% -> 17%
where the time goes in v3:
time: 246 us; the launch traced here: 245 us
  waiting for transfers between devices  82.8 us (34%)
  starting transfers between devices  54.8 us (22%)
  Pallas kernels  51.4 us (21%)
  local copies, waits for them, and re-layouts  22.1 us (9%)
  between operations  15.8 us (6%)
  other arithmetic  11.7 us (5%)
  matrix products  6.06 us (2%)
    ppermute x21, waiting for transfers between devices, swap(): return lax.ppermute(values, axis, [(0, 1), (1, 0)])  60.8 us
    all_to_all x5, starting transfers between devices, exchange(): return lax.all_to_all(values, axes, 0, 0, tiled=True)  35.4 us
    pallas_call x2, Pallas kernels, density_part(): pl.pallas_call(kernel, out_shape=jax.ShapeDtypeStruct((rows, 4, width), j...  34.6 us
    ppermute x1, waiting for transfers between devices, body(): vec_keep_x = lax.ppermute(vec_give, ('xl', 'xh'), both_flip)  12.1 us
    ppermute x21, starting transfers between devices, swap(): return lax.ppermute(values, axis, [(0, 1), (1, 0)])  10.7 us
    unnamed x52, local copies, waits for them, and re-layouts  10.5 us
    dot_general x5, matrix products, dot(): lax.dot_general(left, right, (dims, ((), ())), preferred_element_type=jnp...  6.06 us
    all_to_all x5, waiting for transfers between devices, exchange(): return lax.all_to_all(values, axes, 0, 0, tiled=True)  5.23 us
  transfers between devices with their start and end apart: 31, of which 16 were waited for; matrix products, arithmetic and copies ran while one was open for 11% of the time, Pallas kernels for 17%

profile of v3, /device:TPU:1, one launch (start us, length us, event | category | flops | bytes accessed | tf_op | source)
XLA Modules:
  0.0 244.7 jit_solution(15924450233879879744)
XLA Ops:
  8.5 4.6 %pack.1 = (bf16[16,112,512]{2,1,0:T(8,128)(2,1)}, bf16[16,64,512]{2,1,0:T(8,128)(2,1)}) custom-call(s32[1]{0:T(128)} %bitcast.2.side, f32[64,16384]{1,0:T(8,128)} %orbs.3, bf16[8,16384]{1,0:T(8,128)(2,1)} %panel_one.1, bf16[8,16384]{1,0:T(8,128)(2,1)} %panel_two.1, bf16[16,512]{1,0:T(8,128)(2,1)} %fusion.34.extra), custom_call_target="tpu_custom_call" | custom-call | bytes 7340032 | tf_op jit(solution)/shard_map/pack/pack/pallas_call | solution.py:244
  13.2 8.6 %all-to-all-start = ((bf16[16,112,512]{2,1,0:T(8,128)(2,1)}), bf16[16,112,512]{2,1,0:T(8,128)(2,1)S(1)}, u32[]{:S(2)}, u32[]{:S(2)}) async-start(bf16[16,112,512]{2,1,0:T(8,128)(2,1)} %get-tuple-element.60), calls=%async_computation | async-start | bytes 3670016 | tf_op jit(solution)/shard_map/transpose_give/all_to_all | solution.py:30
  22.5 1.6 constant_dynamic-slice_fusion
  24.1 1.5 dynamic-slice_convert_fusion
  26.7 3.8 %collective-permute-start.2 = (bf16[80,1024]{1,0:T(8,128)(2,1)S(1)}, bf16[80,1024]{1,0:T(8,128)(2,1)S(1)}, u32[]{:S(2)}, u32[]{:S(2)}) collective-permute-start(bf16[80,1024]{1,0:T(8,128)(2,1)S(1)} %get-tuple-element.128), channel_id=1, source_target_pairs={{0,3},{1,2},{2,1},{3,0},{4,7},{5,6},{6,5},{7,4},{8,11},{9,10},{10,... | collective-permute-start | bytes 491528 | tf_op jit(solution)/shard_map/window_exchange/ppermute | solution.py:87
  31.0 4.6 %collective-permute-done.2 = bf16[80,1024]{1,0:T(8,128)(2,1)S(1)} collective-permute-done((bf16[80,1024]{1,0:T(8,128)(2,1)S(1)}, bf16[80,1024]{1,0:T(8,128)(2,1)S(1)}, u32[]{:S(2)}, u32[]{:S(2)}) %collective-permute-start.2) | collective-permute-done | bytes 163872 | tf_op jit(solution)/shard_map/window_exchange/ppermute | solution.py:87
  35.5 3.4 %collective-permute-done.1 = bf16[80,1024]{1,0:T(8,128)(2,1)S(1)} collective-permute-done((bf16[80,1024]{1,0:T(8,128)(2,1)S(1)}, bf16[80,1024]{1,0:T(8,128)(2,1)S(1)}, u32[]{:S(2)}, u32[]{:S(2)}) %collective-permute-start.1) | collective-permute-done | bytes 163872 | tf_op jit(solution)/shard_map/window_exchange/ppermute | solution.py:26
  40.9 5.1 %collective-permute-done.3 = bf16[80,1024]{1,0:T(8,128)(2,1)S(1)} collective-permute-done((bf16[80,1024]{1,0:T(8,128)(2,1)S(1)}, bf16[80,1024]{1,0:T(8,128)(2,1)S(1)}, u32[]{:S(2)}, u32[]{:S(2)}) %collective-permute-start.3) | collective-permute-done | bytes 163872 | tf_op jit(solution)/shard_map/window_exchange/ppermute | solution.py:26
  46.9 1.6 all-to-all-done
  49.9 1.2 lt.87
  53.9 2.5 %collective-permute-start.5 = (bf16[512,512]{1,0:T(8,128)(2,1)}, bf16[512,512]{1,0:T(8,128)(2,1)}, u32[]{:S(2)}, u32[]{:S(2)}) collective-permute-start(bf16[512,512]{1,0:T(8,128)(2,1)} %bitcast.11), channel_id=1, source_target_pairs={{0,6},{2,4},{4,2},{6,0},{1,7},{3,5},{5,3},{7,1},{8,14},{10,12},{12... | collective-permute-start | bytes 1572872 | tf_op jit(solution)/shard_map/transpose_keep/ppermute | solution.py:110
  56.4 4.7 %all-to-all-start.1 = ((bf16[16,64,512]{2,1,0:T(8,128)(2,1)}), bf16[16,64,512]{2,1,0:T(8,128)(2,1)S(1)}, u32[]{:S(2)}, u32[]{:S(2)}) async-start(bf16[16,64,512]{2,1,0:T(8,128)(2,1)} %get-tuple-element.64), calls=%async_computation.1 | async-start | bytes 2097152 | tf_op jit(solution)/shard_map/transpose_keep/all_to_all | solution.py:30
  61.0 1.3 collective-permute-start.7
  63.9 1.8 broadcast_select_fusion.3.refs_1_
  65.7 3.5 %collective-permute-done.7 = bf16[16,16,128]{2,1,0:T(8,128)(2,1)} collective-permute-done((bf16[16,16,128]{2,1,0:T(8,128)(2,1)}, bf16[16,16,128]{2,1,0:T(8,128)(2,1)}, u32[]{:S(2)}, u32[]{:S(2)}) %collective-permute-start.7) | collective-permute-done | bytes 65568 | tf_op jit(solution)/shard_map/transpose_keep/ppermute | solution.py:26
  71.3 9.0 %collective-permute-done.6 = bf16[16,32,512]{2,1,0:T(8,128)(2,1)S(1)} collective-permute-done((bf16[16,32,512]{2,1,0:T(8,128)(2,1)}, bf16[16,32,512]{2,1,0:T(8,128)(2,1)S(1)}, u32[]{:S(2)}, u32[]{:S(2)}) %collective-permute-start.6) | collective-permute-done | bytes 524320 | tf_op jit(solution)/shard_map/transpose_keep/ppermute | solution.py:26
  80.3 1.6 fusion.2
  81.9 1.3 subtract_convert_fusion
  83.2 1.3 broadcast_select_fusion.1
  84.7 1.1 dynamic-slice_bitcast_fusion
  87.4 1.7 convolution_add_fusion
  89.1 1.4 copy-done.4
  90.5 2.1 project.1
  93.7 8.2 %all-to-all-start.2 = ((bf16[32,32,640]{2,1,0:T(8,128)(2,1)}), bf16[32,32,640]{2,1,0:T(8,128)(2,1)}, u32[]{:S(2)}, u32[]{:S(2)}) async-start(bf16[32,32,640]{2,1,0:T(8,128)(2,1)} %copy-done.3), calls=%async_computation.2 | async-start | bytes 2621440 | tf_op jit(solution)/shard_map/project/all_to_all | solution.py:30
  101.9 1.2 collective-permute-start.13
  104.6 12.1 %collective-permute-done.13.refs_10_.refs_13_ = bf16[512,512]{1,0:T(8,128)(2,1)S(1)} collective-permute-done((bf16[512,512]{1,0:T(8,128)(2,1)}, bf16[512,512]{1,0:T(8,128)(2,1)S(1)}, u32[]{:S(2)}, u32[]{:S(2)}) %collective-permute-start.13) | collective-permute-done | bytes 524320 | tf_op jit(solution)/shard_map/transpose_keep/ppermute | solution.py:142
  118.4 12.2 %collective-permute-done.8.refs_4_ = bf16[512,512]{1,0:T(8,128)(2,1)S(1)} collective-permute-done((bf16[512,512]{1,0:T(8,128)(2,1)S(1)}, bf16[512,512]{1,0:T(8,128)(2,1)S(1)}, u32[]{:S(2)}, u32[]{:S(2)}) %collective-permute-start.8) | collective-permute-done | bytes 524320 | tf_op jit(solution)/shard_map/project/ppermute | solution.py:26
  131.5 1.5 convert_reduce_fusion
  133.5 4.4 %collective-permute-done.14 = f32[32,640]{1,0:T(8,128)S(1)} collective-permute-done((f32[32,640]{1,0:T(8,128)S(1)}, f32[32,640]{1,0:T(8,128)S(1)}, u32[]{:S(2)}, u32[]{:S(2)}) %collective-permute-start.14) | collective-permute-done | bytes 81952 | tf_op jit(solution)/shard_map/project/ppermute | solution.py:26
  138.6 1.2 broadcast_in_dim.8
  139.8 10.2 %all-to-all-start.3 = ((bf16[32,32,640]{2,1,0:T(8,128)(2,1)}), bf16[32,32,640]{2,1,0:T(8,128)(2,1)}, u32[]{:S(2)}, u32[]{:S(2)}) async-start(bf16[32,32,640]{2,1,0:T(8,128)(2,1)} %broadcast_in_dim.8), calls=%async_computation.3 | async-start | bytes 2621440 | tf_op jit(solution)/shard_map/coefficients/all_to_all | solution.py:30
  150.7 1.5 collective-permute-done.16.refs_6_
  153.8 11.7 %collective-permute-done.15.refs_5_ = bf16[512,512]{1,0:T(8,128)(2,1)} collective-permute-done((bf16[512,512]{1,0:T(8,128)(2,1)S(1)}, bf16[512,512]{1,0:T(8,128)(2,1)}, u32[]{:S(2)}, u32[]{:S(2)}) %collective-permute-start.15) | collective-permute-done | bytes 524320 | tf_op jit(solution)/shard_map/coefficients/ppermute | solution.py:26
  165.5 3.6 %all-to-all-done.3.every = bf16[32,32,640]{2,1,0:T(8,128)(2,1)} async-done(((bf16[32,32,640]{2,1,0:T(8,128)(2,1)}), bf16[32,32,640]{2,1,0:T(8,128)(2,1)}, u32[]{:S(2)}, u32[]{:S(2)}) %all-to-all-start.3) | async-done | bytes 1310752 | tf_op jit(solution)/shard_map/coefficients/all_to_all | solution.py:30
  169.2 1.9 collective-permute-start.18
  171.2 4.9 %expand.1 = (bf16[1024,512]{1,0:T(8,128)(2,1)S(1)}, bf16[512,512]{1,0:T(8,128)(2,1)S(1)}, bf16[16,64,1024]{2,1,0:T(8,128)(2,1)S(1)}) custom-call(s32[2]{0:T(128)S(1)} %pad_add_fusion.place, bf16[32,32,640]{2,1,0:T(8,128)(2,1)} %all-to-all-done.3.every, bf16[256,512]{1,0:T(8,128)(2,1)S(1)} %copy-done.8, bf16[256,512]{1,0:T(8,128)(2,1)S(1)} %copy-done.7, ...), custom_call_target="tpu_custom_call" | custom-call | flops 1610612736 | bytes 6291456 | tf_op jit(solution)/shard_map/coefficients/expand/pallas_call | solution.py:366
  176.1 1.3 copy-done.5
  178.4 3.7 %all-to-all-start.4 = ((bf16[16,64,1024]{2,1,0:T(8,128)(2,1)}), bf16[16,64,1024]{2,1,0:T(8,128)(2,1)S(1)}, u32[]{:S(2)}, u32[]{:S(2)}) async-start(bf16[16,64,1024]{2,1,0:T(8,128)(2,1)} %copy-done.5), calls=%async_computation.4 | async-start | bytes 4194304 | tf_op jit(solution)/shard_map/transpose_out/all_to_all | solution.py:30
  182.2 1.2 collective-permute-start.21
  183.4 1.5 collective-permute-start.19
  184.8 16.5 %density_own.1.refs_15_ = f32[1024,4,512]{2,1,0:T(4,128)} custom-call(s32[2]{0:T(128)} %copy-done.9, bf16[16,160,1024]{2,1,0:T(8,128)(2,1)} %bitcast.54, bf16[16,160,1024]{2,1,0:T(8,128)(2,1)} %bitcast.55, bf16[1024,512]{1,0:T(8,128)(2,1)} %copy-done.6, f32[1024,1]{1,0:T(8,128)} %broadcast_select_fusion.3.refs_1_, bf16[1024,512]{1,0:T(8,128)(2,1)} %bitcast.48, ...), custom_call_target="tpu_custom_call" | custom-call | flops 6442450944 | bytes 20971520 | tf_op jit(solution)/shard_map/density/density_own/pallas_call | solution.py:451
  201.4 6.8 %collective-permute-done.19.refs_0_ = bf16[512,512]{1,0:T(8,128)(2,1)} collective-permute-done((bf16[512,512]{1,0:T(8,128)(2,1)S(1)}, bf16[512,512]{1,0:T(8,128)(2,1)}, u32[]{:S(2)}, u32[]{:S(2)}) %collective-permute-start.19) | collective-permute-done | bytes 524320 | tf_op jit(solution)/shard_map/density/ppermute | solution.py:26
  208.2 1.1 collective-permute-start.22
  209.8 1.2 collective-permute-done.22.refs_1_
  211.0 1.5 collective-permute-done.23.refs_6_
  213.3 18.1 %density_other.1 = f32[1024,4,512]{2,1,0:T(4,128)} custom-call(s32[2]{0:T(128)} %copy-done.9, bf16[16,160,1024]{2,1,0:T(8,128)(2,1)} %bitcast.56, bf16[16,160,1024]{2,1,0:T(8,128)(2,1)} %bitcast.57, bf16[512,512]{1,0:T(8,128)(2,1)} %collective-permute-done.19.refs_0_, bf16[512,512]{1,0:T(8,128)(2,1)} %copy-done.21, ...), custom_call_target="tpu_custom_call", output_to_operand_aliasing={{}: (18, {})} | custom-call | flops 6442450944 | bytes 20971520 | tf_op jit(solution)/shard_map/density/density_other/pallas_call | solution.py:451
  231.4 1.3 copy-done.11
  232.7 5.2 %subtract_update.1 = f32[64,16384]{1,0:T(8,128)} custom-call(f32[64,16384]{1,0:T(8,128)} %orbs.3, bf16[16,64,1024]{2,1,0:T(8,128)(2,1)} %copy-done.11), custom_call_target="tpu_custom_call" | custom-call | flops 1048576 | bytes 10485760 | tf_op jit(solution)/shard_map/subtract/subtract_update/pallas_call | solution.py:278
  (123 shorter events, 25.6 us)
Async XLA Ops:
  7.2 74.7 %copy-start = (f32[256,256]{1,0:T(8,128)S(1)}, f32[256,256]{1,0:T(8,128)}, u32[]{:S(2)}) copy-start(f32[256,256]{1,0:T(8,128)} %param.14) | copy-start | bytes 786436
  13.2 35.3 %all-to-all-start = ((bf16[16,112,512]{2,1,0:T(8,128)(2,1)}), bf16[16,112,512]{2,1,0:T(8,128)(2,1)S(1)}, u32[]{:S(2)}, u32[]{:S(2)}) async-start(bf16[16,112,512]{2,1,0:T(8,128)(2,1)} %get-tuple-element.60), calls=%async_computation | async-start | bytes 3670016 | tf_op jit(solution)/shard_map/transpose_give/all_to_all | solution.py:30
  21.8 163.1 %all-gather.3.cloned.1.call-start = ((), (), s32[]{:S(2)}) async-start(), calls=%async_computation.5 | async-start | bytes 5570560 | tf_op jit(solution)/shard_map/window_exchange/all_gather | solution.py:98
  26.7 8.9 %collective-permute-start.2 = (bf16[80,1024]{1,0:T(8,128)(2,1)S(1)}, bf16[80,1024]{1,0:T(8,128)(2,1)S(1)}, u32[]{:S(2)}, u32[]{:S(2)}) collective-permute-start(bf16[80,1024]{1,0:T(8,128)(2,1)S(1)} %get-tuple-element.128), channel_id=1, source_target_pairs={{0,3},{1,2},{2,1},{3,0},{4,7},{5,6},{6,5},{7,4},{8,11},{9,10},{10,... | collective-permute-start | bytes 491528 | tf_op jit(solution)/shard_map/window_exchange/ppermute | solution.py:87
  30.5 8.4 %collective-permute-start.1 = (bf16[80,1024]{1,0:T(8,128)(2,1)S(1)}, bf16[80,1024]{1,0:T(8,128)(2,1)S(1)}, u32[]{:S(2)}, u32[]{:S(2)}) collective-permute-start(bf16[80,1024]{1,0:T(8,128)(2,1)S(1)} %get-tuple-element.129), channel_id=1, source_target_pairs={{0,2},{2,0},{1,3},{3,1},{4,6},{6,4},{5,7},{7,5},{8,10},{10,8},{9,1... | collective-permute-start | bytes 491528 | tf_op jit(solution)/shard_map/window_exchange/ppermute | solution.py:26
  30.7 8.2 %collective-permute-start = (bf16[80,1024]{1,0:T(8,128)(2,1)S(1)}, bf16[80,1024]{1,0:T(8,128)(2,1)S(1)}, u32[]{:S(2)}, u32[]{:S(2)}) collective-permute-start(bf16[80,1024]{1,0:T(8,128)(2,1)S(1)} %get-tuple-element.130), channel_id=1, source_target_pairs={{0,1},{1,0},{2,3},{3,2},{4,5},{5,4},{6,7},{7,6},{8,9},{9,8},{10,11... | collective-permute-start | bytes 491528 | tf_op jit(solution)/shard_map/window_exchange/ppermute | solution.py:26
  40.0 6.1 %collective-permute-start.3 = (bf16[80,1024]{1,0:T(8,128)(2,1)S(1)}, bf16[80,1024]{1,0:T(8,128)(2,1)S(1)}, u32[]{:S(2)}, u32[]{:S(2)}) collective-permute-start(bf16[80,1024]{1,0:T(8,128)(2,1)S(1)} %fusion.24), channel_id=1, source_target_pairs={{0,4},{4,0},{1,5},{5,1},{2,6},{6,2},{3,7},{7,3},{8,12},{12,8},{9,1... | collective-permute-start | bytes 491528 | tf_op jit(solution)/shard_map/window_exchange/ppermute | solution.py:26
  48.5 4.3 %copy-start.10 = (bf16[16,112,512]{2,1,0:T(8,128)(2,1)}, bf16[16,112,512]{2,1,0:T(8,128)(2,1)S(1)}, u32[]{:S(2)}) copy-start(bf16[16,112,512]{2,1,0:T(8,128)(2,1)S(1)} %all-to-all-done) | copy-start | bytes 5505028
  53.9 35.2 %collective-permute-start.5 = (bf16[512,512]{1,0:T(8,128)(2,1)}, bf16[512,512]{1,0:T(8,128)(2,1)}, u32[]{:S(2)}, u32[]{:S(2)}) collective-permute-start(bf16[512,512]{1,0:T(8,128)(2,1)} %bitcast.11), channel_id=1, source_target_pairs={{0,6},{2,4},{4,2},{6,0},{1,7},{3,5},{5,3},{7,1},{8,14},{10,12},{12... | collective-permute-start | bytes 1572872 | tf_op jit(solution)/shard_map/transpose_keep/ppermute | solution.py:110
  56.3 32.7 %collective-permute-start.4 = (bf16[512,512]{1,0:T(8,128)(2,1)}, bf16[512,512]{1,0:T(8,128)(2,1)}, u32[]{:S(2)}, u32[]{:S(2)}) collective-permute-start(bf16[512,512]{1,0:T(8,128)(2,1)} %bitcast.11), channel_id=1, source_target_pairs={{0,4},{4,0},{1,5},{5,1},{2,6},{6,2},{3,7},{7,3},{8,12},{12,8},{9,1... | collective-permute-start | bytes 1572872 | tf_op jit(solution)/shard_map/transpose_keep/ppermute | solution.py:26
  56.4 32.7 %all-to-all-start.1 = ((bf16[16,64,512]{2,1,0:T(8,128)(2,1)}), bf16[16,64,512]{2,1,0:T(8,128)(2,1)S(1)}, u32[]{:S(2)}, u32[]{:S(2)}) async-start(bf16[16,64,512]{2,1,0:T(8,128)(2,1)} %get-tuple-element.64), calls=%async_computation.1 | async-start | bytes 2097152 | tf_op jit(solution)/shard_map/transpose_keep/all_to_all | solution.py:30
  61.0 8.1 %collective-permute-start.7 = (bf16[16,16,128]{2,1,0:T(8,128)(2,1)}, bf16[16,16,128]{2,1,0:T(8,128)(2,1)}, u32[]{:S(2)}, u32[]{:S(2)}) collective-permute-start(bf16[16,16,128]{2,1,0:T(8,128)(2,1)} %slice.112), channel_id=1, source_target_pairs={{0,4},{4,0},{1,5},{5,1},{2,6},{6,2},{3,7},{7,3},{8,12},{12,8},{9,1... | collective-permute-start | bytes 196616 | tf_op jit(solution)/shard_map/transpose_keep/ppermute | solution.py:26
  63.6 16.6 %collective-permute-start.6 = (bf16[16,32,512]{2,1,0:T(8,128)(2,1)}, bf16[16,32,512]{2,1,0:T(8,128)(2,1)S(1)}, u32[]{:S(2)}, u32[]{:S(2)}) collective-permute-start(bf16[16,32,512]{2,1,0:T(8,128)(2,1)} %slice.106), channel_id=1, source_target_pairs={{0,4},{4,0},{1,5},{5,1},{2,6},{6,2},{3,7},{7,3},{8,12},{12,8},{9,1... | collective-permute-start | bytes 1572872 | tf_op jit(solution)/shard_map/transpose_keep/ppermute | solution.py:26
  80.3 1.6 copy-start.25
  89.1 61.5 %copy-start.2 = (bf16[16,64,512]{2,1,0:T(8,128)(2,1)}, bf16[16,64,512]{2,1,0:T(8,128)(2,1)S(1)}, u32[]{:S(2)}) copy-start(bf16[16,64,512]{2,1,0:T(8,128)(2,1)S(1)} %all-to-all-done.1) | copy-start | bytes 3145732
  89.1 1.4 copy-start.4
  93.7 10.6 %copy-start.12 = (bf16[512,512]{1,0:T(8,128)(2,1)S(1)}, bf16[512,512]{1,0:T(8,128)(2,1)}, u32[]{:S(2)}) copy-start(bf16[512,512]{1,0:T(8,128)(2,1)} %get-tuple-element.75.refs_8_.refs_11_) | copy-start | bytes 1572868
  93.7 37.8 %all-to-all-start.2 = ((bf16[32,32,640]{2,1,0:T(8,128)(2,1)}), bf16[32,32,640]{2,1,0:T(8,128)(2,1)}, u32[]{:S(2)}, u32[]{:S(2)}) async-start(bf16[32,32,640]{2,1,0:T(8,128)(2,1)} %copy-done.3), calls=%async_computation.2 | async-start | bytes 2621440 | tf_op jit(solution)/shard_map/project/all_to_all | solution.py:30
  101.9 14.8 %collective-permute-start.13 = (bf16[512,512]{1,0:T(8,128)(2,1)}, bf16[512,512]{1,0:T(8,128)(2,1)S(1)}, u32[]{:S(2)}, u32[]{:S(2)}) collective-permute-start(bf16[512,512]{1,0:T(8,128)(2,1)} %get-tuple-element.116), channel_id=1, source_target_pairs={{0,6},{2,4},{4,2},{6,0},{1,7},{3,5},{5,3},{7,1},{8,14},{10,12},{12... | collective-permute-start | bytes 1572872 | tf_op jit(solution)/shard_map/transpose_keep/ppermute | solution.py:142
  103.1 28.3 %collective-permute-start.9 = (bf16[1024,512]{1,0:T(8,128)(2,1)S(1)}, bf16[1024,512]{1,0:T(8,128)(2,1)}, u32[]{:S(2)}, u32[]{:S(2)}) collective-permute-start(bf16[1024,512]{1,0:T(8,128)(2,1)S(1)} %bitcast.46), channel_id=1, source_target_pairs={{0,1},{1,0},{2,3},{3,2},{4,5},{5,4},{6,7},{7,6},{8,9},{9,8},{10,11... | collective-permute-start | bytes 3145736 | tf_op jit(solution)/shard_map/project/ppermute | solution.py:26
  103.7 13.0 %collective-permute-start.10 = (bf16[512,512]{1,0:T(8,128)(2,1)}, bf16[512,512]{1,0:T(8,128)(2,1)S(1)}, u32[]{:S(2)}, u32[]{:S(2)}) collective-permute-start(bf16[512,512]{1,0:T(8,128)(2,1)} %collective-permute-done.4.refs_3_), channel_id=1, source_target_pairs={{0,1},{1,0},{2,3},{3,2},{4,5},{5,4},{6,7},{7,6},{8,9},{9,8},{10,11... | collective-permute-start | bytes 1572872 | tf_op jit(solution)/shard_map/project/ppermute | solution.py:26
  103.8 12.9 %collective-permute-start.11 = (bf16[512,512]{1,0:T(8,128)(2,1)}, bf16[512,512]{1,0:T(8,128)(2,1)S(1)}, u32[]{:S(2)}, u32[]{:S(2)}) collective-permute-start(bf16[512,512]{1,0:T(8,128)(2,1)} %collective-permute-done.5.refs_7_), channel_id=1, source_target_pairs={{0,1},{1,0},{2,3},{3,2},{4,5},{5,4},{6,7},{7,6},{8,9},{9,8},{10,11... | collective-permute-start | bytes 1572872 | tf_op jit(solution)/shard_map/project/ppermute | solution.py:26
  104.3 13.2 %collective-permute-start.12 = (bf16[512,512]{1,0:T(8,128)(2,1)S(1)}, bf16[512,512]{1,0:T(8,128)(2,1)S(1)}, u32[]{:S(2)}, u32[]{:S(2)}) collective-permute-start(bf16[512,512]{1,0:T(8,128)(2,1)S(1)} %copy-done.12), channel_id=1, source_target_pairs={{0,1},{1,0},{2,3},{3,2},{4,5},{5,4},{6,7},{7,6},{8,9},{9,8},{10,11... | collective-permute-start | bytes 1572872 | tf_op jit(solution)/shard_map/project/ppermute | solution.py:26
  116.7 13.9 %collective-permute-start.8 = (bf16[512,512]{1,0:T(8,128)(2,1)S(1)}, bf16[512,512]{1,0:T(8,128)(2,1)S(1)}, u32[]{:S(2)}, u32[]{:S(2)}) collective-permute-start(bf16[512,512]{1,0:T(8,128)(2,1)S(1)} %bitcast.60), channel_id=1, source_target_pairs={{0,2},{2,0},{1,3},{3,1},{4,6},{6,4},{5,7},{7,5},{8,10},{10,8},{9,1... | collective-permute-start | bytes 1572872 | tf_op jit(solution)/shard_map/project/ppermute | solution.py:26
  116.7 13.9 %copy-start.18 = (bf16[512,512]{1,0:T(8,128)(2,1)}, bf16[512,512]{1,0:T(8,128)(2,1)S(1)}, u32[]{:S(2)}) copy-start(bf16[512,512]{1,0:T(8,128)(2,1)S(1)} %collective-permute-done.10.refs_5_) | copy-start | bytes 1572868
  117.6 13.1 %copy-start.19 = (bf16[512,512]{1,0:T(8,128)(2,1)}, bf16[512,512]{1,0:T(8,128)(2,1)S(1)}, u32[]{:S(2)}) copy-start(bf16[512,512]{1,0:T(8,128)(2,1)S(1)} %collective-permute-done.11.refs_9_) | copy-start | bytes 1572868
  118.4 19.5 %copy-start.13 = (f32[512,512]{1,0:T(8,128)S(1)}, f32[512,512]{1,0:T(8,128)}, u32[]{:S(2)}) copy-start(f32[512,512]{1,0:T(8,128)} %convolution_add_fusion) | copy-start | bytes 3145732
  133.0 4.9 %collective-permute-start.14 = (f32[32,640]{1,0:T(8,128)S(1)}, f32[32,640]{1,0:T(8,128)S(1)}, u32[]{:S(2)}, u32[]{:S(2)}) collective-permute-start(f32[32,640]{1,0:T(8,128)S(1)} %convert_reduce_fusion), channel_id=1, source_target_pairs={{0,2},{2,0},{1,3},{3,1},{4,6},{6,4},{5,7},{7,5},{8,10},{10,8},{9,1... | collective-permute-start | bytes 245768 | tf_op jit(solution)/shard_map/project/ppermute | solution.py:26
  138.6 11.8 %copy-start.15 = (bf16[512,512]{1,0:T(8,128)(2,1)S(1)}, bf16[512,512]{1,0:T(8,128)(2,1)}, u32[]{:S(2)}) copy-start(bf16[512,512]{1,0:T(8,128)(2,1)} %copy-done.14) | copy-start | bytes 1572868
  139.8 31.4 %copy-start.7 = (bf16[256,512]{1,0:T(8,128)(2,1)S(1)}, bf16[256,512]{1,0:T(8,128)(2,1)}, u32[]{:S(2)}) copy-start(bf16[256,512]{1,0:T(8,128)(2,1)} %get-tuple-element.84.wide_low) | copy-start | bytes 786436
  139.8 31.4 %copy-start.8 = (bf16[256,512]{1,0:T(8,128)(2,1)S(1)}, bf16[256,512]{1,0:T(8,128)(2,1)}, u32[]{:S(2)}) copy-start(bf16[256,512]{1,0:T(8,128)(2,1)} %get-tuple-element.83.wide_high) | copy-start | bytes 786436
  139.8 29.4 %all-to-all-start.3 = ((bf16[32,32,640]{2,1,0:T(8,128)(2,1)}), bf16[32,32,640]{2,1,0:T(8,128)(2,1)}, u32[]{:S(2)}, u32[]{:S(2)}) async-start(bf16[32,32,640]{2,1,0:T(8,128)(2,1)} %broadcast_in_dim.8), calls=%async_computation.3 | async-start | bytes 2621440 | tf_op jit(solution)/shard_map/coefficients/all_to_all | solution.py:30
  150.0 2.2 collective-permute-start.16
  150.4 2.4 collective-permute-start.17
  150.6 14.9 %collective-permute-start.15 = (bf16[512,512]{1,0:T(8,128)(2,1)S(1)}, bf16[512,512]{1,0:T(8,128)(2,1)}, u32[]{:S(2)}, u32[]{:S(2)}) collective-permute-start(bf16[512,512]{1,0:T(8,128)(2,1)S(1)} %slice.121), channel_id=1, source_target_pairs={{0,2},{2,0},{1,3},{3,1},{4,6},{6,4},{5,7},{7,5},{8,10},{10,8},{9,1... | collective-permute-start | bytes 1572872 | tf_op jit(solution)/shard_map/coefficients/ppermute | solution.py:26
  169.2 15.7 %collective-permute-start.18 = (bf16[512,512]{1,0:T(8,128)(2,1)}, bf16[512,512]{1,0:T(8,128)(2,1)}, u32[]{:S(2)}, u32[]{:S(2)}) collective-permute-start(bf16[512,512]{1,0:T(8,128)(2,1)} %collective-permute-done.15.refs_5_), channel_id=1, source_target_pairs={{0,1},{1,0},{2,3},{3,2},{4,5},{5,4},{6,7},{7,6},{8,9},{9,8},{10,11... | collective-permute-start | bytes 1572872 | tf_op jit(solution)/shard_map/density/ppermute | solution.py:26
  171.2 4.9 %copy-start.9 = (s32[2]{0:T(128)}, s32[2]{0:T(128)S(1)}, u32[]{:S(2)}) copy-start(s32[2]{0:T(128)S(1)} %pad_add_fusion.place) | copy-start | bytes 28
  178.4 53.0 %all-to-all-start.4 = ((bf16[16,64,1024]{2,1,0:T(8,128)(2,1)}), bf16[16,64,1024]{2,1,0:T(8,128)(2,1)S(1)}, u32[]{:S(2)}, u32[]{:S(2)}) async-start(bf16[16,64,1024]{2,1,0:T(8,128)(2,1)} %copy-done.5), calls=%async_computation.4 | async-start | bytes 4194304 | tf_op jit(solution)/shard_map/transpose_out/all_to_all | solution.py:30
  182.2 19.2 %collective-permute-start.21 = (bf16[512,512]{1,0:T(8,128)(2,1)}, bf16[512,512]{1,0:T(8,128)(2,1)S(1)}, u32[]{:S(2)}, u32[]{:S(2)}) collective-permute-start(bf16[512,512]{1,0:T(8,128)(2,1)} %bitcast.61), channel_id=1, source_target_pairs={{0,6},{2,4},{4,2},{6,0},{1,7},{3,5},{5,3},{7,1},{8,14},{10,12},{12... | collective-permute-start | bytes 1572872 | tf_op jit(solution)/shard_map/density/ppermute | solution.py:184
  183.4 18.0 %collective-permute-start.20 = (bf16[512,512]{1,0:T(8,128)(2,1)}, bf16[512,512]{1,0:T(8,128)(2,1)}, u32[]{:S(2)}, u32[]{:S(2)}) collective-permute-start(bf16[512,512]{1,0:T(8,128)(2,1)} %bitcast.62), channel_id=1, source_target_pairs={{0,4},{4,0},{1,5},{5,1},{2,6},{6,2},{3,7},{7,3},{8,12},{12,8},{9,1... | collective-permute-start | bytes 1572872 | tf_op jit(solution)/shard_map/density/ppermute | solution.py:26
  183.4 24.8 %collective-permute-start.19 = (bf16[512,512]{1,0:T(8,128)(2,1)S(1)}, bf16[512,512]{1,0:T(8,128)(2,1)}, u32[]{:S(2)}, u32[]{:S(2)}) collective-permute-start(bf16[512,512]{1,0:T(8,128)(2,1)S(1)} %get-tuple-element.94), channel_id=1, source_target_pairs={{0,4},{4,0},{1,5},{5,1},{2,6},{6,2},{3,7},{7,3},{8,12},{12,8},{9,1... | collective-permute-start | bytes 1572872 | tf_op jit(solution)/shard_map/density/ppermute | solution.py:26
  201.4 11.1 %copy-start.20 = (bf16[512,512]{1,0:T(8,128)(2,1)}, bf16[512,512]{1,0:T(8,128)(2,1)S(1)}, u32[]{:S(2)}) copy-start(bf16[512,512]{1,0:T(8,128)(2,1)S(1)} %collective-permute-done.21.refs_8_) | copy-start | bytes 1572868
  208.2 2.9 %collective-permute-start.22 = (bf16[512,512]{1,0:T(8,128)(2,1)}, bf16[512,512]{1,0:T(8,128)(2,1)S(1)}, u32[]{:S(2)}, u32[]{:S(2)}) collective-permute-start(bf16[512,512]{1,0:T(8,128)(2,1)} %collective-permute-done.19.refs_0_), channel_id=1, source_target_pairs={{0,1},{1,0},{2,3},{3,2},{4,5},{5,4},{6,7},{7,6},{8,9},{9,8},{10,11... | collective-permute-start | bytes 1572872 | tf_op jit(solution)/shard_map/density/ppermute | solution.py:26
  209.3 3.2 %collective-permute-start.23 = (bf16[512,512]{1,0:T(8,128)(2,1)}, bf16[512,512]{1,0:T(8,128)(2,1)S(1)}, u32[]{:S(2)}, u32[]{:S(2)}) collective-permute-start(bf16[512,512]{1,0:T(8,128)(2,1)} %collective-permute-done.20.refs_4_), channel_id=1, source_target_pairs={{0,1},{1,0},{2,3},{3,2},{4,5},{5,4},{6,7},{7,6},{8,9},{9,8},{10,11... | collective-permute-start | bytes 1572872 | tf_op jit(solution)/shard_map/density/ppermute | solution.py:26
  209.3 3.2 %collective-permute-start.24 = (bf16[512,512]{1,0:T(8,128)(2,1)S(1)}, bf16[512,512]{1,0:T(8,128)(2,1)}, u32[]{:S(2)}, u32[]{:S(2)}) collective-permute-start(bf16[512,512]{1,0:T(8,128)(2,1)S(1)} %collective-permute-done.21.refs_8_), channel_id=1, source_target_pairs={{0,1},{1,0},{2,3},{3,2},{4,5},{5,4},{6,7},{7,6},{8,9},{9,8},{10,11... | collective-permute-start | bytes 1572872 | tf_op jit(solution)/shard_map/density/ppermute | solution.py:26
  211.0 1.5 copy-start.21
  231.4 1.3 copy-start.11
  232.7 5.2 %copy-start.1 = (f32[256,256]{1,0:T(8,128)S(1)}, f32[256,256]{1,0:T(8,128)}, u32[]{:S(2)}) copy-start(f32[256,256]{1,0:T(8,128)} %param.14) | copy-start | bytes 786436
  (9 other events, 8.3 us)
Sparse Core Ops, SparseCore 0:
  48.7 77.6 all-gather.2

commit v4 on v3

v4 whole, which is shorter than its diff:
```python
import functools
import math

import jax
import jax.numpy as jnp
from jax import lax
from jax.experimental import pallas as pl
from jax.experimental.pallas import tpu as pltpu
from jax.sharding import Mesh
from jax.sharding import PartitionSpec as P

OCC = 2048
R = 4096
ZY = ("z", "y")
ZYC = ("z", "y", "c")
TILE = 256
STEPS = 8


def dot(left, right, dims, **kwargs):
    return lax.dot_general(
        left, right, (dims, ((), ())), preferred_element_type=jnp.float32, **kwargs
    )


def swap(values, axis):
    return lax.ppermute(values, axis, [(0, 1), (1, 0)])


def exchange(values, axes):
    return lax.all_to_all(values, axes, 0, 0, tiled=True)


def tie(*values):
    return lax.optimization_barrier(values)


def pick(first, second, flag):
    return jnp.where(flag == 0, first, second)


def body(
    eigvecs, panel_one, panel_two, factor_one, factor_two, occupations, occupied_count, row_offset
):
    bf16 = jnp.bfloat16
    xl, xh, c = (lax.axis_index(name) for name in ("xl", "xh", "c"))
    zy = lax.axis_index(ZY)
    n_orbs, n_basis = eigvecs.shape
    n_vec = panel_one.shape[0]
    chunk = n_basis // 16
    half = chunk // 2
    pw = factor_one.shape[0]
    rows = R // 4

    n_all = 2 * n_vec
    side_xl = xl.astype(jnp.int32).reshape(1)
    place = jnp.stack([xh * 2 + c, c]).astype(jnp.int32)

    with jax.named_scope("pack"):
        occ_high = occupations.astype(bf16)
        rest = occupations - occ_high.astype(jnp.float32)
        occ_mid = rest.astype(bf16)
        occ_low = (rest - occ_mid.astype(jnp.float32)).astype(bf16)
        extra = jnp.zeros((16, half), bf16)
        extra = extra.at[:3, :n_orbs].set(jnp.stack([occ_high, occ_mid, occ_low]))
        give_p, keep_p = pack(side_xl, eigvecs, panel_one, panel_two, extra, chunk)

    with jax.named_scope("transpose_give"):
        got = exchange(give_p, ZY)

    with jax.named_scope("window_exchange"):
        start = row_offset[0] - (xh * 2 + c) * n_basis
        held, _ = tie(eigvecs, give_p)

        def cut(part):
            first = start + part * rows
            at = jnp.clip(first, 0, n_basis - rows)
            pieces = (held, panel_one, panel_two)
            pieces = [lax.dynamic_slice_in_dim(v, at, rows, 1).astype(bf16) for v in pieces]
            piece = jnp.concatenate(pieces)
            zeros = jnp.zeros_like(piece)
            piece = jnp.concatenate([zeros, piece, zeros], axis=1)
            shift = jnp.clip(first - at, -rows, rows)
            return lax.dynamic_slice_in_dim(piece, rows + shift, rows, 1)

        both_flip = [(i, 3 - i) for i in range(4)]
        from_xh = swap(cut((1 - xh) * 2 + c), "xh")
        from_both = lax.ppermute(cut((1 - xh) * 2 + 1 - c), ("xh", "c"), both_flip)
        from_c = swap(cut(xh * 2 + 1 - c), "c")
        mine = (cut(xh * 2 + c) + from_c) + (from_xh + from_both)
        mine_x = swap(mine, "xl")

        def by_xl(own, other, axis):
            return jnp.stack([pick(own, other, xl), pick(other, own, xl)], axis=axis)

        win_vecs = by_xl(mine[n_orbs:], mine_x[n_orbs:], 0).reshape(2 * n_all, rows)
        window = jnp.concatenate([mine[:n_orbs], mine_x[:n_orbs], win_vecs], axis=0)
        got, keep_p, window = tie(got, keep_p, window)
        window = lax.all_gather(window, ZY, axis=0)

    with jax.named_scope("transpose_keep"):
        keep = exchange(keep_p, ZY)
        give = got[:, :n_orbs].reshape(16 * n_orbs, half)
        vec_own = got[:, n_orbs : n_orbs + 2 * n_all]
        occ_own = got[:, n_orbs + 2 * n_all :, :128]
        vec_oth = swap(vec_own, "xl")
        occ_oth = swap(occ_own, "xl")
        quarter = 8 * n_orbs
        count, factor_one, factor_two, give, occ_oth = tie(
            occupied_count, factor_one, factor_two, give, occ_oth
        )
        give_a, give_b = give[:quarter], give[quarter:]
        same_a = swap(give_a, "xl")
        diff_a = lax.ppermute(give_a, ("xl", "xh"), both_flip)

        def weight_of(occ, side):
            occ = occ[:, :3, :n_orbs].astype(jnp.float32)
            occ = (occ[:, 0] + occ[:, 1]) + occ[:, 2]
            index = (jnp.arange(16, dtype=jnp.int32)[:, None] * 2 + side) * n_orbs
            index = index + jnp.arange(n_orbs, dtype=jnp.int32)[None]
            occ = jnp.where(index < count[0], occ / math.sqrt(OCC), jnp.float32(0.0))
            return occ.reshape(16 * n_orbs, 1)

        weight_own, weight_oth = weight_of(occ_own, xl), weight_of(occ_oth, 1 - xl)
        vecs = by_xl(vec_own.reshape(16, 2, n_all, half), vec_oth.reshape(16, 2, n_all, half), 2)
        vecs = vecs.transpose(1, 0, 2, 3, 4)
        vec_two = vecs.reshape(2, 32, 2, n_vec, half)[:, :, 1].reshape(2, pw, half)
        vecs = vecs.reshape(2, 2 * pw, half)
        vec_keep = lax.dynamic_index_in_dim(vecs, xl, 0, keepdims=False)
        vec_give = lax.dynamic_index_in_dim(vecs, 1 - xl, 0, keepdims=False)

        high = lax.Precision.HIGHEST
        at_v = jnp.arange(pw, dtype=jnp.int32)[:, None]
        at_q = jnp.arange(2 * pw, dtype=jnp.int32)[None]
        factor = jnp.zeros((2 * pw, 2 * pw), jnp.float32)
        for panel, one in enumerate((factor_one, factor_two)):
            spot = (at_v // n_vec) * 2 * n_vec + panel * n_vec + at_v % n_vec
            place_of = (at_q == spot).astype(jnp.float32)
            wide = dot(one, place_of, ((0,), (0,)), precision=high)
            factor = factor + dot(place_of, wide, ((0,), (0,)), precision=high)
        wide_high = wide.astype(bf16)
        wide_low = (wide - wide_high.astype(jnp.float32)).astype(bf16)
        vec_keep_c = swap(vec_keep, "c")
        keep, same_a, diff_a, vecs, vec_two, vec_keep = tie(
            keep, same_a, diff_a, vecs, vec_two, vec_keep
        )
        keep, vec_keep_c = tie(keep, vec_keep_c)
        keep, weight_own, weight_oth, factor, wide_high, wide_low = tie(
            keep, weight_own, weight_oth, factor, wide_high, wide_low
        )
        keep = keep.reshape(16 * n_orbs, half)

    with jax.named_scope("project"):
        cross = swap(keep, "xh")
        parts, parts_c = project(side_xl, place, give, keep, vecs, vec_two)
        parts = parts.astype(jnp.float32) + swap(parts_c, "c").astype(jnp.float32)
        summed = exchange(parts.astype(bf16), ZY)
        summed, cross = tie(summed, cross)
        summed = summed.astype(jnp.float32).sum(0)
        summed = summed + swap(summed, "xh")
        summed, give_b = tie(summed, give_b)

    with jax.named_scope("coefficients"):
        share = dot(summed[:, : 2 * pw], factor, ((1,), (0,)), precision=high)
        share = jnp.concatenate([share, summed[:, 2 * pw :]], axis=1).astype(bf16)
        every = exchange(jnp.broadcast_to(share[None], (16,) + share.shape), ZY)
        same_b = swap(give_b, "xl")
        diff_b = lax.ppermute(give_b, ("xl", "xh"), both_flip)
        keep_c, cross_c, same_a_c, diff_a_c = (swap(v, "c") for v in (keep, cross, same_a, diff_a))
        every, keep_c, cross_c, same_a_c, diff_a_c, same_b, diff_b = tie(
            every, keep_c, cross_c, same_a_c, diff_a_c, same_b, diff_b
        )
        every, vec_give = tie(every, vec_give)
        every_c = swap(every, "c")
        coeffs_x = swap(every[:, :, : 2 * pw].reshape(quarter, 2 * pw), "xl")
        coeffs, mixed, update = expand(place, every, every_c, wide_high, wide_low, vecs, n_orbs)

    with jax.named_scope("transpose_out"):
        back = exchange(update, ZY)

    with jax.named_scope("density"):
        vec_keep_x = lax.ppermute(vec_give, ("xl", "xh"), both_flip)
        vec_keep_xc = swap(vec_keep_x, "c")
        same_b_c, diff_b_c = swap(same_b, "c"), swap(diff_b, "c")
        coeffs_y = swap(coeffs_x, "c")
        density = density_of(
            place,
            window,
            coeffs,
            [coeffs_x, coeffs_y],
            mixed,
            [weight_own, weight_oth],
            [vec_keep, vec_keep_c, vec_keep_x, vec_keep_xc],
            [
                ([keep], [same_a, same_b]),
                ([keep_c], [same_a_c, same_b_c]),
                ([cross], [diff_a, diff_b]),
                ([cross_c], [diff_a_c, diff_b_c]),
            ],
        )

    with jax.named_scope("subtract"):
        back, density = tie(back, density)
        out = subtract(eigvecs, back)
    return (out, density)


def cost(flops, bytes_accessed):
    return pl.CostEstimate(flops=flops, bytes_accessed=bytes_accessed, transcendentals=0)


def pack_kernel(side, orbs, panel_one, panel_two, extra, give, keep, *scratch):
    orbs_v, one_v, two_v, give_v, keep_v, sems = scratch
    parts, n_orbs, half = keep.shape
    n_vec = panel_one.shape[0]
    step = parts // STEPS
    loads = [
        pltpu.make_async_copy(panel_one, one_v, sems.at[0]),
        pltpu.make_async_copy(panel_two, two_v, sems.at[1]),
    ]
    for i in range(STEPS):
        at = pl.ds(i * step * 2 * half, step * 2 * half)
        loads.append(pltpu.make_async_copy(orbs.at[:, at], orbs_v.at[:, at], sems.at[2 + i]))
    for load in loads:
        load.start()
    for load in loads[:2]:
        load.wait()
    stores = []
    for i in range(STEPS):
        loads[2 + i].wait()
        for part in range(i * step, (i + 1) * step):
            for out, which in ((keep_v, side[0]), (give_v, 1 - side[0])):
                at = pl.multiple_of((2 * part + which) * half, half)
                out[part, :n_orbs, :] = orbs_v[:, pl.ds(at, half)].astype(jnp.bfloat16)
            for which in range(2):
                at = pl.ds((2 * part + which) * half, half)
                rows = pl.ds(n_orbs + which * 2 * n_vec, 2 * n_vec)
                both = jnp.concatenate([one_v[:, at], two_v[:, at]], axis=0)
                give_v[part, rows, :] = both
            give_v[part, pl.ds(n_orbs + 4 * n_vec, 16), :] = extra[...]
        at = pl.ds(i * step, step)
        for j, (source, target) in enumerate(((give_v, give), (keep_v, keep))):
            sem = sems.at[2 + (1 + j) * STEPS + i]
            stores.append(pltpu.make_async_copy(source.at[at], target.at[at], sem))
            stores[-1].start()
    for store in stores:
        store.wait()


def pack(side, orbs, panel_one, panel_two, extra, chunk):
    n_orbs, n_basis = orbs.shape
    parts, half = n_basis // chunk, chunk // 2
    n_give = n_orbs + 4 * panel_one.shape[0] + 16
    anywhere = pl.BlockSpec(memory_space=pl.ANY)
    give = (parts, n_give, half)
    keep = (parts, n_orbs, half)
    return pl.pallas_call(
        pack_kernel,
        out_shape=(
            jax.ShapeDtypeStruct(give, jnp.bfloat16),
            jax.ShapeDtypeStruct(keep, jnp.bfloat16),
        ),
        grid_spec=pltpu.PrefetchScalarGridSpec(
            num_scalar_prefetch=1,
            grid=(1,),
            in_specs=[anywhere, anywhere, anywhere]
            + [pl.BlockSpec(extra.shape, lambda i, _: (0, 0))],
            out_specs=(anywhere, anywhere),
            scratch_shapes=[
                pltpu.VMEM(orbs.shape, jnp.float32),
                pltpu.VMEM(panel_one.shape, jnp.bfloat16),
                pltpu.VMEM(panel_two.shape, jnp.bfloat16),
                pltpu.VMEM(give, jnp.bfloat16),
                pltpu.VMEM(keep, jnp.bfloat16),
                pltpu.SemaphoreType.DMA((2 + 3 * STEPS,)),
            ],
        ),
        compiler_params=pltpu.CompilerParams(vmem_limit_bytes=62 * 2**20),
        cost_estimate=cost(0, 7 * n_orbs * n_basis),
        name="pack",
    )(side, orbs, panel_one, panel_two, extra)


def subtract_kernel(orbs, update, out, orbs_v, update_v, sems):
    parts, _, chunk = update.shape
    step = parts // STEPS
    loads = []
    for i in range(STEPS):
        at, cols = pl.ds(i * step, step), pl.ds(i * step * chunk, step * chunk)
        loads.append(
            (
                pltpu.make_async_copy(update.at[at], update_v.at[at], sems.at[i]),
                pltpu.make_async_copy(orbs.at[:, cols], orbs_v.at[:, cols], sems.at[STEPS + i]),
            )
        )
        for load in loads[-1]:
            load.start()
    stores = []
    for i in range(STEPS):
        for load in loads[i]:
            load.wait()
        for part in range(i * step, (i + 1) * step):
            at = pl.ds(part * chunk, chunk)
            orbs_v[:, at] = orbs_v[:, at] - update_v[part].astype(jnp.float32)
        cols = pl.ds(i * step * chunk, step * chunk)
        sem = sems.at[2 * STEPS + i]
        stores.append(pltpu.make_async_copy(orbs_v.at[:, cols], out.at[:, cols], sem))
        stores[-1].start()
    for store in stores:
        store.wait()


def subtract(orbs, update):
    n_orbs, n_basis = orbs.shape
    anywhere = pl.BlockSpec(memory_space=pl.ANY)
    return pl.pallas_call(
        subtract_kernel,
        out_shape=jax.ShapeDtypeStruct(orbs.shape, jnp.float32),
        in_specs=[anywhere, anywhere],
        out_specs=anywhere,
        scratch_shapes=[
            pltpu.VMEM(orbs.shape, jnp.float32),
            pltpu.VMEM(update.shape, jnp.bfloat16),
            pltpu.SemaphoreType.DMA((3 * STEPS,)),
        ],
        compiler_params=pltpu.CompilerParams(vmem_limit_bytes=62 * 2**20),
        cost_estimate=cost(n_orbs * n_basis, 10 * n_orbs * n_basis),
        name="subtract_update",
    )(orbs, update)


def project_kernel(side, place, give, keep, vecs, vec_two, mine, theirs):
    blocks, n_own, lanes = mine.shape
    width = vecs.shape[1]
    proj = dot(give[...], vecs[1 - side[0]], ((1,), (1,)))
    proj = proj + dot(keep[...], vecs[side[0]], ((1,), (1,)))
    cross = dot(vecs[0], vec_two[0], ((1,), (1,)))
    cross = cross + dot(vecs[1], vec_two[1], ((1,), (1,)))

    def store(out):
        out[:, :, :width] = proj.astype(jnp.bfloat16).reshape(blocks, n_own, width)
        out[:, :, width:] = cross.astype(jnp.bfloat16).reshape(blocks, n_own, lanes - width)

    pl.when(pl.program_id(0) == place[1])(lambda: store(mine))
    pl.when(pl.program_id(0) != place[1])(lambda: store(theirs))


def project(side, place, give, keep, vecs, vec_two):
    n_orbs, half = give.shape
    width, n_two = vecs.shape[1], vec_two.shape[1]
    tile, lanes = n_orbs // 2, n_two // 2
    shape = (16, n_orbs // 32, width + lanes)
    return pl.pallas_call(
        project_kernel,
        out_shape=(jax.ShapeDtypeStruct(shape, jnp.bfloat16),) * 2,
        grid_spec=pltpu.PrefetchScalarGridSpec(
            num_scalar_prefetch=2,
            grid=(2,),
            in_specs=[
                pl.BlockSpec((tile, half), lambda i, *_: (i, 0)),
                pl.BlockSpec((tile, half), lambda i, *_: (i, 0)),
                pl.BlockSpec(vecs.shape, lambda i, *_: (0, 0, 0)),
                pl.BlockSpec((2, lanes, half), lambda i, *_: (0, i, 0)),
            ],
            out_specs=(pl.BlockSpec(shape, lambda i, *_: (0, 0, 0)),) * 2,
        ),
        compiler_params=pltpu.CompilerParams(vmem_limit_bytes=62 * 2**20),
        cost_estimate=cost(1, 1),
        name="project",
    )(side, place, give, keep, vecs, vec_two)


def expand_kernel(place, mine, theirs, wide_high, wide_low, vecs, coeffs, mixed, update):
    width, half = vecs.shape[1:]
    blocks, n_own, lanes = mine.shape
    lanes = lanes - width

    @pl.when(pl.program_id(0) == 0)
    def _():
        total = None
        for core, every in ((place[1], mine), (1 - place[1], theirs)):
            cross = every[:, :, width:].reshape(width, lanes)
            for wide in (wide_high, wide_low):
                term = dot(cross, wide[core], ((1,), (0,)))
                total = term if total is None else total + term
        row = lax.broadcasted_iota(jnp.int32, total.shape, 0)
        first = jnp.bitwise_and(lax.shift_right_logical(row, 3), 1) == 0
        mixed[...] = jnp.where(first, total, 0.0).astype(jnp.bfloat16)

    def fill(every):
        base = every[:, :, :width].reshape(blocks * n_own, width)
        fixed = base.astype(jnp.float32) - dot(base, mixed[...], ((1,), (0,)))
        fixed = fixed.astype(jnp.bfloat16)
        coeffs[...] = fixed
        for part in range(2):
            new = dot(fixed, vecs[part], ((1,), (0,))).astype(jnp.bfloat16)
            shape = update.shape[:2] + (half,)
            update[:, :, part * half : (part + 1) * half] = new.reshape(shape)

    pl.when(pl.program_id(0) == 0)(lambda: fill(mine))
    pl.when(pl.program_id(0) == 1)(lambda: fill(theirs))


def expand(place, mine, theirs, wide_high, wide_low, vecs, n_orbs):
    _, width, half = vecs.shape
    total = 2 * mine.shape[0] * mine.shape[1]
    wide_high, wide_low = (v.reshape(2, v.shape[0] // 2, width) for v in (wide_high, wide_low))

    def whole(value):
        return pl.BlockSpec(value.shape, lambda i, _: (0, 0, 0), pipeline_mode=pl.Buffered(1))

    def core(i, place):
        return i + place[1] - 2 * i * place[1]

    return pl.pallas_call(
        expand_kernel,
        out_shape=(
            jax.ShapeDtypeStruct((total, width), jnp.bfloat16),
            jax.ShapeDtypeStruct((width, width), jnp.bfloat16),
            jax.ShapeDtypeStruct((16, n_orbs, 2 * half), jnp.bfloat16),
        ),
        grid_spec=pltpu.PrefetchScalarGridSpec(
            num_scalar_prefetch=1,
            grid=(2,),
            in_specs=[whole(value) for value in (mine, theirs, wide_high, wide_low, vecs)],
            out_specs=(
                pl.BlockSpec((total // 2, width), lambda i, place: (core(i, place), 0)),
                pl.BlockSpec((width, width), lambda i, _: (0, 0)),
                pl.BlockSpec((8, n_orbs, 2 * half), lambda i, place: (core(i, place), 0, 0)),
            ),
        ),
        compiler_params=pltpu.CompilerParams(vmem_limit_bytes=62 * 2**20),
        cost_estimate=cost(2 * total * width * (width + 2 * half), 6 * 2**20),
        name="expand",
    )(place, mine, theirs, wide_high, wide_low, vecs)


def density_kernel(counts, place, win_orbs, win_vecs, *refs):
    coeffs, coeffs_x, coeffs_y, mixed, weight_own, weight_oth = refs[:6]
    vecs, refs = refs[6:10], refs[10:]
    n_pieces = sum(counts)
    pieces, refs = refs[:n_pieces], refs[n_pieces:]
    out, orbs_v, vecs_v, coeffs_v, raw_v, mixed_v, weight_v, sems = refs
    n_half, width = coeffs.shape
    n_orbs, tile = n_half // 16, win_orbs.shape[2]

    @pl.when(pl.program_id(0) == 0)
    def _():
        copies = []

        def fetch(source, target):
            copy = pltpu.make_async_copy(source, target, sems.at[len(copies)])
            copy.start()
            copies.append(copy)
            return copy

        factors = [fetch(coeffs, coeffs_v.at[0]), fetch(mixed, mixed_v)]
        factors += [fetch(coeffs_x, raw_v.at[0]), fetch(coeffs_y, raw_v.at[1])]
        factors += [fetch(weight_own, weight_v.at[0]), fetch(weight_oth, weight_v.at[1])]
        sides, used = [], 0
        for side in range(4):
            needed = [fetch(vecs[side], vecs_v.at[side])]
            for part in range(2):
                n = counts[2 * side + part]
                for i in range(n):
                    at = pl.ds(i * (n_half // n), n_half // n)
                    needed.append(fetch(pieces[used + i], orbs_v.at[2 * side + part, at]))
                used += n
            sides.append(needed)

        for copy in factors:
            copy.wait()
        for i, core in enumerate((place[1], 1 - place[1])):
            raw = raw_v[i]
            fixed = raw.astype(jnp.float32) - dot(raw, mixed_v[...], ((1,), (0,)))
            to = pl.multiple_of(core * (n_half // 2), n_half // 2)
            coeffs_v[1, pl.ds(to, n_half // 2), :] = fixed.astype(jnp.bfloat16)
        for side in range(4):
            for copy in sides[side]:
                copy.wait()
            for part in range(2):
                slot = 2 * side + part
                update = dot(coeffs_v[part], vecs_v[side], ((1,), (0,)))
                new = (orbs_v[slot].astype(jnp.float32) - update) * weight_v[part]
                orbs_v[slot] = new.astype(jnp.bfloat16)

    vec_tile = win_vecs[...].reshape(width, tile)
    turned = []
    for part in range(2):
        update = dot(coeffs_v[part], vec_tile, ((1,), (0,)))
        value = win_orbs[:, part * n_orbs : (part + 1) * n_orbs, :].reshape(n_half, tile)
        turned.append((value.astype(jnp.float32) - update).astype(jnp.bfloat16).T)
    for block in range(4):
        side = jnp.bitwise_xor(place[0], block)
        total = dot(turned[0], orbs_v[2 * side], ((1,), (0,)))
        out[:, block, :] = total + dot(turned[1], orbs_v[2 * side + 1], ((1,), (0,)))


def density_of(place, window, coeffs, others, mixed, weights, vecs, orbs):
    rows = window.shape[2]
    n_half, width = coeffs.shape
    half = vecs[0].shape[1]
    n_vec, n_orbs = width // 16, n_half // 16
    counts = [len(part) for side in orbs for part in side]
    pieces = [piece for side in orbs for part in side for piece in part]
    operands = [coeffs, *others, mixed, *weights, *vecs, *pieces]
    specs = [
        pl.BlockSpec((16, 2 * n_orbs, TILE), lambda i, _: (0, 0, i)),
        pl.BlockSpec((16, n_vec, TILE), lambda i, _: (0, 2 * n_orbs // n_vec, i)),
    ]
    return pl.pallas_call(
        functools.partial(density_kernel, counts),
        out_shape=jax.ShapeDtypeStruct((rows, 4, half), jnp.float32),
        grid_spec=pltpu.PrefetchScalarGridSpec(
            num_scalar_prefetch=1,
            grid=(rows // TILE,),
            in_specs=specs + [pl.BlockSpec(memory_space=pl.ANY)] * len(operands),
            out_specs=pl.BlockSpec((TILE, 4, half), lambda i, _: (i, 0, 0)),
            scratch_shapes=[
                pltpu.VMEM((8, n_half, half), jnp.bfloat16),
                pltpu.VMEM((4, width, half), jnp.bfloat16),
                pltpu.VMEM((2, n_half, width), jnp.bfloat16),
                pltpu.VMEM((2, n_half // 2, width), jnp.bfloat16),
                pltpu.VMEM((width, width), jnp.bfloat16),
                pltpu.VMEM((2, n_half, 1), jnp.float32),
                pltpu.SemaphoreType.DMA((len(operands),)),
            ],
        ),
        compiler_params=pltpu.CompilerParams(vmem_limit_bytes=62 * 2**20),
        cost_estimate=cost(16 * rows * n_half * half + 16 * n_half * width * half, 28 * 2**20),
        name="density",
    )(place, window, window, *operands)


def solution(mesh):
    mesh = Mesh(mesh.devices.reshape(4, 4, 2, 2, 2), ("z", "y", "xl", "xh", "c"))
    slab, grid = ("z", "y", "xl"), ("xh", "c")
    both = P(slab, grid)
    in_specs = (both, both, both, P(), P(), P(slab), P(), P())
    out_specs = (both, P(grid, None, slab))
    return jax.shard_map(body, mesh=mesh, in_specs=in_specs, out_specs=out_specs, check_vma=False)
```

time: 246 us -> 212 us (0.86)
  waiting for transfers between devices: 82.8 us -> 58.7 us
  starting transfers between devices: 54.8 us -> 63.2 us
  local copies, waits for them, and re-layouts: 22.1 us -> 15 us
  Pallas kernels: 51.4 us -> 44.5 us
    ppermute x21, waiting for transfers between devices: 60.8 us -> 31.8 us  [swap(): return lax.ppermute(values, axis, [(0, 1), (1, 0)])]
    ppermute x1, waiting for transfers between devices: 0.01 us -> 12.5 us  [body(): diff_b = lax.ppermute(give_b, ('xl', 'xh'), both_flip)]
    ppermute x1, waiting for transfers between devices: 12.1 us -> 0.01 us  [body(): vec_keep_x = lax.ppermute(vec_give, ('xl', 'xh'), both_flip)]
    ppermute x21, starting transfers between devices: 10.7 us -> 22.1 us  [swap(): return lax.ppermute(values, axis, [(0, 1), (1, 0)])]
    pallas_call x4 -> x3, Pallas kernels: 41.3 us -> 33.3 us  [the longest x1 23.3 us: density_of(): pl.pallas_call(functools.partial(density_kernel, counts), out_shape=jax.S...]
    unnamed x52 -> x42, local copies, waits for them, and re-layouts: 10.5 us -> 4.85 us
    all_to_all x5, waiting for transfers between devices: 5.23 us -> 9.89 us  [exchange(): return lax.all_to_all(values, axes, 0, 0, tiled=True)]
    all_to_all x5, starting transfers between devices: 35.4 us -> 31 us  [exchange(): return lax.all_to_all(values, axes, 0, 0, tiled=True)]
where the time goes in v4:
time: 212 us
  starting transfers between devices  63.2 us (30%)
  waiting for transfers between devices  58.7 us (28%)
  Pallas kernels  44.5 us (21%)
  between operations  15.8 us (7%)
  local copies, waits for them, and re-layouts  15 us (7%)
  other arithmetic  9.36 us (4%)
  matrix products  4.91 us (2%)
    ppermute x21, waiting for transfers between devices, swap(): return lax.ppermute(values, axis, [(0, 1), (1, 0)])  31.8 us
    all_to_all x5, starting transfers between devices, exchange(): return lax.all_to_all(values, axes, 0, 0, tiled=True)  31 us
    pallas_call x1, Pallas kernels, density_of(): pl.pallas_call(functools.partial(density_kernel, counts), out_shape=jax.S...  23.3 us
    ppermute x21, starting transfers between devices, swap(): return lax.ppermute(values, axis, [(0, 1), (1, 0)])  22.1 us
    ppermute x1, waiting for transfers between devices, body(): diff_b = lax.ppermute(give_b, ('xl', 'xh'), both_flip)  12.5 us
    all_to_all x5, waiting for transfers between devices, exchange(): return lax.all_to_all(values, axes, 0, 0, tiled=True)  9.89 us
    pallas_call x1, Pallas kernels, expand(): pl.pallas_call(expand_kernel, out_shape=(jax.ShapeDtypeStruct((total, wid...  6.44 us
    pallas_call x1, Pallas kernels, project(): pl.pallas_call(project_kernel, out_shape=(jax.ShapeDtypeStruct(shape, jnp...  5.54 us
  transfers between devices with their start and end apart: 31, of which 16 were waited for; matrix products, arithmetic and copies ran while one was open for 11% of the time, Pallas kernels for 17%

profile of v4, /device:TPU:1, one launch (start us, length us, event | category | flops | bytes accessed | tf_op | source)
XLA Modules:
  0.0 211.5 jit_solution(10348311480066644426)
XLA Ops:
  8.5 4.4 %pack.1 = (bf16[16,112,512]{2,1,0:T(8,128)(2,1)}, bf16[16,64,512]{2,1,0:T(8,128)(2,1)}) custom-call(s32[1]{0:T(128)} %bitcast.2.side, f32[64,16384]{1,0:T(8,128)} %orbs.3, bf16[8,16384]{1,0:T(8,128)(2,1)} %panel_one.1, bf16[8,16384]{1,0:T(8,128)(2,1)} %panel_two.1, bf16[16,512]{1,0:T(8,128)(2,1)} %fusion.34.extra), custom_call_target="tpu_custom_call" | custom-call | bytes 7340032 | tf_op jit(solution)/shard_map/pack/pack/pallas_call | solution.py:257
  13.0 8.6 %all-to-all-start = ((bf16[16,112,512]{2,1,0:T(8,128)(2,1)}), bf16[16,112,512]{2,1,0:T(8,128)(2,1)S(1)}, u32[]{:S(2)}, u32[]{:S(2)}) async-start(bf16[16,112,512]{2,1,0:T(8,128)(2,1)} %get-tuple-element.59), calls=%async_computation | async-start | bytes 3670016 | tf_op jit(solution)/shard_map/transpose_give/all_to_all | solution.py:31
  22.3 1.6 constant_dynamic-slice_fusion
  23.9 1.5 dynamic-slice_convert_fusion
  25.5 1.1 fusion.10
  26.6 3.5 %collective-permute-start.2 = (bf16[80,1024]{1,0:T(8,128)(2,1)S(1)}, bf16[80,1024]{1,0:T(8,128)(2,1)S(1)}, u32[]{:S(2)}, u32[]{:S(2)}) collective-permute-start(bf16[80,1024]{1,0:T(8,128)(2,1)S(1)} %get-tuple-element.126), channel_id=1, source_target_pairs={{0,3},{1,2},{2,1},{3,0},{4,7},{5,6},{6,5},{7,4},{8,11},{9,10},{10,... | collective-permute-start | bytes 491528 | tf_op jit(solution)/shard_map/window_exchange/ppermute | solution.py:88
  30.6 4.5 %collective-permute-done.2 = bf16[80,1024]{1,0:T(8,128)(2,1)S(1)} collective-permute-done((bf16[80,1024]{1,0:T(8,128)(2,1)S(1)}, bf16[80,1024]{1,0:T(8,128)(2,1)S(1)}, u32[]{:S(2)}, u32[]{:S(2)}) %collective-permute-start.2) | collective-permute-done | bytes 163872 | tf_op jit(solution)/shard_map/window_exchange/ppermute | solution.py:88
  35.1 3.6 %collective-permute-done.1 = bf16[80,1024]{1,0:T(8,128)(2,1)S(1)} collective-permute-done((bf16[80,1024]{1,0:T(8,128)(2,1)S(1)}, bf16[80,1024]{1,0:T(8,128)(2,1)S(1)}, u32[]{:S(2)}, u32[]{:S(2)}) %collective-permute-start.1) | collective-permute-done | bytes 163872 | tf_op jit(solution)/shard_map/window_exchange/ppermute | solution.py:27
  39.1 1.1 collective-permute-start.3
  40.2 4.4 %collective-permute-done.3 = bf16[80,1024]{1,0:T(8,128)(2,1)S(1)} collective-permute-done((bf16[80,1024]{1,0:T(8,128)(2,1)S(1)}, bf16[80,1024]{1,0:T(8,128)(2,1)S(1)}, u32[]{:S(2)}, u32[]{:S(2)}) %collective-permute-start.3) | collective-permute-done | bytes 163872 | tf_op jit(solution)/shard_map/window_exchange/ppermute | solution.py:27
  45.4 2.9 %all-to-all-done = bf16[16,112,512]{2,1,0:T(8,128)(2,1)S(1)} async-done(((bf16[16,112,512]{2,1,0:T(8,128)(2,1)}), bf16[16,112,512]{2,1,0:T(8,128)(2,1)S(1)}, u32[]{:S(2)}, u32[]{:S(2)}) %all-to-all-start) | async-done | bytes 1835040 | tf_op jit(solution)/shard_map/transpose_give/all_to_all | solution.py:31
  50.9 0.9 slice.92
  51.8 4.5 %all-to-all-start.1 = ((bf16[16,64,512]{2,1,0:T(8,128)(2,1)}), bf16[16,64,512]{2,1,0:T(8,128)(2,1)}, u32[]{:S(2)}, u32[]{:S(2)}) async-start(bf16[16,64,512]{2,1,0:T(8,128)(2,1)} %get-tuple-element.64), calls=%async_computation.1 | async-start | bytes 2097152 | tf_op jit(solution)/shard_map/transpose_keep/all_to_all | solution.py:31
  56.3 1.3 collective-permute-start.4
  58.5 0.8 broadcast_select_fusion.3.refs_4_
  60.4 1.1 fusion.43
  61.5 2.5 %collective-permute-start.6 = (bf16[512,512]{1,0:T(8,128)(2,1)}, bf16[512,512]{1,0:T(8,128)(2,1)}, u32[]{:S(2)}, u32[]{:S(2)}) collective-permute-start(bf16[512,512]{1,0:T(8,128)(2,1)} %get-tuple-element.115), channel_id=1, source_target_pairs={{0,6},{2,4},{4,2},{6,0},{1,7},{3,5},{5,3},{7,1},{8,14},{10,12},{12... | collective-permute-start | bytes 1572872 | tf_op jit(solution)/shard_map/transpose_keep/ppermute | solution.py:114
  65.4 0.9 broadcast_select_fusion.2.refs_5_
  66.8 1.3 subtract_convert_fusion
  68.9 2.2 %collective-permute-done.7 = bf16[16,32,512]{2,1,0:T(8,128)(2,1)S(1)} collective-permute-done((bf16[16,32,512]{2,1,0:T(8,128)(2,1)}, bf16[16,32,512]{2,1,0:T(8,128)(2,1)S(1)}, u32[]{:S(2)}, u32[]{:S(2)}) %collective-permute-start.7) | collective-permute-done | bytes 524320 | tf_op jit(solution)/shard_map/transpose_keep/ppermute | solution.py:27
  71.4 1.0 dynamic-slice_bitcast_fusion
  72.4 4.4 %collective-permute-start.8 = (bf16[512,512]{1,0:T(8,128)(2,1)S(1)}, bf16[512,512]{1,0:T(8,128)(2,1)S(1)}, u32[]{:S(2)}, u32[]{:S(2)}) collective-permute-start(bf16[512,512]{1,0:T(8,128)(2,1)S(1)} %get-tuple-element.93.refs_6_), channel_id=1, source_target_pairs={{0,1},{1,0},{2,3},{3,2},{4,5},{5,4},{6,7},{7,6},{8,9},{9,8},{10,11... | collective-permute-start | bytes 1572872 | tf_op jit(solution)/shard_map/transpose_keep/ppermute | solution.py:27
  76.9 1.7 convolution_add_fusion
  79.4 3.0 %collective-permute-done.5.refs_11_ = bf16[512,512]{1,0:T(8,128)(2,1)} collective-permute-done((bf16[512,512]{1,0:T(8,128)(2,1)}, bf16[512,512]{1,0:T(8,128)(2,1)}, u32[]{:S(2)}, u32[]{:S(2)}) %collective-permute-start.5) | collective-permute-done | bytes 524320 | tf_op jit(solution)/shard_map/transpose_keep/ppermute | solution.py:27
  83.1 5.5 %project.1 = (bf16[16,32,640]{2,1,0:T(8,128)(2,1)}, bf16[16,32,640]{2,1,0:T(8,128)(2,1)}) custom-call(s32[1]{0:T(128)} %bitcast.2.side, s32[2]{0:T(128)} %pad_add_fusion.place, bf16[1024,512]{1,0:T(8,128)(2,1)} %bitcast.50, bf16[1024,512]{1,0:T(8,128)(2,1)} %bitcast.20.keep.refs_10_, bf16[2,512,512]{2,1,0:T(8,128)(2,1)} %bitcast.47, ...), custom_call_target="tpu_custom_call" | custom-call | flops 1 | bytes 1 | tf_op jit(solution)/shard_map/project/project/pallas_call | solution.py:353
  88.7 2.5 %collective-permute-start.9 = (bf16[16,32,640]{2,1,0:T(8,128)(2,1)}, bf16[16,32,640]{2,1,0:T(8,128)(2,1)S(1)}, u32[]{:S(2)}, u32[]{:S(2)}) collective-permute-start(bf16[16,32,640]{2,1,0:T(8,128)(2,1)} %get-tuple-element.75), channel_id=1, source_target_pairs={{0,1},{1,0},{2,3},{3,2},{4,5},{5,4},{6,7},{7,6},{8,9},{9,8},{10,11... | collective-permute-start | bytes 1966088 | tf_op jit(solution)/shard_map/project/ppermute | solution.py:27
  91.2 2.4 %collective-permute-start.10 = (bf16[1024,512]{1,0:T(8,128)(2,1)}, bf16[1024,512]{1,0:T(8,128)(2,1)S(1)}, u32[]{:S(2)}, u32[]{:S(2)}) collective-permute-start(bf16[1024,512]{1,0:T(8,128)(2,1)} %bitcast.20.keep.refs_10_), channel_id=1, source_target_pairs={{0,2},{2,0},{1,3},{3,1},{4,6},{6,4},{5,7},{7,5},{8,10},{10,8},{9,1... | collective-permute-start | bytes 3145736 | tf_op jit(solution)/shard_map/project/ppermute | solution.py:27
  93.6 2.2 %add_convert_fusion = bf16[16,32,640]{2,1,0:T(8,128)(2,1)} fusion(bf16[16,32,640]{2,1,0:T(8,128)(2,1)S(1)} %collective-permute-done.9, bf16[16,32,640]{2,1,0:T(8,128)(2,1)} %get-tuple-element.74), kind=kLoop, calls=%fused_computation.2 | loop fusion | flops 1310720 | bytes 1966080 | tf_op jit(solution)/shard_map/project/convert_element_type | solution.py:157
  95.8 6.5 %all-to-all-start.2 = ((bf16[16,32,640]{2,1,0:T(8,128)(2,1)}), bf16[16,32,640]{2,1,0:T(8,128)(2,1)S(1)}, u32[]{:S(2)}, u32[]{:S(2)}) async-start(bf16[16,32,640]{2,1,0:T(8,128)(2,1)} %add_convert_fusion), calls=%async_computation.2 | async-start | bytes 1310720 | tf_op jit(solution)/shard_map/project/all_to_all | solution.py:31
  102.3 15.3 %collective-permute-done.10.refs_16_ = bf16[1024,512]{1,0:T(8,128)(2,1)S(1)} collective-permute-done((bf16[1024,512]{1,0:T(8,128)(2,1)}, bf16[1024,512]{1,0:T(8,128)(2,1)S(1)}, u32[]{:S(2)}, u32[]{:S(2)}) %collective-permute-start.10) | collective-permute-done | bytes 1048608 | tf_op jit(solution)/shard_map/project/ppermute | solution.py:27
  117.7 3.2 %all-to-all-done.2 = bf16[16,32,640]{2,1,0:T(8,128)(2,1)S(1)} async-done(((bf16[16,32,640]{2,1,0:T(8,128)(2,1)}), bf16[16,32,640]{2,1,0:T(8,128)(2,1)S(1)}, u32[]{:S(2)}, u32[]{:S(2)}) %all-to-all-start.2) | async-done | bytes 655392 | tf_op jit(solution)/shard_map/project/all_to_all | solution.py:31
  120.9 2.8 %collective-permute-start.11 = (f32[32,640]{1,0:T(8,128)S(1)}, f32[32,640]{1,0:T(8,128)S(1)}, u32[]{:S(2)}, u32[]{:S(2)}) collective-permute-start(f32[32,640]{1,0:T(8,128)S(1)} %convert_reduce_fusion), channel_id=1, source_target_pairs={{0,2},{2,0},{1,3},{3,1},{4,6},{6,4},{5,7},{7,5},{8,10},{10,8},{9,1... | collective-permute-start | bytes 245768 | tf_op jit(solution)/shard_map/project/ppermute | solution.py:27
  123.7 1.0 collective-permute-start.12
  126.6 0.9 broadcast_in_dim.8
  127.5 4.3 %all-to-all-start.3 = ((bf16[16,32,640]{2,1,0:T(8,128)(2,1)}), bf16[16,32,640]{2,1,0:T(8,128)(2,1)S(1)}, u32[]{:S(2)}, u32[]{:S(2)}) async-start(bf16[16,32,640]{2,1,0:T(8,128)(2,1)} %broadcast_in_dim.8), calls=%async_computation.3 | async-start | bytes 1310720 | tf_op jit(solution)/shard_map/coefficients/all_to_all | solution.py:31
  131.8 2.3 %collective-permute-start.15 = (bf16[512,512]{1,0:T(8,128)(2,1)}, bf16[512,512]{1,0:T(8,128)(2,1)S(1)}, u32[]{:S(2)}, u32[]{:S(2)}) collective-permute-start(bf16[512,512]{1,0:T(8,128)(2,1)} %collective-permute-done.6.refs_17_), channel_id=1, source_target_pairs={{0,1},{1,0},{2,3},{3,2},{4,5},{5,4},{6,7},{7,6},{8,9},{9,8},{10,11... | collective-permute-start | bytes 1572872 | tf_op jit(solution)/shard_map/coefficients/ppermute | solution.py:27
  134.1 2.1 collective-permute-start.17
  136.3 12.5 %collective-permute-done.17.refs_18_ = bf16[512,512]{1,0:T(8,128)(2,1)S(1)} collective-permute-done((bf16[512,512]{1,0:T(8,128)(2,1)S(1)}, bf16[512,512]{1,0:T(8,128)(2,1)S(1)}, u32[]{:S(2)}, u32[]{:S(2)}) %collective-permute-start.17) | collective-permute-done | bytes 524320 | tf_op jit(solution)/shard_map/coefficients/ppermute | solution.py:168
  149.7 1.1 collective-permute-start.18
  150.9 2.0 collective-permute-start.21
  152.9 0.8 copy-done.12
  153.8 6.4 %expand.1 = (bf16[1024,512]{1,0:T(8,128)(2,1)}, bf16[512,512]{1,0:T(8,128)(2,1)}, bf16[16,64,1024]{2,1,0:T(8,128)(2,1)}) custom-call(s32[2]{0:T(128)} %pad_add_fusion.place, bf16[16,32,640]{2,1,0:T(8,128)(2,1)} %copy-done.5, bf16[16,32,640]{2,1,0:T(8,128)(2,1)} %copy-done.12, bf16[2,128,512]{2,1,0:T(8,128)(2,1)} %bitcast.56, bf16[2,128,512]{2,1,0:T(8,128)(2,1)} %bitcast.55, ...), custom_call_target="tpu_custom_call" | custom-call | flops 1610612736 | bytes 6291456 | tf_op jit(solution)/shard_map/coefficients/expand/pallas_call | solution.py:415
  160.2 7.0 %all-to-all-start.4 = ((bf16[16,64,1024]{2,1,0:T(8,128)(2,1)}), bf16[16,64,1024]{2,1,0:T(8,128)(2,1)}, u32[]{:S(2)}, u32[]{:S(2)}) async-start(bf16[16,64,1024]{2,1,0:T(8,128)(2,1)} %get-tuple-element.87), calls=%async_computation.4 | async-start | bytes 4194304 | tf_op jit(solution)/shard_map/transpose_out/all_to_all | solution.py:31
  168.7 0.9 collective-permute-done.23.refs_15_
  169.7 1.3 collective-permute-done.24.refs_21_
  172.7 23.3 %density.1 = f32[1024,4,512]{2,1,0:T(4,128)} custom-call(s32[2]{0:T(128)} %pad_add_fusion.place, bf16[16,160,1024]{2,1,0:T(8,128)(2,1)} %bitcast.57, bf16[16,160,1024]{2,1,0:T(8,128)(2,1)} %bitcast.58, bf16[1024,512]{1,0:T(8,128)(2,1)} %get-tuple-element.89.refs_0_, bf16[512,512]{1,0:T(8,128)(2,1)} %collective-permute-done.19.refs_1_, ...), custom_call_target="tpu_custom_call" | custom-call | flops 12884901888 | bytes 29360128 | tf_op jit(solution)/shard_map/density/density/pallas_call | solution.py:511
  196.0 3.8 %all-to-all-done.4.update = bf16[16,64,1024]{2,1,0:T(8,128)(2,1)} async-done(((bf16[16,64,1024]{2,1,0:T(8,128)(2,1)}), bf16[16,64,1024]{2,1,0:T(8,128)(2,1)}, u32[]{:S(2)}, u32[]{:S(2)}) %all-to-all-start.4) | async-done | bytes 2097184 | tf_op jit(solution)/shard_map/transpose_out/all_to_all | solution.py:31
  199.8 4.8 %subtract_update.1 = f32[64,16384]{1,0:T(8,128)} custom-call(f32[64,16384]{1,0:T(8,128)} %orbs.3, bf16[16,64,1024]{2,1,0:T(8,128)(2,1)} %all-to-all-done.4.update), custom_call_target="tpu_custom_call" | custom-call | flops 1048576 | bytes 10485760 | tf_op jit(solution)/shard_map/subtract/subtract_update/pallas_call | solution.py:316
  (112 shorter events, 17.7 us)
Async XLA Ops:
  7.2 59.7 %copy-start = (f32[256,256]{1,0:T(8,128)S(1)}, f32[256,256]{1,0:T(8,128)}, u32[]{:S(2)}) copy-start(f32[256,256]{1,0:T(8,128)} %param.14) | copy-start | bytes 786436
  13.0 35.4 %all-to-all-start = ((bf16[16,112,512]{2,1,0:T(8,128)(2,1)}), bf16[16,112,512]{2,1,0:T(8,128)(2,1)S(1)}, u32[]{:S(2)}, u32[]{:S(2)}) async-start(bf16[16,112,512]{2,1,0:T(8,128)(2,1)} %get-tuple-element.59), calls=%async_computation | async-start | bytes 3670016 | tf_op jit(solution)/shard_map/transpose_give/all_to_all | solution.py:31
  21.6 150.3 %all-gather.3.cloned.1.call-start = ((), (), s32[]{:S(2)}) async-start(), calls=%async_computation.5 | async-start | bytes 5570560 | tf_op jit(solution)/shard_map/window_exchange/all_gather | solution.py:99
  26.6 8.5 %collective-permute-start.2 = (bf16[80,1024]{1,0:T(8,128)(2,1)S(1)}, bf16[80,1024]{1,0:T(8,128)(2,1)S(1)}, u32[]{:S(2)}, u32[]{:S(2)}) collective-permute-start(bf16[80,1024]{1,0:T(8,128)(2,1)S(1)} %get-tuple-element.126), channel_id=1, source_target_pairs={{0,3},{1,2},{2,1},{3,0},{4,7},{5,6},{6,5},{7,4},{8,11},{9,10},{10,... | collective-permute-start | bytes 491528 | tf_op jit(solution)/shard_map/window_exchange/ppermute | solution.py:88
  30.1 8.6 %collective-permute-start.1 = (bf16[80,1024]{1,0:T(8,128)(2,1)S(1)}, bf16[80,1024]{1,0:T(8,128)(2,1)S(1)}, u32[]{:S(2)}, u32[]{:S(2)}) collective-permute-start(bf16[80,1024]{1,0:T(8,128)(2,1)S(1)} %get-tuple-element.127), channel_id=1, source_target_pairs={{0,2},{2,0},{1,3},{3,1},{4,6},{6,4},{5,7},{7,5},{8,10},{10,8},{9,1... | collective-permute-start | bytes 491528 | tf_op jit(solution)/shard_map/window_exchange/ppermute | solution.py:27
  30.5 8.2 %collective-permute-start = (bf16[80,1024]{1,0:T(8,128)(2,1)S(1)}, bf16[80,1024]{1,0:T(8,128)(2,1)S(1)}, u32[]{:S(2)}, u32[]{:S(2)}) collective-permute-start(bf16[80,1024]{1,0:T(8,128)(2,1)S(1)} %get-tuple-element.128), channel_id=1, source_target_pairs={{0,1},{1,0},{2,3},{3,2},{4,5},{5,4},{6,7},{7,6},{8,9},{9,8},{10,11... | collective-permute-start | bytes 491528 | tf_op jit(solution)/shard_map/window_exchange/ppermute | solution.py:27
  39.1 5.5 %collective-permute-start.3 = (bf16[80,1024]{1,0:T(8,128)(2,1)S(1)}, bf16[80,1024]{1,0:T(8,128)(2,1)S(1)}, u32[]{:S(2)}, u32[]{:S(2)}) collective-permute-start(bf16[80,1024]{1,0:T(8,128)(2,1)S(1)} %fusion.24), channel_id=1, source_target_pairs={{0,4},{4,0},{1,5},{5,1},{2,6},{6,2},{3,7},{7,3},{8,12},{12,8},{9,1... | collective-permute-start | bytes 491528 | tf_op jit(solution)/shard_map/window_exchange/ppermute | solution.py:27
  51.8 30.5 %all-to-all-start.1 = ((bf16[16,64,512]{2,1,0:T(8,128)(2,1)}), bf16[16,64,512]{2,1,0:T(8,128)(2,1)}, u32[]{:S(2)}, u32[]{:S(2)}) async-start(bf16[16,64,512]{2,1,0:T(8,128)(2,1)} %get-tuple-element.64), calls=%async_computation.1 | async-start | bytes 2097152 | tf_op jit(solution)/shard_map/transpose_keep/all_to_all | solution.py:31
  56.3 3.2 %collective-permute-start.4 = (bf16[16,16,128]{2,1,0:T(8,128)(2,1)S(1)}, bf16[16,16,128]{2,1,0:T(8,128)(2,1)S(1)}, u32[]{:S(2)}, u32[]{:S(2)}) collective-permute-start(bf16[16,16,128]{2,1,0:T(8,128)(2,1)S(1)} %slice.90), channel_id=1, source_target_pairs={{0,4},{4,0},{1,5},{5,1},{2,6},{6,2},{3,7},{7,3},{8,12},{12,8},{9,1... | collective-permute-start | bytes 196616 | tf_op jit(solution)/shard_map/transpose_keep/ppermute | solution.py:27
  58.1 13.0 %collective-permute-start.7 = (bf16[16,32,512]{2,1,0:T(8,128)(2,1)}, bf16[16,32,512]{2,1,0:T(8,128)(2,1)S(1)}, u32[]{:S(2)}, u32[]{:S(2)}) collective-permute-start(bf16[16,32,512]{2,1,0:T(8,128)(2,1)} %slice.92), channel_id=1, source_target_pairs={{0,4},{4,0},{1,5},{5,1},{2,6},{6,2},{3,7},{7,3},{8,12},{12,8},{9,1... | collective-permute-start | bytes 1572872 | tf_op jit(solution)/shard_map/transpose_keep/ppermute | solution.py:27
  59.4 1.0 copy-start.3
  60.4 5.9 %copy-start.9 = (f32[256,256]{1,0:T(8,128)S(1)}, f32[256,256]{1,0:T(8,128)}, u32[]{:S(2)}) copy-start(f32[256,256]{1,0:T(8,128)} %param.13) | copy-start | bytes 786436
  61.5 17.9 %collective-permute-start.6 = (bf16[512,512]{1,0:T(8,128)(2,1)}, bf16[512,512]{1,0:T(8,128)(2,1)}, u32[]{:S(2)}, u32[]{:S(2)}) collective-permute-start(bf16[512,512]{1,0:T(8,128)(2,1)} %get-tuple-element.115), channel_id=1, source_target_pairs={{0,6},{2,4},{4,2},{6,0},{1,7},{3,5},{5,3},{7,1},{8,14},{10,12},{12... | collective-permute-start | bytes 1572872 | tf_op jit(solution)/shard_map/transpose_keep/ppermute | solution.py:114
  64.0 18.4 %collective-permute-start.5 = (bf16[512,512]{1,0:T(8,128)(2,1)}, bf16[512,512]{1,0:T(8,128)(2,1)}, u32[]{:S(2)}, u32[]{:S(2)}) collective-permute-start(bf16[512,512]{1,0:T(8,128)(2,1)} %get-tuple-element.115), channel_id=1, source_target_pairs={{0,4},{4,0},{1,5},{5,1},{2,6},{6,2},{3,7},{7,3},{8,12},{12,8},{9,1... | collective-permute-start | bytes 1572872 | tf_op jit(solution)/shard_map/transpose_keep/ppermute | solution.py:27
  71.4 7.2 %copy-start.2 = (bf16[16,2,2,16,512]{4,3,2,0,1:T(8,128)(2,1)}, bf16[16,2,2,16,512]{4,3,2,0,1:T(8,128)(2,1)S(1)}, u32[]{:S(2)}) copy-start(bf16[16,2,2,16,512]{4,3,2,0,1:T(8,128)(2,1)S(1)} %copy.20) | copy-start | bytes 3145732
  72.4 7.0 %copy-start.6 = (bf16[512,512]{1,0:T(8,128)(2,1)}, bf16[512,512]{1,0:T(8,128)(2,1)S(1)}, u32[]{:S(2)}) copy-start(bf16[512,512]{1,0:T(8,128)(2,1)S(1)} %get-tuple-element.93.refs_6_) | copy-start | bytes 1572868
  72.4 9.9 %collective-permute-start.8 = (bf16[512,512]{1,0:T(8,128)(2,1)S(1)}, bf16[512,512]{1,0:T(8,128)(2,1)S(1)}, u32[]{:S(2)}, u32[]{:S(2)}) collective-permute-start(bf16[512,512]{1,0:T(8,128)(2,1)S(1)} %get-tuple-element.93.refs_6_), channel_id=1, source_target_pairs={{0,1},{1,0},{2,3},{3,2},{4,5},{5,4},{6,7},{7,6},{8,9},{9,8},{10,11... | collective-permute-start | bytes 1572872 | tf_op jit(solution)/shard_map/transpose_keep/ppermute | solution.py:27
  88.7 4.9 %collective-permute-start.9 = (bf16[16,32,640]{2,1,0:T(8,128)(2,1)}, bf16[16,32,640]{2,1,0:T(8,128)(2,1)S(1)}, u32[]{:S(2)}, u32[]{:S(2)}) collective-permute-start(bf16[16,32,640]{2,1,0:T(8,128)(2,1)} %get-tuple-element.75), channel_id=1, source_target_pairs={{0,1},{1,0},{2,3},{3,2},{4,5},{5,4},{6,7},{7,6},{8,9},{9,8},{10,11... | collective-permute-start | bytes 1966088 | tf_op jit(solution)/shard_map/project/ppermute | solution.py:27
  91.2 26.5 %collective-permute-start.10 = (bf16[1024,512]{1,0:T(8,128)(2,1)}, bf16[1024,512]{1,0:T(8,128)(2,1)S(1)}, u32[]{:S(2)}, u32[]{:S(2)}) collective-permute-start(bf16[1024,512]{1,0:T(8,128)(2,1)} %bitcast.20.keep.refs_10_), channel_id=1, source_target_pairs={{0,2},{2,0},{1,3},{3,1},{4,6},{6,4},{5,7},{7,5},{8,10},{10,8},{9,1... | collective-permute-start | bytes 3145736 | tf_op jit(solution)/shard_map/project/ppermute | solution.py:27
  93.6 32.2 %copy-start.4 = (f32[512,512]{1,0:T(8,128)S(1)}, f32[512,512]{1,0:T(8,128)}, u32[]{:S(2)}) copy-start(f32[512,512]{1,0:T(8,128)} %convolution_add_fusion) | copy-start | bytes 3145732
  95.8 25.1 %all-to-all-start.2 = ((bf16[16,32,640]{2,1,0:T(8,128)(2,1)}), bf16[16,32,640]{2,1,0:T(8,128)(2,1)S(1)}, u32[]{:S(2)}, u32[]{:S(2)}) async-start(bf16[16,32,640]{2,1,0:T(8,128)(2,1)} %add_convert_fusion), calls=%async_computation.2 | async-start | bytes 1310720 | tf_op jit(solution)/shard_map/project/all_to_all | solution.py:31
  117.7 3.2 %copy-start.11 = (bf16[1024,512]{1,0:T(8,128)(2,1)}, bf16[1024,512]{1,0:T(8,128)(2,1)S(1)}, u32[]{:S(2)}) copy-start(bf16[1024,512]{1,0:T(8,128)(2,1)S(1)} %collective-permute-done.10.refs_16_) | copy-start | bytes 3145732
  120.9 13.2 %copy-start.8 = (bf16[512,512]{1,0:T(8,128)(2,1)S(1)}, bf16[512,512]{1,0:T(8,128)(2,1)}, u32[]{:S(2)}) copy-start(bf16[512,512]{1,0:T(8,128)(2,1)} %get-tuple-element.82) | copy-start | bytes 1572868
  120.9 4.9 %collective-permute-start.11 = (f32[32,640]{1,0:T(8,128)S(1)}, f32[32,640]{1,0:T(8,128)S(1)}, u32[]{:S(2)}, u32[]{:S(2)}) collective-permute-start(f32[32,640]{1,0:T(8,128)S(1)} %convert_reduce_fusion), channel_id=1, source_target_pairs={{0,2},{2,0},{1,3},{3,1},{4,6},{6,4},{5,7},{7,5},{8,10},{10,8},{9,1... | collective-permute-start | bytes 245768 | tf_op jit(solution)/shard_map/project/ppermute | solution.py:27
  123.7 12.6 %collective-permute-start.12 = (bf16[1024,512]{1,0:T(8,128)(2,1)}, bf16[1024,512]{1,0:T(8,128)(2,1)}, u32[]{:S(2)}, u32[]{:S(2)}) collective-permute-start(bf16[1024,512]{1,0:T(8,128)(2,1)} %bitcast.20.keep.refs_10_), channel_id=1, source_target_pairs={{0,1},{1,0},{2,3},{3,2},{4,5},{5,4},{6,7},{7,6},{8,9},{9,8},{10,11... | collective-permute-start | bytes 3145736 | tf_op jit(solution)/shard_map/coefficients/ppermute | solution.py:27
  124.7 11.5 %collective-permute-start.14 = (bf16[512,512]{1,0:T(8,128)(2,1)}, bf16[512,512]{1,0:T(8,128)(2,1)}, u32[]{:S(2)}, u32[]{:S(2)}) collective-permute-start(bf16[512,512]{1,0:T(8,128)(2,1)} %collective-permute-done.5.refs_11_), channel_id=1, source_target_pairs={{0,1},{1,0},{2,3},{3,2},{4,5},{5,4},{6,7},{7,6},{8,9},{9,8},{10,11... | collective-permute-start | bytes 1572872 | tf_op jit(solution)/shard_map/coefficients/ppermute | solution.py:27
  124.8 24.9 %collective-permute-start.13 = (bf16[1024,512]{1,0:T(8,128)(2,1)}, bf16[1024,512]{1,0:T(8,128)(2,1)}, u32[]{:S(2)}, u32[]{:S(2)}) collective-permute-start(bf16[1024,512]{1,0:T(8,128)(2,1)} %copy-done.11), channel_id=1, source_target_pairs={{0,1},{1,0},{2,3},{3,2},{4,5},{5,4},{6,7},{7,6},{8,9},{9,8},{10,11... | collective-permute-start | bytes 3145736 | tf_op jit(solution)/shard_map/coefficients/ppermute | solution.py:27
  126.6 24.4 %copy-start.7 = (bf16[512,512]{1,0:T(8,128)(2,1)S(1)}, bf16[512,512]{1,0:T(8,128)(2,1)}, u32[]{:S(2)}) copy-start(bf16[512,512]{1,0:T(8,128)(2,1)} %get-tuple-element.95) | copy-start | bytes 1572868
  127.5 22.2 %all-to-all-start.3 = ((bf16[16,32,640]{2,1,0:T(8,128)(2,1)}), bf16[16,32,640]{2,1,0:T(8,128)(2,1)S(1)}, u32[]{:S(2)}, u32[]{:S(2)}) async-start(bf16[16,32,640]{2,1,0:T(8,128)(2,1)} %broadcast_in_dim.8), calls=%async_computation.3 | async-start | bytes 1310720 | tf_op jit(solution)/shard_map/coefficients/all_to_all | solution.py:31
  131.8 4.4 %collective-permute-start.15 = (bf16[512,512]{1,0:T(8,128)(2,1)}, bf16[512,512]{1,0:T(8,128)(2,1)S(1)}, u32[]{:S(2)}, u32[]{:S(2)}) collective-permute-start(bf16[512,512]{1,0:T(8,128)(2,1)} %collective-permute-done.6.refs_17_), channel_id=1, source_target_pairs={{0,1},{1,0},{2,3},{3,2},{4,5},{5,4},{6,7},{7,6},{8,9},{9,8},{10,11... | collective-permute-start | bytes 1572872 | tf_op jit(solution)/shard_map/coefficients/ppermute | solution.py:27
  134.1 14.7 %collective-permute-start.17 = (bf16[512,512]{1,0:T(8,128)(2,1)S(1)}, bf16[512,512]{1,0:T(8,128)(2,1)S(1)}, u32[]{:S(2)}, u32[]{:S(2)}) collective-permute-start(bf16[512,512]{1,0:T(8,128)(2,1)S(1)} %copy-done.8), channel_id=1, source_target_pairs={{0,6},{2,4},{4,2},{6,0},{1,7},{3,5},{5,3},{7,1},{8,14},{10,12},{12... | collective-permute-start | bytes 1572872 | tf_op jit(solution)/shard_map/coefficients/ppermute | solution.py:168
  136.2 13.4 %collective-permute-start.16 = (bf16[512,512]{1,0:T(8,128)(2,1)S(1)}, bf16[512,512]{1,0:T(8,128)(2,1)}, u32[]{:S(2)}, u32[]{:S(2)}) collective-permute-start(bf16[512,512]{1,0:T(8,128)(2,1)S(1)} %copy-done.8), channel_id=1, source_target_pairs={{0,4},{4,0},{1,5},{5,1},{2,6},{6,2},{3,7},{7,3},{8,12},{12,8},{9,1... | collective-permute-start | bytes 1572872 | tf_op jit(solution)/shard_map/coefficients/ppermute | solution.py:27
  136.3 12.5 %copy-start.14 = (bf16[512,512]{1,0:T(8,128)(2,1)}, bf16[512,512]{1,0:T(8,128)(2,1)S(1)}, u32[]{:S(2)}) copy-start(bf16[512,512]{1,0:T(8,128)(2,1)S(1)} %collective-permute-done.15.refs_20_) | copy-start | bytes 1572868
  148.8 0.8 copy-start.15
  149.7 4.1 %copy-start.5 = (bf16[16,32,640]{2,1,0:T(8,128)(2,1)}, bf16[16,32,640]{2,1,0:T(8,128)(2,1)S(1)}, u32[]{:S(2)}) copy-start(bf16[16,32,640]{2,1,0:T(8,128)(2,1)S(1)} %all-to-all-done.3.mine) | copy-start | bytes 1966084
  149.7 3.3 %collective-permute-start.18 = (bf16[16,32,640]{2,1,0:T(8,128)(2,1)S(1)}, bf16[16,32,640]{2,1,0:T(8,128)(2,1)S(1)}, u32[]{:S(2)}, u32[]{:S(2)}) collective-permute-start(bf16[16,32,640]{2,1,0:T(8,128)(2,1)S(1)} %all-to-all-done.3.mine), channel_id=1, source_target_pairs={{0,1},{1,0},{2,3},{3,2},{4,5},{5,4},{6,7},{7,6},{8,9},{9,8},{10,11... | collective-permute-start | bytes 1966088 | tf_op jit(solution)/shard_map/coefficients/ppermute | solution.py:27
  150.8 17.2 %collective-permute-start.19 = (bf16[512,512]{1,0:T(8,128)(2,1)S(1)}, bf16[512,512]{1,0:T(8,128)(2,1)}, u32[]{:S(2)}, u32[]{:S(2)}) collective-permute-start(bf16[512,512]{1,0:T(8,128)(2,1)S(1)} %bitcast.53), channel_id=1, source_target_pairs={{0,4},{4,0},{1,5},{5,1},{2,6},{6,2},{3,7},{7,3},{8,12},{12,8},{9,1... | collective-permute-start | bytes 1572872 | tf_op jit(solution)/shard_map/coefficients/ppermute | solution.py:27
  150.9 17.5 %collective-permute-start.21 = (bf16[512,512]{1,0:T(8,128)(2,1)S(1)}, bf16[512,512]{1,0:T(8,128)(2,1)}, u32[]{:S(2)}, u32[]{:S(2)}) collective-permute-start(bf16[512,512]{1,0:T(8,128)(2,1)S(1)} %copy-done.7), channel_id=1, source_target_pairs={{0,6},{2,4},{4,2},{6,0},{1,7},{3,5},{5,3},{7,1},{8,14},{10,12},{12... | collective-permute-start | bytes 1572872 | tf_op jit(solution)/shard_map/density/ppermute | solution.py:182
  152.9 0.8 copy-start.12
  160.2 7.7 %copy-start.16 = (bf16[512,512]{1,0:T(8,128)(2,1)S(1)}, bf16[512,512]{1,0:T(8,128)(2,1)}, u32[]{:S(2)}) copy-start(bf16[512,512]{1,0:T(8,128)(2,1)} %copy-done.15) | copy-start | bytes 1572868
  160.2 39.6 %all-to-all-start.4 = ((bf16[16,64,1024]{2,1,0:T(8,128)(2,1)}), bf16[16,64,1024]{2,1,0:T(8,128)(2,1)}, u32[]{:S(2)}, u32[]{:S(2)}) async-start(bf16[16,64,1024]{2,1,0:T(8,128)(2,1)} %get-tuple-element.87), calls=%async_computation.4 | async-start | bytes 4194304 | tf_op jit(solution)/shard_map/transpose_out/all_to_all | solution.py:31
  167.3 2.4 %collective-permute-start.23 = (bf16[512,512]{1,0:T(8,128)(2,1)}, bf16[512,512]{1,0:T(8,128)(2,1)S(1)}, u32[]{:S(2)}, u32[]{:S(2)}) collective-permute-start(bf16[512,512]{1,0:T(8,128)(2,1)} %collective-permute-done.16.refs_12_), channel_id=1, source_target_pairs={{0,1},{1,0},{2,3},{3,2},{4,5},{5,4},{6,7},{7,6},{8,9},{9,8},{10,11... | collective-permute-start | bytes 1572872 | tf_op jit(solution)/shard_map/density/ppermute | solution.py:27
  167.9 3.0 %collective-permute-start.24 = (bf16[512,512]{1,0:T(8,128)(2,1)S(1)}, bf16[512,512]{1,0:T(8,128)(2,1)S(1)}, u32[]{:S(2)}, u32[]{:S(2)}) collective-permute-start(bf16[512,512]{1,0:T(8,128)(2,1)S(1)} %copy-done.16), channel_id=1, source_target_pairs={{0,1},{1,0},{2,3},{3,2},{4,5},{5,4},{6,7},{7,6},{8,9},{9,8},{10,11... | collective-permute-start | bytes 1572872 | tf_op jit(solution)/shard_map/density/ppermute | solution.py:27
  168.0 3.1 %collective-permute-start.20 = (bf16[512,512]{1,0:T(8,128)(2,1)}, bf16[512,512]{1,0:T(8,128)(2,1)S(1)}, u32[]{:S(2)}, u32[]{:S(2)}) collective-permute-start(bf16[512,512]{1,0:T(8,128)(2,1)} %collective-permute-done.19.refs_1_), channel_id=1, source_target_pairs={{0,1},{1,0},{2,3},{3,2},{4,5},{5,4},{6,7},{7,6},{8,9},{9,8},{10,11... | collective-permute-start | bytes 1572872 | tf_op jit(solution)/shard_map/density/ppermute | solution.py:27
  168.4 3.5 %collective-permute-start.22 = (bf16[512,512]{1,0:T(8,128)(2,1)}, bf16[512,512]{1,0:T(8,128)(2,1)S(1)}, u32[]{:S(2)}, u32[]{:S(2)}) collective-permute-start(bf16[512,512]{1,0:T(8,128)(2,1)} %collective-permute-done.21.refs_8_), channel_id=1, source_target_pairs={{0,1},{1,0},{2,3},{3,2},{4,5},{5,4},{6,7},{7,6},{8,9},{9,8},{10,11... | collective-permute-start | bytes 1572872 | tf_op jit(solution)/shard_map/density/ppermute | solution.py:27
  169.7 1.3 copy-start.17
  171.9 0.8 copy-start.20
  199.8 4.8 %copy-start.1 = (f32[256,256]{1,0:T(8,128)S(1)}, f32[256,256]{1,0:T(8,128)}, u32[]{:S(2)}) copy-start(f32[256,256]{1,0:T(8,128)} %param.14) | copy-start | bytes 786436
  (4 other events, 3.2 us)
Sparse Core Ops, SparseCore 0:
  48.5 69.5 all-gather.2

commit v5 on v4

--- a/solution.py
+++ b/solution.py
@@ -63,7 +63,7 @@
         occ_low = (rest - occ_mid.astype(jnp.float32)).astype(bf16)
         extra = jnp.zeros((16, half), bf16)
         extra = extra.at[:3, :n_orbs].set(jnp.stack([occ_high, occ_mid, occ_low]))
-        give_p, keep_p = pack(side_xl, eigvecs, panel_one, panel_two, extra, chunk)
+        give_p = pack(1 - side_xl, eigvecs, chunk, (panel_one, panel_two))
 
     with jax.named_scope("transpose_give"):
         got = exchange(give_p, ZY)
@@ -95,35 +95,22 @@
 
         win_vecs = by_xl(mine[n_orbs:], mine_x[n_orbs:], 0).reshape(2 * n_all, rows)
         window = jnp.concatenate([mine[:n_orbs], mine_x[:n_orbs], win_vecs], axis=0)
+        keep_p = pack(side_xl, eigvecs, chunk, (extra,))
         got, keep_p, window = tie(got, keep_p, window)
         window = lax.all_gather(window, ZY, axis=0)
 
     with jax.named_scope("transpose_keep"):
-        keep = exchange(keep_p, ZY)
+        kept = exchange(keep_p, ZY)
         give = got[:, :n_orbs].reshape(16 * n_orbs, half)
-        vec_own = got[:, n_orbs : n_orbs + 2 * n_all]
-        occ_own = got[:, n_orbs + 2 * n_all :, :128]
-        vec_oth = swap(vec_own, "xl")
-        occ_oth = swap(occ_own, "xl")
+        vec_own = [got[:, n_orbs + i * n_all : n_orbs + (i + 1) * n_all] for i in range(2)]
+        vec_oth = [swap(value, "xl") for value in vec_own]
         quarter = 8 * n_orbs
-        count, factor_one, factor_two, give, occ_oth = tie(
-            occupied_count, factor_one, factor_two, give, occ_oth
-        )
+        diff_oth = lax.ppermute(give, ("xl", "xh"), both_flip)
+        factor_one, factor_two, give, *vec_oth = tie(factor_one, factor_two, give, *vec_oth)
         give_a, give_b = give[:quarter], give[quarter:]
         same_a = swap(give_a, "xl")
-        diff_a = lax.ppermute(give_a, ("xl", "xh"), both_flip)
-
-        def weight_of(occ, side):
-            occ = occ[:, :3, :n_orbs].astype(jnp.float32)
-            occ = (occ[:, 0] + occ[:, 1]) + occ[:, 2]
-            index = (jnp.arange(16, dtype=jnp.int32)[:, None] * 2 + side) * n_orbs
-            index = index + jnp.arange(n_orbs, dtype=jnp.int32)[None]
-            occ = jnp.where(index < count[0], occ / math.sqrt(OCC), jnp.float32(0.0))
-            return occ.reshape(16 * n_orbs, 1)
-
-        weight_own, weight_oth = weight_of(occ_own, xl), weight_of(occ_oth, 1 - xl)
-        vecs = by_xl(vec_own.reshape(16, 2, n_all, half), vec_oth.reshape(16, 2, n_all, half), 2)
-        vecs = vecs.transpose(1, 0, 2, 3, 4)
+
+        vecs = jnp.stack([by_xl(own, oth, 1) for own, oth in zip(vec_own, vec_oth)])
         vec_two = vecs.reshape(2, 32, 2, n_vec, half)[:, :, 1].reshape(2, pw, half)
         vecs = vecs.reshape(2, 2 * pw, half)
         vec_keep = lax.dynamic_index_in_dim(vecs, xl, 0, keepdims=False)
@@ -141,36 +128,45 @@
         wide_high = wide.astype(bf16)
         wide_low = (wide - wide_high.astype(jnp.float32)).astype(bf16)
         vec_keep_c = swap(vec_keep, "c")
-        keep, same_a, diff_a, vecs, vec_two, vec_keep = tie(
-            keep, same_a, diff_a, vecs, vec_two, vec_keep
+        kept, same_a, diff_oth, vecs, vec_two, vec_keep = tie(
+            kept, same_a, diff_oth, vecs, vec_two, vec_keep
         )
-        keep, vec_keep_c = tie(keep, vec_keep_c)
-        keep, weight_own, weight_oth, factor, wide_high, wide_low = tie(
-            keep, weight_own, weight_oth, factor, wide_high, wide_low
-        )
-        keep = keep.reshape(16 * n_orbs, half)
+        kept, vec_keep_c = tie(kept, vec_keep_c)
+        kept, factor, wide_high, wide_low = tie(kept, factor, wide_high, wide_low)
+        keep = kept[:, :n_orbs].reshape(16 * n_orbs, half)
+        occ_own = kept[:, n_orbs:, :128]
 
     with jax.named_scope("project"):
         cross = swap(keep, "xh")
-        parts, parts_c = project(side_xl, place, give, keep, vecs, vec_two)
+        occ_oth = swap(occ_own, "xl")
+        parts, parts_c = project(side_xl, place, give, kept, vecs, vec_two)
         parts = parts.astype(jnp.float32) + swap(parts_c, "c").astype(jnp.float32)
         summed = exchange(parts.astype(bf16), ZY)
-        summed, cross = tie(summed, cross)
+        summed, cross, occ_oth = tie(summed, cross, occ_oth)
         summed = summed.astype(jnp.float32).sum(0)
         summed = summed + swap(summed, "xh")
-        summed, give_b = tie(summed, give_b)
+        summed, give_b, vec_give = tie(summed, give_b, vec_give)
 
     with jax.named_scope("coefficients"):
         share = dot(summed[:, : 2 * pw], factor, ((1,), (0,)), precision=high)
         share = jnp.concatenate([share, summed[:, 2 * pw :]], axis=1).astype(bf16)
         every = exchange(jnp.broadcast_to(share[None], (16,) + share.shape), ZY)
+        def weight_of(occ, side):
+            occ = occ[:, :3, :n_orbs].astype(jnp.float32)
+            occ = (occ[:, 0] + occ[:, 1]) + occ[:, 2]
+            index = (jnp.arange(16, dtype=jnp.int32)[:, None] * 2 + side) * n_orbs
+            index = index + jnp.arange(n_orbs, dtype=jnp.int32)[None]
+            occ = jnp.where(index < occupied_count[0], occ / math.sqrt(OCC), jnp.float32(0.0))
+            return occ.reshape(16 * n_orbs, 1)
+
+        weight_own, weight_oth = weight_of(occ_own, xl), weight_of(occ_oth, 1 - xl)
         same_b = swap(give_b, "xl")
-        diff_b = lax.ppermute(give_b, ("xl", "xh"), both_flip)
-        keep_c, cross_c, same_a_c, diff_a_c = (swap(v, "c") for v in (keep, cross, same_a, diff_a))
-        every, keep_c, cross_c, same_a_c, diff_a_c, same_b, diff_b = tie(
-            every, keep_c, cross_c, same_a_c, diff_a_c, same_b, diff_b
+        vec_keep_x = lax.ppermute(vec_give, ("xl", "xh"), both_flip)
+        keep_c, cross_c, same_a_c, diff_c = (swap(v, "c") for v in (keep, cross, same_a, diff_oth))
+        every, keep_c, cross_c, same_a_c, diff_c, same_b, vec_keep_x = tie(
+            every, keep_c, cross_c, same_a_c, diff_c, same_b, vec_keep_x
         )
-        every, vec_give = tie(every, vec_give)
+        every, weight_own, weight_oth = tie(every, weight_own, weight_oth)
         every_c = swap(every, "c")
         coeffs_x = swap(every[:, :, : 2 * pw].reshape(quarter, 2 * pw), "xl")
         coeffs, mixed, update = expand(place, every, every_c, wide_high, wide_low, vecs, n_orbs)
@@ -179,9 +175,7 @@
         back = exchange(update, ZY)
 
     with jax.named_scope("density"):
-        vec_keep_x = lax.ppermute(vec_give, ("xl", "xh"), both_flip)
-        vec_keep_xc = swap(vec_keep_x, "c")
-        same_b_c, diff_b_c = swap(same_b, "c"), swap(diff_b, "c")
+        vec_keep_xc, same_b_c = swap(vec_keep_x, "c"), swap(same_b, "c")
         coeffs_y = swap(coeffs_x, "c")
         density = density_of(
             place,
@@ -194,8 +188,8 @@
             [
                 ([keep], [same_a, same_b]),
                 ([keep_c], [same_a_c, same_b_c]),
-                ([cross], [diff_a, diff_b]),
-                ([cross_c], [diff_a_c, diff_b_c]),
+                ([cross], [diff_oth]),
+                ([cross_c], [diff_c]),
             ],
         )
 
@@ -209,76 +203,60 @@
     return pl.CostEstimate(flops=flops, bytes_accessed=bytes_accessed, transcendentals=0)
 
 
-def pack_kernel(side, orbs, panel_one, panel_two, extra, give, keep, *scratch):
-    orbs_v, one_v, two_v, give_v, keep_v, sems = scratch
-    parts, n_orbs, half = keep.shape
-    n_vec = panel_one.shape[0]
-    step = parts // STEPS
-    loads = [
-        pltpu.make_async_copy(panel_one, one_v, sems.at[0]),
-        pltpu.make_async_copy(panel_two, two_v, sems.at[1]),
-    ]
-    for i in range(STEPS):
-        at = pl.ds(i * step * 2 * half, step * 2 * half)
-        loads.append(pltpu.make_async_copy(orbs.at[:, at], orbs_v.at[:, at], sems.at[2 + i]))
+def pack_kernel(n_tails, which, orbs, *refs):
+    tails, out, orbs_v, out_v = refs[:n_tails], refs[n_tails], refs[n_tails + 1], refs[n_tails + 2]
+    sems, tails_v = refs[-1], refs[n_tails + 3 : -1]
+    parts, n_orbs, half = orbs_v.shape
+    loads = []
+    for i in range(parts):
+        at = pl.ds(pl.multiple_of((2 * i + which[0]) * half, half), half)
+        loads.append(pltpu.make_async_copy(orbs.at[:, at], orbs_v.at[i], sems.at[i]))
+    for i, (tail, tail_v) in enumerate(zip(tails, tails_v)):
+        loads.append(pltpu.make_async_copy(tail, tail_v, sems.at[parts + i]))
     for load in loads:
         load.start()
-    for load in loads[:2]:
+    for load in loads[parts:]:
         load.wait()
     stores = []
-    for i in range(STEPS):
-        loads[2 + i].wait()
-        for part in range(i * step, (i + 1) * step):
-            for out, which in ((keep_v, side[0]), (give_v, 1 - side[0])):
-                at = pl.multiple_of((2 * part + which) * half, half)
-                out[part, :n_orbs, :] = orbs_v[:, pl.ds(at, half)].astype(jnp.bfloat16)
-            for which in range(2):
-                at = pl.ds((2 * part + which) * half, half)
-                rows = pl.ds(n_orbs + which * 2 * n_vec, 2 * n_vec)
-                both = jnp.concatenate([one_v[:, at], two_v[:, at]], axis=0)
-                give_v[part, rows, :] = both
-            give_v[part, pl.ds(n_orbs + 4 * n_vec, 16), :] = extra[...]
-        at = pl.ds(i * step, step)
-        for j, (source, target) in enumerate(((give_v, give), (keep_v, keep))):
-            sem = sems.at[2 + (1 + j) * STEPS + i]
-            stores.append(pltpu.make_async_copy(source.at[at], target.at[at], sem))
+    for i in range(parts):
+        loads[i].wait()
+        out_v[i, :n_orbs, :] = orbs_v[i].astype(jnp.bfloat16)
+        if n_tails == 2:
+            for side in range(2):
+                at = pl.ds((2 * i + side) * half, half)
+                both = jnp.concatenate([tail_v[:, at] for tail_v in tails_v], axis=0)
+                out_v[i, pl.ds(n_orbs + side * 16, 16), :] = both
+        else:
+            out_v[i, pl.ds(n_orbs, 16), :] = tails_v[0][...]
+        if i % 4 == 3:
+            at = pl.ds(i - 3, 4)
+            sem = sems.at[parts + n_tails + i // 4]
+            stores.append(pltpu.make_async_copy(out_v.at[at], out.at[at], sem))
             stores[-1].start()
     for store in stores:
         store.wait()
 
 
-def pack(side, orbs, panel_one, panel_two, extra, chunk):
+def pack(which, orbs, chunk, tails):
     n_orbs, n_basis = orbs.shape
     parts, half = n_basis // chunk, chunk // 2
-    n_give = n_orbs + 4 * panel_one.shape[0] + 16
     anywhere = pl.BlockSpec(memory_space=pl.ANY)
-    give = (parts, n_give, half)
-    keep = (parts, n_orbs, half)
+    shape = (parts, n_orbs + 16 * (2 if len(tails) == 2 else 1), half)
     return pl.pallas_call(
-        pack_kernel,
-        out_shape=(
-            jax.ShapeDtypeStruct(give, jnp.bfloat16),
-            jax.ShapeDtypeStruct(keep, jnp.bfloat16),
-        ),
-        grid_spec=pltpu.PrefetchScalarGridSpec(
-            num_scalar_prefetch=1,
-            grid=(1,),
-            in_specs=[anywhere, anywhere, anywhere]
-            + [pl.BlockSpec(extra.shape, lambda i, _: (0, 0))],
-            out_specs=(anywhere, anywhere),
-            scratch_shapes=[
-                pltpu.VMEM(orbs.shape, jnp.float32),
-                pltpu.VMEM(panel_one.shape, jnp.bfloat16),
-                pltpu.VMEM(panel_two.shape, jnp.bfloat16),
-                pltpu.VMEM(give, jnp.bfloat16),
-                pltpu.VMEM(keep, jnp.bfloat16),
-                pltpu.SemaphoreType.DMA((2 + 3 * STEPS,)),
-            ],
-        ),
+        functools.partial(pack_kernel, len(tails)),
+        out_shape=jax.ShapeDtypeStruct(shape, jnp.bfloat16),
+        in_specs=[pl.BlockSpec(memory_space=pltpu.SMEM)] + [anywhere] * (1 + len(tails)),
+        out_specs=anywhere,
+        scratch_shapes=[
+            pltpu.VMEM((parts, n_orbs, half), jnp.float32),
+            pltpu.VMEM(shape, jnp.bfloat16),
+            *[pltpu.VMEM(tail.shape, jnp.bfloat16) for tail in tails],
+            pltpu.SemaphoreType.DMA((parts + len(tails) + parts // 4,)),
+        ],
         compiler_params=pltpu.CompilerParams(vmem_limit_bytes=62 * 2**20),
-        cost_estimate=cost(0, 7 * n_orbs * n_basis),
-        name="pack",
-    )(side, orbs, panel_one, panel_two, extra)
+        cost_estimate=cost(0, 3 * n_orbs * n_basis),
+        name="pack_vectors" if len(tails) == 2 else "pack_weights",
+    )(which, orbs, *tails)
 
 
 def subtract_kernel(orbs, update, out, orbs_v, update_v, sems):
@@ -329,89 +307,91 @@
     )(orbs, update)
 
 
-def project_kernel(side, place, give, keep, vecs, vec_two, mine, theirs):
+def project_kernel(side, place, give, keep, vecs, vec_two, mine, theirs, blocks_v, sems):
     blocks, n_own, lanes = mine.shape
     width = vecs.shape[1]
-    proj = dot(give[...], vecs[1 - side[0]], ((1,), (1,)))
-    proj = proj + dot(keep[...], vecs[side[0]], ((1,), (1,)))
-    cross = dot(vecs[0], vec_two[0], ((1,), (1,)))
-    cross = cross + dot(vecs[1], vec_two[1], ((1,), (1,)))
-
-    def store(out):
-        out[:, :, :width] = proj.astype(jnp.bfloat16).reshape(blocks, n_own, width)
-        out[:, :, width:] = cross.astype(jnp.bfloat16).reshape(blocks, n_own, lanes - width)
-
-    pl.when(pl.program_id(0) == place[1])(lambda: store(mine))
-    pl.when(pl.program_id(0) != place[1])(lambda: store(theirs))
+    n_rows, n_two = blocks * n_own, lanes - width
+    stores = []
+    for i, (out, half) in enumerate(((theirs, 1 - place[1]), (mine, place[1]))):
+        at = pl.ds(pl.multiple_of(half * n_rows, n_rows), n_rows)
+        proj = dot(give[at, :], vecs[1 - side[0]], ((1,), (1,)))
+        rows = keep[pl.ds(half * (blocks // 2), blocks // 2), : 2 * n_own, :]
+        rows = rows.reshape(n_rows, keep.shape[2])
+        proj = proj + dot(rows, vecs[side[0]], ((1,), (1,)))
+        blocks_v[i, :, :, :width] = proj.astype(jnp.bfloat16).reshape(blocks, n_own, width)
+        at = pl.ds(pl.multiple_of(half * n_two, n_two), n_two)
+        cross = dot(vecs[0], vec_two[0, at, :], ((1,), (1,)))
+        cross = cross + dot(vecs[1], vec_two[1, at, :], ((1,), (1,)))
+        blocks_v[i, :, :, width:] = cross.astype(jnp.bfloat16).reshape(blocks, n_own, n_two)
+        stores.append(pltpu.make_async_copy(blocks_v.at[i], out, sems.at[i]))
+        stores[-1].start()
+    for store in stores:
+        store.wait()
+
+
+def specs_of(n_scalars, n_arrays):
+    scalar = pl.BlockSpec(memory_space=pltpu.SMEM)
+    return [scalar] * n_scalars + [pl.BlockSpec(memory_space=pltpu.VMEM)] * n_arrays
 
 
 def project(side, place, give, keep, vecs, vec_two):
-    n_orbs, half = give.shape
-    width, n_two = vecs.shape[1], vec_two.shape[1]
-    tile, lanes = n_orbs // 2, n_two // 2
-    shape = (16, n_orbs // 32, width + lanes)
+    shape = (16, give.shape[0] // 32, vecs.shape[1] + vec_two.shape[1] // 2)
     return pl.pallas_call(
         project_kernel,
         out_shape=(jax.ShapeDtypeStruct(shape, jnp.bfloat16),) * 2,
-        grid_spec=pltpu.PrefetchScalarGridSpec(
-            num_scalar_prefetch=2,
-            grid=(2,),
-            in_specs=[
-                pl.BlockSpec((tile, half), lambda i, *_: (i, 0)),
-                pl.BlockSpec((tile, half), lambda i, *_: (i, 0)),
-                pl.BlockSpec(vecs.shape, lambda i, *_: (0, 0, 0)),
-                pl.BlockSpec((2, lanes, half), lambda i, *_: (0, i, 0)),
-            ],
-            out_specs=(pl.BlockSpec(shape, lambda i, *_: (0, 0, 0)),) * 2,
-        ),
-        compiler_params=pltpu.CompilerParams(vmem_limit_bytes=62 * 2**20),
+        in_specs=specs_of(2, 4),
+        out_specs=(pl.BlockSpec(memory_space=pltpu.HBM),) * 2,
+        scratch_shapes=[
+            pltpu.VMEM((2,) + shape, jnp.bfloat16),
+            pltpu.SemaphoreType.DMA((2,)),
+        ],
+        compiler_params=pltpu.CompilerParams(vmem_limit_bytes=20 * 2**20),
         cost_estimate=cost(1, 1),
         name="project",
     )(side, place, give, keep, vecs, vec_two)
 
 
-def expand_kernel(place, mine, theirs, wide_high, wide_low, vecs, coeffs, mixed, update):
+def expand_kernel(place, mine, theirs, wide_high, wide_low, vecs, *rest):
+    coeffs, mixed, update, coeffs_v, mixed_v, update_v, sems = rest
     width, half = vecs.shape[1:]
     blocks, n_own, lanes = mine.shape
     lanes = lanes - width
-
-    @pl.when(pl.program_id(0) == 0)
-    def _():
-        total = None
-        for core, every in ((place[1], mine), (1 - place[1], theirs)):
-            cross = every[:, :, width:].reshape(width, lanes)
-            for wide in (wide_high, wide_low):
-                term = dot(cross, wide[core], ((1,), (0,)))
-                total = term if total is None else total + term
-        row = lax.broadcasted_iota(jnp.int32, total.shape, 0)
-        first = jnp.bitwise_and(lax.shift_right_logical(row, 3), 1) == 0
-        mixed[...] = jnp.where(first, total, 0.0).astype(jnp.bfloat16)
-
-    def fill(every):
-        base = every[:, :, :width].reshape(blocks * n_own, width)
-        fixed = base.astype(jnp.float32) - dot(base, mixed[...], ((1,), (0,)))
+    n_rows, n_parts, n_orbs = blocks * n_own, update.shape[0] // 2, update.shape[1]
+    halves = ((place[1], mine), (1 - place[1], theirs))
+    total = None
+    for core, every in halves:
+        cross = every[:, :, width:].reshape(width, lanes)
+        for wide in (wide_high, wide_low):
+            term = dot(cross, wide[core], ((1,), (0,)))
+            total = term if total is None else total + term
+    row = lax.broadcasted_iota(jnp.int32, total.shape, 0)
+    first = jnp.bitwise_and(lax.shift_right_logical(row, 3), 1) == 0
+    mixed_v[...] = jnp.where(first, total, 0.0).astype(jnp.bfloat16)
+    stores = [pltpu.make_async_copy(mixed_v, mixed, sems.at[0])]
+    stores[0].start()
+    for i, (core, every) in enumerate(halves):
+        base = every[:, :, :width].reshape(n_rows, width)
+        fixed = base.astype(jnp.float32) - dot(base, mixed_v[...], ((1,), (0,)))
         fixed = fixed.astype(jnp.bfloat16)
-        coeffs[...] = fixed
+        coeffs_v[i] = fixed
         for part in range(2):
             new = dot(fixed, vecs[part], ((1,), (0,))).astype(jnp.bfloat16)
-            shape = update.shape[:2] + (half,)
-            update[:, :, part * half : (part + 1) * half] = new.reshape(shape)
-
-    pl.when(pl.program_id(0) == 0)(lambda: fill(mine))
-    pl.when(pl.program_id(0) == 1)(lambda: fill(theirs))
+            new = new.reshape(n_parts, n_orbs, half)
+            update_v[i, :, :, part * half : (part + 1) * half] = new
+        at = pl.ds(pl.multiple_of(core * n_rows, n_rows), n_rows)
+        stores.append(pltpu.make_async_copy(coeffs_v.at[i], coeffs.at[at], sems.at[1 + i]))
+        at = pl.ds(core * n_parts, n_parts)
+        stores.append(pltpu.make_async_copy(update_v.at[i], update.at[at], sems.at[3 + i]))
+        for store in stores[-2:]:
+            store.start()
+    for store in stores:
+        store.wait()
 
 
 def expand(place, mine, theirs, wide_high, wide_low, vecs, n_orbs):
     _, width, half = vecs.shape
     total = 2 * mine.shape[0] * mine.shape[1]
     wide_high, wide_low = (v.reshape(2, v.shape[0] // 2, width) for v in (wide_high, wide_low))
-
-    def whole(value):
-        return pl.BlockSpec(value.shape, lambda i, _: (0, 0, 0), pipeline_mode=pl.Buffered(1))
-
-    def core(i, place):
-        return i + place[1] - 2 * i * place[1]
-
     return pl.pallas_call(
         expand_kernel,
         out_shape=(
@@ -419,17 +399,15 @@
             jax.ShapeDtypeStruct((width, width), jnp.bfloat16),
             jax.ShapeDtypeStruct((16, n_orbs, 2 * half), jnp.bfloat16),
         ),
-        grid_spec=pltpu.PrefetchScalarGridSpec(
-            num_scalar_prefetch=1,
-            grid=(2,),
-            in_specs=[whole(value) for value in (mine, theirs, wide_high, wide_low, vecs)],
-            out_specs=(
-                pl.BlockSpec((total // 2, width), lambda i, place: (core(i, place), 0)),
-                pl.BlockSpec((width, width), lambda i, _: (0, 0)),
-                pl.BlockSpec((8, n_orbs, 2 * half), lambda i, place: (core(i, place), 0, 0)),
-            ),
-        ),
-        compiler_params=pltpu.CompilerParams(vmem_limit_bytes=62 * 2**20),
+        in_specs=specs_of(1, 5),
+        out_specs=(pl.BlockSpec(memory_space=pltpu.HBM),) * 3,
+        scratch_shapes=[
+            pltpu.VMEM((2, total // 2, width), jnp.bfloat16),
+            pltpu.VMEM((width, width), jnp.bfloat16),
+            pltpu.VMEM((2, 8, n_orbs, 2 * half), jnp.bfloat16),
+            pltpu.SemaphoreType.DMA((5,)),
+        ],
+        compiler_params=pltpu.CompilerParams(vmem_limit_bytes=60 * 2**20 + 768 * 2**10),
         cost_estimate=cost(2 * total * width * (width + 2 * half), 6 * 2**20),
         name="expand",
     )(place, mine, theirs, wide_high, wide_low, vecs)

time: 212 us -> 206 us (0.972)
  waiting for transfers between devices: 58.7 us -> 54 us
    ppermute x2 -> x1, waiting for transfers between devices: 12.5 us -> 7.61 us  [body(): diff_oth = lax.ppermute(give, ('xl', 'xh'), both_flip)]
    all_to_all x5, waiting for transfers between devices: 9.89 us -> 5.79 us  [exchange(): return lax.all_to_all(values, axes, 0, 0, tiled=True)]
    ppermute x21, waiting for transfers between devices: 31.8 us -> 35.3 us  [swap(): return lax.ppermute(values, axis, [(0, 1), (1, 0)])]
    ppermute x1, starting transfers between devices: 3.53 us -> 0.18 us  [body(): from_both = lax.ppermute(cut((1 - xh) * 2 + 1 - c), ('xh', 'c'), both_flip)]
    all_to_all x5, starting transfers between devices: 31 us -> 34 us  [exchange(): return lax.all_to_all(values, axes, 0, 0, tiled=True)]
    ppermute x21, starting transfers between devices: 22.1 us -> 25.1 us  [swap(): return lax.ppermute(values, axis, [(0, 1), (1, 0)])]
    ppermute x2 -> x1, starting transfers between devices: 4.55 us -> 2.77 us  [body(): diff_oth = lax.ppermute(give, ('xl', 'xh'), both_flip)]
    pallas_call x1 -> x2, Pallas kernels: 4.43 us -> 5.91 us  [pack(): pl.pallas_call(functools.partial(pack_kernel, len(tails)), out_shape=jax....]
  transfers between devices with their start and end apart: 31 -> 30, of which waited for: 16 -> 15; matrix products, arithmetic and copies ran while one was open for 11% -> 13% of each run, Pallas kernels for 17% -> 17%
where the time goes in v5:
time: 206 us
  starting transfers between devices  62.9 us (31%)
  waiting for transfers between devices  54 us (26%)
  Pallas kernels  42.7 us (21%)
  between operations  15.8 us (8%)
  local copies, waits for them, and re-layouts  14.5 us (7%)
  other arithmetic  10.7 us (5%)
  matrix products  4.91 us (2%)
    ppermute x21, waiting for transfers between devices, swap(): return lax.ppermute(values, axis, [(0, 1), (1, 0)])  35.3 us
    all_to_all x5, starting transfers between devices, exchange(): return lax.all_to_all(values, axes, 0, 0, tiled=True)  34 us
    ppermute x21, starting transfers between devices, swap(): return lax.ppermute(values, axis, [(0, 1), (1, 0)])  25.1 us
    pallas_call x1, Pallas kernels, density_of(): pl.pallas_call(functools.partial(density_kernel, counts), out_shape=jax.S...  23.3 us
    ppermute x1, waiting for transfers between devices, body(): diff_oth = lax.ppermute(give, ('xl', 'xh'), both_flip)  7.61 us
    pallas_call x2, Pallas kernels, pack(): pl.pallas_call(functools.partial(pack_kernel, len(tails)), out_shape=jax....  5.91 us
    all_to_all x5, waiting for transfers between devices, exchange(): return lax.all_to_all(values, axes, 0, 0, tiled=True)  5.79 us
    pallas_call x1, Pallas kernels, expand(): pl.pallas_call(expand_kernel, out_shape=(jax.ShapeDtypeStruct((total, wid...  5.2 us
  transfers between devices with their start and end apart: 30, of which 15 were waited for; matrix products, arithmetic and copies ran while one was open for 13% of the time, Pallas kernels for 17%

profile of v5, /device:TPU:1, one launch (start us, length us, event | category | flops | bytes accessed | tf_op | source)
XLA Modules:
  0.0 205.5 jit_solution(16637245452492750336)
XLA Ops:
  7.2 3.2 %pack_vectors.1 = bf16[16,96,512]{2,1,0:T(8,128)(2,1)} custom-call(s32[1]{0:T(128)S(6)} %sub.55.which, f32[64,16384]{1,0:T(8,128)} %orbs.5, bf16[8,16384]{1,0:T(8,128)(2,1)} %refs_0_.1, bf16[8,16384]{1,0:T(8,128)(2,1)} %refs_1_.1), custom_call_target="tpu_custom_call" | custom-call | bytes 3145728 | tf_op jit(solution)/shard_map/pack/pack_vectors/pallas_call | solution.py:245
  10.4 8.6 %all-to-all-start = ((bf16[16,96,512]{2,1,0:T(8,128)(2,1)}), bf16[16,96,512]{2,1,0:T(8,128)(2,1)S(1)}, u32[]{:S(2)}, u32[]{:S(2)}) async-start(bf16[16,96,512]{2,1,0:T(8,128)(2,1)} %pack_vectors.1), calls=%async_computation | async-start | bytes 3145728 | tf_op jit(solution)/shard_map/transpose_give/all_to_all | solution.py:31
  19.7 1.0 constant_dynamic-slice_fusion
  20.8 1.7 dynamic-slice_convert_fusion
  22.5 1.1 fusion.15
  24.4 3.0 %collective-permute-start.1 = (bf16[80,1024]{1,0:T(8,128)(2,1)S(1)}, bf16[80,1024]{1,0:T(8,128)(2,1)S(1)}, u32[]{:S(2)}, u32[]{:S(2)}) collective-permute-start(bf16[80,1024]{1,0:T(8,128)(2,1)S(1)} %get-tuple-element.131), channel_id=1, source_target_pairs={{0,2},{2,0},{1,3},{3,1},{4,6},{6,4},{5,7},{7,5},{8,10},{10,8},{9,1... | collective-permute-start | bytes 491528 | tf_op jit(solution)/shard_map/window_exchange/ppermute | solution.py:27
  27.6 4.1 %collective-permute-done.1 = bf16[80,1024]{1,0:T(8,128)(2,1)S(1)} collective-permute-done((bf16[80,1024]{1,0:T(8,128)(2,1)S(1)}, bf16[80,1024]{1,0:T(8,128)(2,1)S(1)}, u32[]{:S(2)}, u32[]{:S(2)}) %collective-permute-start.1) | collective-permute-done | bytes 163872 | tf_op jit(solution)/shard_map/window_exchange/ppermute | solution.py:27
  31.7 3.9 %collective-permute-done.2 = bf16[80,1024]{1,0:T(8,128)(2,1)S(1)} collective-permute-done((bf16[80,1024]{1,0:T(8,128)(2,1)S(1)}, bf16[80,1024]{1,0:T(8,128)(2,1)S(1)}, u32[]{:S(2)}, u32[]{:S(2)}) %collective-permute-start.2) | collective-permute-done | bytes 163872 | tf_op jit(solution)/shard_map/window_exchange/ppermute | solution.py:88
  36.0 1.2 collective-permute-start.3
  37.9 2.7 %pack_weights.1 = bf16[16,80,512]{2,1,0:T(8,128)(2,1)} custom-call(s32[1]{0:T(128)} %bitcast.2.which.side, f32[64,16384]{1,0:T(8,128)} %orbs.5, bf16[16,512]{1,0:T(8,128)(2,1)} %fusion.39.refs_0_), custom_call_target="tpu_custom_call" | custom-call | bytes 3145728 | tf_op jit(solution)/shard_map/window_exchange/pack_weights/pallas_call | solution.py:245
  40.6 1.2 collective-permute-done.3
  45.3 1.5 collective-permute-start.4
  46.8 1.3 slice.95
  48.2 6.9 %all-to-all-start.1 = ((bf16[16,80,512]{2,1,0:T(8,128)(2,1)}), bf16[16,80,512]{2,1,0:T(8,128)(2,1)S(1)}, u32[]{:S(2)}, u32[]{:S(2)}) async-start(bf16[16,80,512]{2,1,0:T(8,128)(2,1)} %pack_weights.1), calls=%async_computation.1 | async-start | bytes 2621440 | tf_op jit(solution)/shard_map/transpose_keep/all_to_all | solution.py:31
  55.1 2.8 %collective-permute-start.7 = (bf16[1024,512]{1,0:T(8,128)(2,1)S(1)}, bf16[1024,512]{1,0:T(8,128)(2,1)}, u32[]{:S(2)}, u32[]{:S(2)}) collective-permute-start(bf16[1024,512]{1,0:T(8,128)(2,1)S(1)} %bitcast.48), channel_id=1, source_target_pairs={{0,6},{2,4},{4,2},{6,0},{1,7},{3,5},{5,3},{7,1},{8,14},{10,12},{12... | collective-permute-start | bytes 3145736 | tf_op jit(solution)/shard_map/transpose_keep/ppermute | solution.py:108
  58.9 1.8 collective-permute-start.6
  60.7 1.3 select_bitcast_fusion.3
  62.1 1.4 fusion.3
  63.5 1.8 collective-permute-start.8
  65.4 1.1 pad_maximum_fusion.vecs
  67.7 1.3 subtract_convert_fusion
  69.1 1.7 convolution_add_fusion
  71.9 7.6 %collective-permute-done.7.refs_17_ = bf16[1024,512]{1,0:T(8,128)(2,1)} collective-permute-done((bf16[1024,512]{1,0:T(8,128)(2,1)S(1)}, bf16[1024,512]{1,0:T(8,128)(2,1)}, u32[]{:S(2)}, u32[]{:S(2)}) %collective-permute-start.7) | collective-permute-done | bytes 1048608 | tf_op jit(solution)/shard_map/transpose_keep/ppermute | solution.py:108
  79.6 1.2 copy-done.2
  80.8 3.5 %project.1 = (bf16[16,32,640]{2,1,0:T(8,128)(2,1)S(1)}, bf16[16,32,640]{2,1,0:T(8,128)(2,1)S(1)}) custom-call(s32[1]{0:T(128)} %bitcast.2.which.side, s32[2]{0:T(128)S(1)} %pad_add_fusion.place, bf16[1024,512]{1,0:T(8,128)(2,1)S(1)} %bitcast.50, bf16[16,80,512]{2,1,0:T(8,128)(2,1)S(1)} %all-to-all-done.1.keep, bf16[2,512,512]{2,1,0:T(8,128)(2,1)S(1)} %copy-done.2, ...), custom_call_target="tpu_custom_call" | custom-call | flops 1 | bytes 1 | tf_op jit(solution)/shard_map/project/project/pallas_call | solution.py:339
  84.3 2.6 %collective-permute-start.9 = (bf16[16,32,640]{2,1,0:T(8,128)(2,1)S(1)}, bf16[16,32,640]{2,1,0:T(8,128)(2,1)S(1)}, u32[]{:S(2)}, u32[]{:S(2)}) collective-permute-start(bf16[16,32,640]{2,1,0:T(8,128)(2,1)S(1)} %get-tuple-element.72), channel_id=1, source_target_pairs={{0,1},{1,0},{2,3},{3,2},{4,5},{5,4},{6,7},{7,6},{8,9},{9,8},{10,11... | collective-permute-start | bytes 1966088 | tf_op jit(solution)/shard_map/project/ppermute | solution.py:27
  87.6 1.0 slice.100
  88.7 2.0 collective-permute-start.10
  90.7 1.0 add_convert_fusion
  91.7 6.7 %all-to-all-start.2 = ((bf16[16,32,640]{2,1,0:T(8,128)(2,1)}), bf16[16,32,640]{2,1,0:T(8,128)(2,1)S(1)}, u32[]{:S(2)}, u32[]{:S(2)}) async-start(bf16[16,32,640]{2,1,0:T(8,128)(2,1)} %add_convert_fusion), calls=%async_computation.2 | async-start | bytes 1310720 | tf_op jit(solution)/shard_map/project/all_to_all | solution.py:31
  100.3 1.2 collective-permute-start.11
  102.2 14.7 %collective-permute-done.11 = bf16[16,16,128]{2,1,0:T(8,128)(2,1)S(1)} collective-permute-done((bf16[16,16,128]{2,1,0:T(8,128)(2,1)S(1)}, bf16[16,16,128]{2,1,0:T(8,128)(2,1)S(1)}, u32[]{:S(2)}, u32[]{:S(2)}) %collective-permute-start.11) | collective-permute-done | bytes 65568 | tf_op jit(solution)/shard_map/project/ppermute | solution.py:27
  116.9 1.5 all-to-all-done.2
  118.6 1.0 collective-permute-start.12
  120.1 1.8 collective-permute-start.14
  121.9 1.5 collective-permute-done.12
  125.1 5.0 %all-to-all-start.3 = ((bf16[16,32,640]{2,1,0:T(8,128)(2,1)}), bf16[16,32,640]{2,1,0:T(8,128)(2,1)S(1)}, u32[]{:S(2)}, u32[]{:S(2)}) async-start(bf16[16,32,640]{2,1,0:T(8,128)(2,1)} %broadcast_in_dim.6), calls=%async_computation.3 | async-start | bytes 1310720 | tf_op jit(solution)/shard_map/coefficients/all_to_all | solution.py:31
  133.5 8.9 %collective-permute-done.17.refs_12_ = bf16[512,512]{1,0:T(8,128)(2,1)S(1)} collective-permute-done((bf16[512,512]{1,0:T(8,128)(2,1)S(1)}, bf16[512,512]{1,0:T(8,128)(2,1)S(1)}, u32[]{:S(2)}, u32[]{:S(2)}) %collective-permute-start.17) | collective-permute-done | bytes 524320 | tf_op jit(solution)/shard_map/coefficients/ppermute | solution.py:27
  142.4 1.4 collective-permute-done.18.refs_8_
  143.8 3.4 %collective-permute-start.19 = (bf16[16,32,640]{2,1,0:T(8,128)(2,1)S(1)}, bf16[16,32,640]{2,1,0:T(8,128)(2,1)S(1)}, u32[]{:S(2)}, u32[]{:S(2)}) collective-permute-start(bf16[16,32,640]{2,1,0:T(8,128)(2,1)S(1)} %all-to-all-done.3.mine), channel_id=1, source_target_pairs={{0,1},{1,0},{2,3},{3,2},{4,5},{5,4},{6,7},{7,6},{8,9},{9,8},{10,11... | collective-permute-start | bytes 1966088 | tf_op jit(solution)/shard_map/coefficients/ppermute | solution.py:27
  147.4 1.6 collective-permute-done.19.theirs
  149.8 5.2 %expand.1 = (bf16[1024,512]{1,0:T(8,128)(2,1)}, bf16[512,512]{1,0:T(8,128)(2,1)}, bf16[16,64,1024]{2,1,0:T(8,128)(2,1)}) custom-call(s32[2]{0:T(128)} %copy-done.3, bf16[16,32,640]{2,1,0:T(8,128)(2,1)} %copy-done.6, bf16[16,32,640]{2,1,0:T(8,128)(2,1)} %copy-done.10, bf16[2,128,512]{2,1,0:T(8,128)(2,1)} %bitcast.60, bf16[2,128,512]{2,1,0:T(8,128)(2,1)} %bitcast.59, ...), custom_call_target="tpu_custom_call" | custom-call | flops 1610612736 | bytes 6291456 | tf_op jit(solution)/shard_map/coefficients/expand/pallas_call | solution.py:395
  155.0 6.7 %all-to-all-start.4 = ((bf16[16,64,1024]{2,1,0:T(8,128)(2,1)}), bf16[16,64,1024]{2,1,0:T(8,128)(2,1)}, u32[]{:S(2)}, u32[]{:S(2)}) async-start(bf16[16,64,1024]{2,1,0:T(8,128)(2,1)} %get-tuple-element.86), calls=%async_computation.4 | async-start | bytes 4194304 | tf_op jit(solution)/shard_map/transpose_out/all_to_all | solution.py:31
  163.0 1.2 collective-permute-done.22.refs_9_
  164.2 1.3 collective-permute-done.23.refs_15_
  166.3 23.3 %density.1 = f32[1024,4,512]{2,1,0:T(4,128)} custom-call(s32[2]{0:T(128)} %copy-done.3, bf16[16,160,1024]{2,1,0:T(8,128)(2,1)} %bitcast.61, bf16[16,160,1024]{2,1,0:T(8,128)(2,1)} %bitcast.62, bf16[1024,512]{1,0:T(8,128)(2,1)} %get-tuple-element.88.refs_0_, bf16[512,512]{1,0:T(8,128)(2,1)} %copy-done.13, bf16[512,512]{1,0:T(8,128)(2,1)} %collective-permute-done.21.refs_2_, ...), custom_call_target="tpu_custom_call" | custom-call | flops 12884901888 | bytes 29360128 | tf_op jit(solution)/shard_map/density/density/pallas_call | solution.py:489
  189.6 4.2 %all-to-all-done.4.update = bf16[16,64,1024]{2,1,0:T(8,128)(2,1)} async-done(((bf16[16,64,1024]{2,1,0:T(8,128)(2,1)}), bf16[16,64,1024]{2,1,0:T(8,128)(2,1)}, u32[]{:S(2)}, u32[]{:S(2)}) %all-to-all-start.4) | async-done | bytes 2097184 | tf_op jit(solution)/shard_map/transpose_out/all_to_all | solution.py:31
  193.9 4.8 %subtract_update.1 = f32[64,16384]{1,0:T(8,128)} custom-call(f32[64,16384]{1,0:T(8,128)} %orbs.5, bf16[16,64,1024]{2,1,0:T(8,128)(2,1)} %all-to-all-done.4.update), custom_call_target="tpu_custom_call" | custom-call | flops 1048576 | bytes 10485760 | tf_op jit(solution)/shard_map/subtract/subtract_update/pallas_call | solution.py:294
  (105 shorter events, 20.3 us)
Async XLA Ops:
  7.2 60.6 %copy-start = (f32[256,256]{1,0:T(8,128)S(1)}, f32[256,256]{1,0:T(8,128)}, u32[]{:S(2)}) copy-start(f32[256,256]{1,0:T(8,128)} %param.14) | copy-start | bytes 786436
  10.4 34.0 %all-to-all-start = ((bf16[16,96,512]{2,1,0:T(8,128)(2,1)}), bf16[16,96,512]{2,1,0:T(8,128)(2,1)S(1)}, u32[]{:S(2)}, u32[]{:S(2)}) async-start(bf16[16,96,512]{2,1,0:T(8,128)(2,1)} %pack_vectors.1), calls=%async_computation | async-start | bytes 3145728 | tf_op jit(solution)/shard_map/transpose_give/all_to_all | solution.py:31
  19.0 147.3 %all-gather.3.cloned.1.call-start = ((), (), s32[]{:S(2)}) async-start(), calls=%async_computation.5 | async-start | bytes 5570560 | tf_op jit(solution)/shard_map/window_exchange/all_gather | solution.py:100
  20.8 16.5 %copy-start.9 = (f32[64]{0:T(128)S(1)}, f32[64]{0:T(128)}, u32[]{:S(2)}) copy-start(f32[64]{0:T(128)} %param.15) | copy-start | bytes 772
  23.6 4.0 %collective-permute-start = (bf16[80,1024]{1,0:T(8,128)(2,1)S(1)}, bf16[80,1024]{1,0:T(8,128)(2,1)S(1)}, u32[]{:S(2)}, u32[]{:S(2)}) collective-permute-start(bf16[80,1024]{1,0:T(8,128)(2,1)S(1)} %get-tuple-element.132), channel_id=1, source_target_pairs={{0,1},{1,0},{2,3},{3,2},{4,5},{5,4},{6,7},{7,6},{8,9},{9,8},{10,11... | collective-permute-start | bytes 491528 | tf_op jit(solution)/shard_map/window_exchange/ppermute | solution.py:27
  24.4 7.4 %collective-permute-start.1 = (bf16[80,1024]{1,0:T(8,128)(2,1)S(1)}, bf16[80,1024]{1,0:T(8,128)(2,1)S(1)}, u32[]{:S(2)}, u32[]{:S(2)}) collective-permute-start(bf16[80,1024]{1,0:T(8,128)(2,1)S(1)} %get-tuple-element.131), channel_id=1, source_target_pairs={{0,2},{2,0},{1,3},{3,1},{4,6},{6,4},{5,7},{7,5},{8,10},{10,8},{9,1... | collective-permute-start | bytes 491528 | tf_op jit(solution)/shard_map/window_exchange/ppermute | solution.py:27
  27.4 8.3 %collective-permute-start.2 = (bf16[80,1024]{1,0:T(8,128)(2,1)S(1)}, bf16[80,1024]{1,0:T(8,128)(2,1)S(1)}, u32[]{:S(2)}, u32[]{:S(2)}) collective-permute-start(bf16[80,1024]{1,0:T(8,128)(2,1)S(1)} %get-tuple-element.130), channel_id=1, source_target_pairs={{0,3},{1,2},{2,1},{3,0},{4,7},{5,6},{6,5},{7,4},{8,11},{9,10},{10,... | collective-permute-start | bytes 491528 | tf_op jit(solution)/shard_map/window_exchange/ppermute | solution.py:88
  36.0 5.8 %collective-permute-start.3 = (bf16[80,1024]{1,0:T(8,128)(2,1)S(1)}, bf16[80,1024]{1,0:T(8,128)(2,1)}, u32[]{:S(2)}, u32[]{:S(2)}) collective-permute-start(bf16[80,1024]{1,0:T(8,128)(2,1)S(1)} %fusion.29), channel_id=1, source_target_pairs={{0,4},{4,0},{1,5},{5,1},{2,6},{6,2},{3,7},{7,3},{8,12},{12,8},{9,1... | collective-permute-start | bytes 491528 | tf_op jit(solution)/shard_map/window_exchange/ppermute | solution.py:27
  44.3 2.5 %copy-start.4 = (bf16[16,96,512]{2,1,0:T(8,128)(2,1)}, bf16[16,96,512]{2,1,0:T(8,128)(2,1)S(1)}, u32[]{:S(2)}) copy-start(bf16[16,96,512]{2,1,0:T(8,128)(2,1)S(1)} %all-to-all-done) | copy-start | bytes 4718596
  45.3 12.6 %collective-permute-start.4 = (bf16[16,16,512]{2,1,0:T(8,128)(2,1)}, bf16[16,16,512]{2,1,0:T(8,128)(2,1)}, u32[]{:S(2)}, u32[]{:S(2)}) collective-permute-start(bf16[16,16,512]{2,1,0:T(8,128)(2,1)} %get-tuple-element.115), channel_id=1, source_target_pairs={{0,4},{4,0},{1,5},{5,1},{2,6},{6,2},{3,7},{7,3},{8,12},{12,8},{9,1... | collective-permute-start | bytes 786440 | tf_op jit(solution)/shard_map/transpose_keep/ppermute | solution.py:27
  46.7 11.3 %collective-permute-start.5 = (bf16[16,16,512]{2,1,0:T(8,128)(2,1)}, bf16[16,16,512]{2,1,0:T(8,128)(2,1)}, u32[]{:S(2)}, u32[]{:S(2)}) collective-permute-start(bf16[16,16,512]{2,1,0:T(8,128)(2,1)} %get-tuple-element.114), channel_id=1, source_target_pairs={{0,4},{4,0},{1,5},{5,1},{2,6},{6,2},{3,7},{7,3},{8,12},{12,8},{9,1... | collective-permute-start | bytes 786440 | tf_op jit(solution)/shard_map/transpose_keep/ppermute | solution.py:27
  46.8 32.7 %copy-start.3 = (s32[2]{0:T(128)}, s32[2]{0:T(128)S(1)}, u32[]{:S(2)}) copy-start(s32[2]{0:T(128)S(1)} %pad_add_fusion.place) | copy-start | bytes 28
  48.2 31.4 %all-to-all-start.1 = ((bf16[16,80,512]{2,1,0:T(8,128)(2,1)}), bf16[16,80,512]{2,1,0:T(8,128)(2,1)S(1)}, u32[]{:S(2)}, u32[]{:S(2)}) async-start(bf16[16,80,512]{2,1,0:T(8,128)(2,1)} %pack_weights.1), calls=%async_computation.1 | async-start | bytes 2621440 | tf_op jit(solution)/shard_map/transpose_keep/all_to_all | solution.py:31
  55.1 24.5 %collective-permute-start.7 = (bf16[1024,512]{1,0:T(8,128)(2,1)S(1)}, bf16[1024,512]{1,0:T(8,128)(2,1)}, u32[]{:S(2)}, u32[]{:S(2)}) collective-permute-start(bf16[1024,512]{1,0:T(8,128)(2,1)S(1)} %bitcast.48), channel_id=1, source_target_pairs={{0,6},{2,4},{4,2},{6,0},{1,7},{3,5},{5,3},{7,1},{8,14},{10,12},{12... | collective-permute-start | bytes 3145736 | tf_op jit(solution)/shard_map/transpose_keep/ppermute | solution.py:108
  58.9 12.3 %collective-permute-start.6 = (bf16[512,512]{1,0:T(8,128)(2,1)S(1)}, bf16[512,512]{1,0:T(8,128)(2,1)S(1)}, u32[]{:S(2)}, u32[]{:S(2)}) collective-permute-start(bf16[512,512]{1,0:T(8,128)(2,1)S(1)} %get-tuple-element.119), channel_id=1, source_target_pairs={{0,4},{4,0},{1,5},{5,1},{2,6},{6,2},{3,7},{7,3},{8,12},{12,8},{9,1... | collective-permute-start | bytes 1572872 | tf_op jit(solution)/shard_map/transpose_keep/ppermute | solution.py:27
  63.5 16.0 %collective-permute-start.8 = (bf16[512,512]{1,0:T(8,128)(2,1)}, bf16[512,512]{1,0:T(8,128)(2,1)}, u32[]{:S(2)}, u32[]{:S(2)}) collective-permute-start(bf16[512,512]{1,0:T(8,128)(2,1)} %get-tuple-element.92.refs_6_), channel_id=1, source_target_pairs={{0,1},{1,0},{2,3},{3,2},{4,5},{5,4},{6,7},{7,6},{8,9},{9,8},{10,11... | collective-permute-start | bytes 1572872 | tf_op jit(solution)/shard_map/transpose_keep/ppermute | solution.py:27
  65.4 1.1 copy-start.8
  71.2 0.8 copy-start.11
  79.6 1.2 copy-start.2
  84.3 6.4 %collective-permute-start.9 = (bf16[16,32,640]{2,1,0:T(8,128)(2,1)S(1)}, bf16[16,32,640]{2,1,0:T(8,128)(2,1)S(1)}, u32[]{:S(2)}, u32[]{:S(2)}) collective-permute-start(bf16[16,32,640]{2,1,0:T(8,128)(2,1)S(1)} %get-tuple-element.72), channel_id=1, source_target_pairs={{0,1},{1,0},{2,3},{3,2},{4,5},{5,4},{6,7},{7,6},{8,9},{9,8},{10,11... | collective-permute-start | bytes 1966088 | tf_op jit(solution)/shard_map/project/ppermute | solution.py:27
  88.7 28.3 %collective-permute-start.10 = (bf16[1024,512]{1,0:T(8,128)(2,1)}, bf16[1024,512]{1,0:T(8,128)(2,1)}, u32[]{:S(2)}, u32[]{:S(2)}) collective-permute-start(bf16[1024,512]{1,0:T(8,128)(2,1)} %bitcast.21.refs_10_), channel_id=1, source_target_pairs={{0,2},{2,0},{1,3},{3,1},{4,6},{6,4},{5,7},{7,5},{8,10},{10,8},{9,1... | collective-permute-start | bytes 3145736 | tf_op jit(solution)/shard_map/project/ppermute | solution.py:27
  91.7 31.8 %copy-start.5 = (f32[512,512]{1,0:T(8,128)S(1)}, f32[512,512]{1,0:T(8,128)}, u32[]{:S(2)}) copy-start(f32[512,512]{1,0:T(8,128)} %convolution_add_fusion) | copy-start | bytes 3145732
  91.7 26.8 %all-to-all-start.2 = ((bf16[16,32,640]{2,1,0:T(8,128)(2,1)}), bf16[16,32,640]{2,1,0:T(8,128)(2,1)S(1)}, u32[]{:S(2)}, u32[]{:S(2)}) async-start(bf16[16,32,640]{2,1,0:T(8,128)(2,1)} %add_convert_fusion), calls=%async_computation.2 | async-start | bytes 1310720 | tf_op jit(solution)/shard_map/project/all_to_all | solution.py:31
  99.7 33.8 %collective-permute-start.13 = (bf16[1024,512]{1,0:T(8,128)(2,1)}, bf16[1024,512]{1,0:T(8,128)(2,1)}, u32[]{:S(2)}, u32[]{:S(2)}) collective-permute-start(bf16[1024,512]{1,0:T(8,128)(2,1)} %bitcast.21.refs_10_), channel_id=1, source_target_pairs={{0,1},{1,0},{2,3},{3,2},{4,5},{5,4},{6,7},{7,6},{8,9},{9,8},{10,11... | collective-permute-start | bytes 3145736 | tf_op jit(solution)/shard_map/coefficients/ppermute | solution.py:27
  100.3 16.6 %collective-permute-start.11 = (bf16[16,16,128]{2,1,0:T(8,128)(2,1)S(1)}, bf16[16,16,128]{2,1,0:T(8,128)(2,1)S(1)}, u32[]{:S(2)}, u32[]{:S(2)}) collective-permute-start(bf16[16,16,128]{2,1,0:T(8,128)(2,1)S(1)} %slice.101), channel_id=1, source_target_pairs={{0,4},{4,0},{1,5},{5,1},{2,6},{6,2},{3,7},{7,3},{8,12},{12,8},{9,1... | collective-permute-start | bytes 196616 | tf_op jit(solution)/shard_map/project/ppermute | solution.py:27
  101.6 29.7 %collective-permute-start.15 = (bf16[512,512]{1,0:T(8,128)(2,1)}, bf16[512,512]{1,0:T(8,128)(2,1)}, u32[]{:S(2)}, u32[]{:S(2)}) collective-permute-start(bf16[512,512]{1,0:T(8,128)(2,1)} %copy-done.11), channel_id=1, source_target_pairs={{0,1},{1,0},{2,3},{3,2},{4,5},{5,4},{6,7},{7,6},{8,9},{9,8},{10,11... | collective-permute-start | bytes 1572872 | tf_op jit(solution)/shard_map/coefficients/ppermute | solution.py:27
  102.0 31.5 %collective-permute-start.16 = (bf16[1024,512]{1,0:T(8,128)(2,1)}, bf16[1024,512]{1,0:T(8,128)(2,1)}, u32[]{:S(2)}, u32[]{:S(2)}) collective-permute-start(bf16[1024,512]{1,0:T(8,128)(2,1)} %collective-permute-done.7.refs_17_), channel_id=1, source_target_pairs={{0,1},{1,0},{2,3},{3,2},{4,5},{5,4},{6,7},{7,6},{8,9},{9,8},{10,11... | collective-permute-start | bytes 3145736 | tf_op jit(solution)/shard_map/coefficients/ppermute | solution.py:27
  118.6 4.9 %collective-permute-start.12 = (f32[32,640]{1,0:T(8,128)S(1)}, f32[32,640]{1,0:T(8,128)S(1)}, u32[]{:S(2)}, u32[]{:S(2)}) collective-permute-start(f32[32,640]{1,0:T(8,128)S(1)} %convert_reduce_fusion), channel_id=1, source_target_pairs={{0,2},{2,0},{1,3},{3,1},{4,6},{6,4},{5,7},{7,5},{8,10},{10,8},{9,1... | collective-permute-start | bytes 245768 | tf_op jit(solution)/shard_map/project/ppermute | solution.py:27
  120.1 23.7 %collective-permute-start.14 = (bf16[1024,512]{1,0:T(8,128)(2,1)}, bf16[1024,512]{1,0:T(8,128)(2,1)}, u32[]{:S(2)}, u32[]{:S(2)}) collective-permute-start(bf16[1024,512]{1,0:T(8,128)(2,1)} %collective-permute-done.10.refs_16_), channel_id=1, source_target_pairs={{0,1},{1,0},{2,3},{3,2},{4,5},{5,4},{6,7},{7,6},{8,9},{9,8},{10,11... | collective-permute-start | bytes 3145736 | tf_op jit(solution)/shard_map/coefficients/ppermute | solution.py:27
  124.2 6.8 %copy-start.7 = (bf16[512,512]{1,0:T(8,128)(2,1)S(1)}, bf16[512,512]{1,0:T(8,128)(2,1)}, u32[]{:S(2)}) copy-start(bf16[512,512]{1,0:T(8,128)(2,1)} %get-tuple-element.79) | copy-start | bytes 1572868
  125.1 18.7 %all-to-all-start.3 = ((bf16[16,32,640]{2,1,0:T(8,128)(2,1)}), bf16[16,32,640]{2,1,0:T(8,128)(2,1)S(1)}, u32[]{:S(2)}, u32[]{:S(2)}) async-start(bf16[16,32,640]{2,1,0:T(8,128)(2,1)} %broadcast_in_dim.6), calls=%async_computation.3 | async-start | bytes 1310720 | tf_op jit(solution)/shard_map/coefficients/all_to_all | solution.py:31
  131.0 11.4 %collective-permute-start.17 = (bf16[512,512]{1,0:T(8,128)(2,1)S(1)}, bf16[512,512]{1,0:T(8,128)(2,1)S(1)}, u32[]{:S(2)}, u32[]{:S(2)}) collective-permute-start(bf16[512,512]{1,0:T(8,128)(2,1)S(1)} %copy-done.7), channel_id=1, source_target_pairs={{0,4},{4,0},{1,5},{5,1},{2,6},{6,2},{3,7},{7,3},{8,12},{12,8},{9,1... | collective-permute-start | bytes 1572872 | tf_op jit(solution)/shard_map/coefficients/ppermute | solution.py:27
  131.3 12.5 %collective-permute-start.18 = (bf16[512,512]{1,0:T(8,128)(2,1)}, bf16[512,512]{1,0:T(8,128)(2,1)}, u32[]{:S(2)}, u32[]{:S(2)}) collective-permute-start(bf16[512,512]{1,0:T(8,128)(2,1)} %get-tuple-element.80), channel_id=1, source_target_pairs={{0,6},{2,4},{4,2},{6,0},{1,7},{3,5},{5,3},{7,1},{8,14},{10,12},{12... | collective-permute-start | bytes 1572872 | tf_op jit(solution)/shard_map/coefficients/ppermute | solution.py:164
  142.4 20.0 %copy-start.12 = (bf16[512,512]{1,0:T(8,128)(2,1)}, bf16[512,512]{1,0:T(8,128)(2,1)S(1)}, u32[]{:S(2)}) copy-start(bf16[512,512]{1,0:T(8,128)(2,1)S(1)} %collective-permute-done.17.refs_12_) | copy-start | bytes 1572868
  143.8 5.2 %copy-start.6 = (bf16[16,32,640]{2,1,0:T(8,128)(2,1)}, bf16[16,32,640]{2,1,0:T(8,128)(2,1)S(1)}, u32[]{:S(2)}) copy-start(bf16[16,32,640]{2,1,0:T(8,128)(2,1)S(1)} %all-to-all-done.3.mine) | copy-start | bytes 1966084
  143.8 5.1 %collective-permute-start.19 = (bf16[16,32,640]{2,1,0:T(8,128)(2,1)S(1)}, bf16[16,32,640]{2,1,0:T(8,128)(2,1)S(1)}, u32[]{:S(2)}, u32[]{:S(2)}) collective-permute-start(bf16[16,32,640]{2,1,0:T(8,128)(2,1)S(1)} %all-to-all-done.3.mine), channel_id=1, source_target_pairs={{0,1},{1,0},{2,3},{3,2},{4,5},{5,4},{6,7},{7,6},{8,9},{9,8},{10,11... | collective-permute-start | bytes 1966088 | tf_op jit(solution)/shard_map/coefficients/ppermute | solution.py:27
  147.3 15.3 %collective-permute-start.20 = (bf16[512,512]{1,0:T(8,128)(2,1)S(1)}, bf16[512,512]{1,0:T(8,128)(2,1)S(1)}, u32[]{:S(2)}, u32[]{:S(2)}) collective-permute-start(bf16[512,512]{1,0:T(8,128)(2,1)S(1)} %bitcast.57), channel_id=1, source_target_pairs={{0,4},{4,0},{1,5},{5,1},{2,6},{6,2},{3,7},{7,3},{8,12},{12,8},{9,1... | collective-permute-start | bytes 1572872 | tf_op jit(solution)/shard_map/coefficients/ppermute | solution.py:27
  149.0 0.8 copy-start.10
  155.0 38.9 %all-to-all-start.4 = ((bf16[16,64,1024]{2,1,0:T(8,128)(2,1)}), bf16[16,64,1024]{2,1,0:T(8,128)(2,1)}, u32[]{:S(2)}, u32[]{:S(2)}) async-start(bf16[16,64,1024]{2,1,0:T(8,128)(2,1)} %get-tuple-element.86), calls=%async_computation.4 | async-start | bytes 4194304 | tf_op jit(solution)/shard_map/transpose_out/all_to_all | solution.py:31
  161.7 2.5 %collective-permute-start.22 = (bf16[512,512]{1,0:T(8,128)(2,1)}, bf16[512,512]{1,0:T(8,128)(2,1)S(1)}, u32[]{:S(2)}, u32[]{:S(2)}) collective-permute-start(bf16[512,512]{1,0:T(8,128)(2,1)} %collective-permute-done.18.refs_8_), channel_id=1, source_target_pairs={{0,1},{1,0},{2,3},{3,2},{4,5},{5,4},{6,7},{7,6},{8,9},{9,8},{10,11... | collective-permute-start | bytes 1572872 | tf_op jit(solution)/shard_map/density/ppermute | solution.py:27
  162.5 3.0 %collective-permute-start.23 = (bf16[512,512]{1,0:T(8,128)(2,1)S(1)}, bf16[512,512]{1,0:T(8,128)(2,1)S(1)}, u32[]{:S(2)}, u32[]{:S(2)}) collective-permute-start(bf16[512,512]{1,0:T(8,128)(2,1)S(1)} %collective-permute-done.17.refs_12_), channel_id=1, source_target_pairs={{0,1},{1,0},{2,3},{3,2},{4,5},{5,4},{6,7},{7,6},{8,9},{9,8},{10,11... | collective-permute-start | bytes 1572872 | tf_op jit(solution)/shard_map/density/ppermute | solution.py:27
  162.6 3.8 %copy-start.13 = (bf16[512,512]{1,0:T(8,128)(2,1)}, bf16[512,512]{1,0:T(8,128)(2,1)S(1)}, u32[]{:S(2)}) copy-start(bf16[512,512]{1,0:T(8,128)(2,1)S(1)} %collective-permute-done.20.refs_1_) | copy-start | bytes 1572868
  162.6 3.7 %collective-permute-start.21 = (bf16[512,512]{1,0:T(8,128)(2,1)S(1)}, bf16[512,512]{1,0:T(8,128)(2,1)}, u32[]{:S(2)}, u32[]{:S(2)}) collective-permute-start(bf16[512,512]{1,0:T(8,128)(2,1)S(1)} %collective-permute-done.20.refs_1_), channel_id=1, source_target_pairs={{0,1},{1,0},{2,3},{3,2},{4,5},{5,4},{6,7},{7,6},{8,9},{9,8},{10,11... | collective-permute-start | bytes 1572872 | tf_op jit(solution)/shard_map/density/ppermute | solution.py:27
  164.2 2.1 %copy-start.14 = (bf16[512,512]{1,0:T(8,128)(2,1)}, bf16[512,512]{1,0:T(8,128)(2,1)S(1)}, u32[]{:S(2)}) copy-start(bf16[512,512]{1,0:T(8,128)(2,1)S(1)} %collective-permute-done.22.refs_9_) | copy-start | bytes 1572868
  165.5 0.8 copy-start.15
  193.9 4.8 %copy-start.1 = (f32[256,256]{1,0:T(8,128)S(1)}, f32[256,256]{1,0:T(8,128)}, u32[]{:S(2)}) copy-start(f32[256,256]{1,0:T(8,128)} %param.14) | copy-start | bytes 786436
Sparse Core Ops, SparseCore 0:
  44.5 76.3 all-gather.2

commit v6 on v5

--- a/solution.py
+++ b/solution.py
@@ -97,7 +97,6 @@
         window = jnp.concatenate([mine[:n_orbs], mine_x[:n_orbs], win_vecs], axis=0)
         keep_p = pack(side_xl, eigvecs, chunk, (extra,))
         got, keep_p, window = tie(got, keep_p, window)
-        window = lax.all_gather(window, ZY, axis=0)
 
     with jax.named_scope("transpose_keep"):
         kept = exchange(keep_p, ZY)
@@ -105,8 +104,11 @@
         vec_own = [got[:, n_orbs + i * n_all : n_orbs + (i + 1) * n_all] for i in range(2)]
         vec_oth = [swap(value, "xl") for value in vec_own]
         quarter = 8 * n_orbs
-        diff_oth = lax.ppermute(give, ("xl", "xh"), both_flip)
-        factor_one, factor_two, give, *vec_oth = tie(factor_one, factor_two, give, *vec_oth)
+        diff_a = lax.ppermute(give[:quarter], ("xl", "xh"), both_flip)
+        diff_b = lax.ppermute(give[quarter:], ("xl", "xh"), both_flip)
+        factor_one, factor_two, give, diff_a, *vec_oth = tie(
+            factor_one, factor_two, give, diff_a, *vec_oth
+        )
         give_a, give_b = give[:quarter], give[quarter:]
         same_a = swap(give_a, "xl")
 
@@ -128,18 +130,19 @@
         wide_high = wide.astype(bf16)
         wide_low = (wide - wide_high.astype(jnp.float32)).astype(bf16)
         vec_keep_c = swap(vec_keep, "c")
-        kept, same_a, diff_oth, vecs, vec_two, vec_keep = tie(
-            kept, same_a, diff_oth, vecs, vec_two, vec_keep
+        kept, same_a, diff_b, vecs, vec_two, vec_keep, vec_keep_c, *ready = tie(
+            kept, same_a, diff_b, vecs, vec_two, vec_keep, vec_keep_c, window, factor, wide_high,
+            wide_low,
         )
-        kept, vec_keep_c = tie(kept, vec_keep_c)
-        kept, factor, wide_high, wide_low = tie(kept, factor, wide_high, wide_low)
-        keep = kept[:, :n_orbs].reshape(16 * n_orbs, half)
+        window, factor, wide_high, wide_low = ready
+        window = lax.all_gather(window, ZY, axis=0)
         occ_own = kept[:, n_orbs:, :128]
 
     with jax.named_scope("project"):
+        occ_oth = swap(occ_own, "xl")
+        parts, parts_c, keep = project(side_xl, place, give, kept, vecs, vec_two)
+        keep = keep.reshape(16 * n_orbs, half)
         cross = swap(keep, "xh")
-        occ_oth = swap(occ_own, "xl")
-        parts, parts_c = project(side_xl, place, give, kept, vecs, vec_two)
         parts = parts.astype(jnp.float32) + swap(parts_c, "c").astype(jnp.float32)
         summed = exchange(parts.astype(bf16), ZY)
         summed, cross, occ_oth = tie(summed, cross, occ_oth)
@@ -162,9 +165,11 @@
         weight_own, weight_oth = weight_of(occ_own, xl), weight_of(occ_oth, 1 - xl)
         same_b = swap(give_b, "xl")
         vec_keep_x = lax.ppermute(vec_give, ("xl", "xh"), both_flip)
-        keep_c, cross_c, same_a_c, diff_c = (swap(v, "c") for v in (keep, cross, same_a, diff_oth))
-        every, keep_c, cross_c, same_a_c, diff_c, same_b, vec_keep_x = tie(
-            every, keep_c, cross_c, same_a_c, diff_c, same_b, vec_keep_x
+        keep_c, cross_c, same_a_c, diff_a_c, diff_b_c = (
+            swap(v, "c") for v in (keep, cross, same_a, diff_a, diff_b)
+        )
+        every, keep_c, cross_c, same_a_c, diff_a_c, diff_b_c, same_b, vec_keep_x = tie(
+            every, keep_c, cross_c, same_a_c, diff_a_c, diff_b_c, same_b, vec_keep_x
         )
         every, weight_own, weight_oth = tie(every, weight_own, weight_oth)
         every_c = swap(every, "c")
@@ -188,8 +193,8 @@
             [
                 ([keep], [same_a, same_b]),
                 ([keep_c], [same_a_c, same_b_c]),
-                ([cross], [diff_oth]),
-                ([cross_c], [diff_c]),
+                ([cross], [diff_a, diff_b]),
+                ([cross_c], [diff_a_c, diff_b_c]),
             ],
         )
 
@@ -307,11 +312,12 @@
     )(orbs, update)
 
 
-def project_kernel(side, place, give, keep, vecs, vec_two, mine, theirs, blocks_v, sems):
+def project_kernel(side, place, give, keep, vecs, vec_two, mine, theirs, kept, blocks_v, sems):
     blocks, n_own, lanes = mine.shape
     width = vecs.shape[1]
     n_rows, n_two = blocks * n_own, lanes - width
-    stores = []
+    stores = [pltpu.make_async_copy(keep.at[:, pl.ds(0, 2 * n_own)], kept, sems.at[2])]
+    stores[0].start()
     for i, (out, half) in enumerate(((theirs, 1 - place[1]), (mine, place[1]))):
         at = pl.ds(pl.multiple_of(half * n_rows, n_rows), n_rows)
         proj = dot(give[at, :], vecs[1 - side[0]], ((1,), (1,)))
@@ -338,12 +344,16 @@
     shape = (16, give.shape[0] // 32, vecs.shape[1] + vec_two.shape[1] // 2)
     return pl.pallas_call(
         project_kernel,
-        out_shape=(jax.ShapeDtypeStruct(shape, jnp.bfloat16),) * 2,
+        out_shape=(
+            jax.ShapeDtypeStruct(shape, jnp.bfloat16),
+            jax.ShapeDtypeStruct(shape, jnp.bfloat16),
+            jax.ShapeDtypeStruct((16, 2 * shape[1], give.shape[1]), jnp.bfloat16),
+        ),
         in_specs=specs_of(2, 4),
-        out_specs=(pl.BlockSpec(memory_space=pltpu.HBM),) * 2,
+        out_specs=(pl.BlockSpec(memory_space=pltpu.HBM),) * 3,
         scratch_shapes=[
             pltpu.VMEM((2,) + shape, jnp.bfloat16),
-            pltpu.SemaphoreType.DMA((2,)),
+            pltpu.SemaphoreType.DMA((3,)),
         ],
         compiler_params=pltpu.CompilerParams(vmem_limit_bytes=20 * 2**20),
         cost_estimate=cost(1, 1),

time: 206 us -> 205 us (level)
  starting transfers between devices: 62.9 us -> 59.5 us
    ppermute x1 -> x2, waiting for transfers between devices: 7.61 us -> 0.01 us  [the longest x1 0.01 us: body(): diff_a = lax.ppermute(give[:quarter], ('xl', 'xh'), both_flip)]
    all_to_all x5, waiting for transfers between devices: 5.79 us -> 11.4 us  [exchange(): return lax.all_to_all(values, axes, 0, 0, tiled=True)]
    all_to_all x5, starting transfers between devices: 34 us -> 28.8 us  [exchange(): return lax.all_to_all(values, axes, 0, 0, tiled=True)]
    ppermute x21 -> x22, waiting for transfers between devices: 35.3 us -> 38.7 us  [swap(): return lax.ppermute(values, axis, [(0, 1), (1, 0)])]
    ppermute x21 -> x22, starting transfers between devices: 25.1 us -> 25.6 us  [swap(): return lax.ppermute(values, axis, [(0, 1), (1, 0)])]
  transfers between devices with their start and end apart: 30 -> 32, of which waited for: 15 -> 18; matrix products, arithmetic and copies ran while one was open for 13% -> 12% of each run, Pallas kernels for 17% -> 17%
where the time goes in v6:
time: 205 us; the launch traced here: 204 us
  starting transfers between devices  59.5 us (29%)
  waiting for transfers between devices  55.8 us (27%)
  Pallas kernels  42.7 us (21%)
  between operations  15.8 us (8%)
  local copies, waits for them, and re-layouts  14.5 us (7%)
  other arithmetic  11.2 us (5%)
  matrix products  4.9 us (2%)
    ppermute x22, waiting for transfers between devices, swap(): return lax.ppermute(values, axis, [(0, 1), (1, 0)])  38.7 us
    all_to_all x5, starting transfers between devices, exchange(): return lax.all_to_all(values, axes, 0, 0, tiled=True)  28.8 us
    ppermute x22, starting transfers between devices, swap(): return lax.ppermute(values, axis, [(0, 1), (1, 0)])  25.6 us
    pallas_call x1, Pallas kernels, density_of(): pl.pallas_call(functools.partial(density_kernel, counts), out_shape=jax.S...  23.3 us
    all_to_all x5, waiting for transfers between devices, exchange(): return lax.all_to_all(values, axes, 0, 0, tiled=True)  11.4 us
    pallas_call x2, Pallas kernels, pack(): pl.pallas_call(functools.partial(pack_kernel, len(tails)), out_shape=jax....  5.91 us
    pallas_call x1, Pallas kernels, expand(): pl.pallas_call(expand_kernel, out_shape=(jax.ShapeDtypeStruct((total, wid...  5.2 us
    dot_general x5, matrix products, dot(): lax.dot_general(left, right, (dims, ((), ())), preferred_element_type=jnp...  4.9 us
  transfers between devices with their start and end apart: 32, of which 18 were waited for; matrix products, arithmetic and copies ran while one was open for 12% of the time, Pallas kernels for 17%

profile of v6, /device:TPU:1, one launch (start us, length us, event | category | flops | bytes accessed | tf_op | source)
XLA Modules:
  0.0 204.5 jit_solution(274057051799374004)
XLA Ops:
  7.2 3.2 %pack_vectors.1 = bf16[16,96,512]{2,1,0:T(8,128)(2,1)} custom-call(s32[1]{0:T(128)S(6)} %sub.55.which, f32[64,16384]{1,0:T(8,128)} %orbs.5, bf16[8,16384]{1,0:T(8,128)(2,1)} %refs_0_.1, bf16[8,16384]{1,0:T(8,128)(2,1)} %refs_1_.1), custom_call_target="tpu_custom_call" | custom-call | bytes 3145728 | tf_op jit(solution)/shard_map/pack/pack_vectors/pallas_call | solution.py:250
  10.4 8.6 %all-to-all-start = ((bf16[16,96,512]{2,1,0:T(8,128)(2,1)}), bf16[16,96,512]{2,1,0:T(8,128)(2,1)S(1)}, u32[]{:S(2)}, u32[]{:S(2)}) async-start(bf16[16,96,512]{2,1,0:T(8,128)(2,1)} %pack_vectors.1), calls=%async_computation | async-start | bytes 3145728 | tf_op jit(solution)/shard_map/transpose_give/all_to_all | solution.py:31
  19.7 1.0 constant_dynamic-slice_fusion
  20.7 1.5 dynamic-slice_convert_fusion
  22.2 1.1 fusion.15
  23.3 1.2 collective-permute-start
  24.4 2.9 %collective-permute-start.1 = (bf16[80,1024]{1,0:T(8,128)(2,1)S(1)}, bf16[80,1024]{1,0:T(8,128)(2,1)S(1)}, u32[]{:S(2)}, u32[]{:S(2)}) collective-permute-start(bf16[80,1024]{1,0:T(8,128)(2,1)S(1)} %get-tuple-element.137), channel_id=1, source_target_pairs={{0,2},{2,0},{1,3},{3,1},{4,6},{6,4},{5,7},{7,5},{8,10},{10,8},{9,1... | collective-permute-start | bytes 491528 | tf_op jit(solution)/shard_map/window_exchange/ppermute | solution.py:27
  27.7 4.0 %collective-permute-done.1 = bf16[80,1024]{1,0:T(8,128)(2,1)S(1)} collective-permute-done((bf16[80,1024]{1,0:T(8,128)(2,1)S(1)}, bf16[80,1024]{1,0:T(8,128)(2,1)S(1)}, u32[]{:S(2)}, u32[]{:S(2)}) %collective-permute-start.1) | collective-permute-done | bytes 163872 | tf_op jit(solution)/shard_map/window_exchange/ppermute | solution.py:27
  31.7 4.0 %collective-permute-done.2 = bf16[80,1024]{1,0:T(8,128)(2,1)S(1)} collective-permute-done((bf16[80,1024]{1,0:T(8,128)(2,1)S(1)}, bf16[80,1024]{1,0:T(8,128)(2,1)S(1)}, u32[]{:S(2)}, u32[]{:S(2)}) %collective-permute-start.2) | collective-permute-done | bytes 163872 | tf_op jit(solution)/shard_map/window_exchange/ppermute | solution.py:88
  36.1 1.3 collective-permute-start.3
  38.0 2.7 %pack_weights.1 = bf16[16,80,512]{2,1,0:T(8,128)(2,1)} custom-call(s32[1]{0:T(128)} %bitcast.2.which.side, f32[64,16384]{1,0:T(8,128)} %orbs.5, bf16[16,512]{1,0:T(8,128)(2,1)} %fusion.39.refs_0_), custom_call_target="tpu_custom_call" | custom-call | bytes 3145728 | tf_op jit(solution)/shard_map/window_exchange/pack_weights/pallas_call | solution.py:250
  40.7 1.3 collective-permute-done.3
  42.0 0.9 slice.129
  44.5 1.2 fusion.48
  45.7 2.8 %collective-permute-start.4 = (bf16[512,512]{1,0:T(8,128)(2,1)}, bf16[512,512]{1,0:T(8,128)(2,1)}, u32[]{:S(2)}, u32[]{:S(2)}) collective-permute-start(bf16[512,512]{1,0:T(8,128)(2,1)} %bitcast.11), channel_id=1, source_target_pairs={{0,6},{2,4},{4,2},{6,0},{1,7},{3,5},{5,3},{7,1},{8,14},{10,12},{12... | collective-permute-start | bytes 1572872 | tf_op jit(solution)/shard_map/transpose_keep/ppermute | solution.py:107
  49.3 1.5 collective-permute-start.6
  50.8 1.3 slice.106
  52.1 6.7 %all-to-all-start.1 = ((bf16[16,80,512]{2,1,0:T(8,128)(2,1)}), bf16[16,80,512]{2,1,0:T(8,128)(2,1)S(1)}, u32[]{:S(2)}, u32[]{:S(2)}) async-start(bf16[16,80,512]{2,1,0:T(8,128)(2,1)} %pack_weights.1), calls=%async_computation.1 | async-start | bytes 2621440 | tf_op jit(solution)/shard_map/transpose_keep/all_to_all | solution.py:31
  58.9 3.1 %collective-permute-done.6 = bf16[16,16,512]{2,1,0:T(8,128)(2,1)S(1)} collective-permute-done((bf16[16,16,512]{2,1,0:T(8,128)(2,1)}, bf16[16,16,512]{2,1,0:T(8,128)(2,1)S(1)}, u32[]{:S(2)}, u32[]{:S(2)}) %collective-permute-start.6) | collective-permute-done | bytes 262176 | tf_op jit(solution)/shard_map/transpose_keep/ppermute | solution.py:27
  63.0 1.1 select_bitcast_fusion.3
  64.3 1.2 fusion.3
  65.5 2.1 %collective-permute-start.9 = (bf16[512,512]{1,0:T(8,128)(2,1)S(1)}, bf16[512,512]{1,0:T(8,128)(2,1)}, u32[]{:S(2)}, u32[]{:S(2)}) collective-permute-start(bf16[512,512]{1,0:T(8,128)(2,1)S(1)} %get-tuple-element.95.refs_6_), channel_id=1, source_target_pairs={{0,1},{1,0},{2,3},{3,2},{4,5},{5,4},{6,7},{7,6},{8,9},{9,8},{10,11... | collective-permute-start | bytes 1572872 | tf_op jit(solution)/shard_map/transpose_keep/ppermute | solution.py:27
  68.5 1.1 pad_maximum_fusion.vecs
  70.8 1.3 subtract_convert_fusion
  72.1 1.7 convolution_add_fusion
  75.4 1.2 all-to-all-done.1.keep
  76.7 1.2 copy-done.2
  77.9 3.5 %project.1 = (bf16[16,32,640]{2,1,0:T(8,128)(2,1)S(1)}, bf16[16,32,640]{2,1,0:T(8,128)(2,1)S(1)}, bf16[16,64,512]{2,1,0:T(8,128)(2,1)}) custom-call(s32[1]{0:T(128)} %bitcast.2.which.side, s32[2]{0:T(128)S(1)} %pad_add_fusion.place, bf16[1024,512]{1,0:T(8,128)(2,1)S(1)} %bitcast.51, bf16[16,80,512]{2,1,0:T(8,128)(2,1)S(1)} %all-to-all-done.1.keep, ...), custom_call_target="tpu_custom_call" | custom-call | flops 1 | bytes 1 | tf_op jit(solution)/shard_map/project/project/pallas_call | solution.py:345
  81.5 3.7 %collective-permute-start.10 = (bf16[16,32,640]{2,1,0:T(8,128)(2,1)S(1)}, bf16[16,32,640]{2,1,0:T(8,128)(2,1)S(1)}, u32[]{:S(2)}, u32[]{:S(2)}) collective-permute-start(bf16[16,32,640]{2,1,0:T(8,128)(2,1)S(1)} %get-tuple-element.73), channel_id=1, source_target_pairs={{0,1},{1,0},{2,3},{3,2},{4,5},{5,4},{6,7},{7,6},{8,9},{9,8},{10,11... | collective-permute-start | bytes 1966088 | tf_op jit(solution)/shard_map/project/ppermute | solution.py:27
  85.8 1.0 collective-permute-start.11
  86.9 1.0 add_convert_fusion
  87.9 4.6 %all-to-all-start.2 = ((bf16[16,32,640]{2,1,0:T(8,128)(2,1)}), bf16[16,32,640]{2,1,0:T(8,128)(2,1)S(1)}, u32[]{:S(2)}, u32[]{:S(2)}) async-start(bf16[16,32,640]{2,1,0:T(8,128)(2,1)} %add_convert_fusion), calls=%async_computation.2 | async-start | bytes 1310720 | tf_op jit(solution)/shard_map/project/all_to_all | solution.py:31
  96.0 15.7 %collective-permute-done.12 = bf16[16,16,128]{2,1,0:T(8,128)(2,1)S(1)} collective-permute-done((bf16[16,16,128]{2,1,0:T(8,128)(2,1)S(1)}, bf16[16,16,128]{2,1,0:T(8,128)(2,1)S(1)}, u32[]{:S(2)}, u32[]{:S(2)}) %collective-permute-start.12) | collective-permute-done | bytes 65568 | tf_op jit(solution)/shard_map/project/ppermute | solution.py:27
  112.8 3.1 %collective-permute-start.13 = (f32[32,640]{1,0:T(8,128)S(1)}, f32[32,640]{1,0:T(8,128)S(1)}, u32[]{:S(2)}, u32[]{:S(2)}) collective-permute-start(f32[32,640]{1,0:T(8,128)S(1)} %convert_reduce_fusion), channel_id=1, source_target_pairs={{0,2},{2,0},{1,3},{3,1},{4,6},{6,4},{5,7},{7,5},{8,10},{10,8},{9,1... | collective-permute-start | bytes 245768 | tf_op jit(solution)/shard_map/project/ppermute | solution.py:27
  116.4 1.4 collective-permute-done.13
  117.7 2.3 %collective-permute-start.15 = (bf16[1024,512]{1,0:T(8,128)(2,1)}, bf16[1024,512]{1,0:T(8,128)(2,1)}, u32[]{:S(2)}, u32[]{:S(2)}) collective-permute-start(bf16[1024,512]{1,0:T(8,128)(2,1)} %collective-permute-done.11.refs_16_), channel_id=1, source_target_pairs={{0,1},{1,0},{2,3},{3,2},{4,5},{5,4},{6,7},{7,6},{8,9},{9,8},{10,11... | collective-permute-start | bytes 3145736 | tf_op jit(solution)/shard_map/coefficients/ppermute | solution.py:27
  121.7 4.5 %all-to-all-start.3 = ((bf16[16,32,640]{2,1,0:T(8,128)(2,1)}), bf16[16,32,640]{2,1,0:T(8,128)(2,1)S(1)}, u32[]{:S(2)}, u32[]{:S(2)}) async-start(bf16[16,32,640]{2,1,0:T(8,128)(2,1)} %broadcast_in_dim.6), calls=%async_computation.3 | async-start | bytes 1310720 | tf_op jit(solution)/shard_map/coefficients/all_to_all | solution.py:31
  127.6 1.9 collective-permute-start.20
  130.9 9.5 %collective-permute-done.19.refs_12_ = bf16[512,512]{1,0:T(8,128)(2,1)S(1)} collective-permute-done((bf16[512,512]{1,0:T(8,128)(2,1)S(1)}, bf16[512,512]{1,0:T(8,128)(2,1)S(1)}, u32[]{:S(2)}, u32[]{:S(2)}) %collective-permute-start.19) | collective-permute-done | bytes 524320 | tf_op jit(solution)/shard_map/coefficients/ppermute | solution.py:27
  140.4 1.7 collective-permute-done.20.refs_8_
  142.1 4.3 %all-to-all-done.3.mine = bf16[16,32,640]{2,1,0:T(8,128)(2,1)S(1)} async-done(((bf16[16,32,640]{2,1,0:T(8,128)(2,1)}), bf16[16,32,640]{2,1,0:T(8,128)(2,1)S(1)}, u32[]{:S(2)}, u32[]{:S(2)}) %all-to-all-start.3) | async-done | bytes 655392 | tf_op jit(solution)/shard_map/coefficients/all_to_all | solution.py:31
  146.4 1.1 collective-permute-start.21
  148.2 1.0 collective-permute-done.21.theirs
  150.0 5.2 %expand.1 = (bf16[1024,512]{1,0:T(8,128)(2,1)}, bf16[512,512]{1,0:T(8,128)(2,1)}, bf16[16,64,1024]{2,1,0:T(8,128)(2,1)}) custom-call(s32[2]{0:T(128)} %copy-done.4, bf16[16,32,640]{2,1,0:T(8,128)(2,1)} %copy-done.7, bf16[16,32,640]{2,1,0:T(8,128)(2,1)} %copy-done.12, bf16[2,128,512]{2,1,0:T(8,128)(2,1)} %bitcast.61, bf16[2,128,512]{2,1,0:T(8,128)(2,1)} %bitcast.60, ...), custom_call_target="tpu_custom_call" | custom-call | flops 1610612736 | bytes 6291456 | tf_op jit(solution)/shard_map/coefficients/expand/pallas_call | solution.py:405
  155.2 4.4 %all-to-all-start.4 = ((bf16[16,64,1024]{2,1,0:T(8,128)(2,1)}), bf16[16,64,1024]{2,1,0:T(8,128)(2,1)}, u32[]{:S(2)}, u32[]{:S(2)}) async-start(bf16[16,64,1024]{2,1,0:T(8,128)(2,1)} %get-tuple-element.89), calls=%async_computation.4 | async-start | bytes 4194304 | tf_op jit(solution)/shard_map/transpose_out/all_to_all | solution.py:31
  163.6 23.3 %density.1 = f32[1024,4,512]{2,1,0:T(4,128)} custom-call(s32[2]{0:T(128)} %copy-done.4, bf16[16,160,1024]{2,1,0:T(8,128)(2,1)} %bitcast.62, bf16[16,160,1024]{2,1,0:T(8,128)(2,1)} %bitcast.63, bf16[1024,512]{1,0:T(8,128)(2,1)} %get-tuple-element.91.refs_0_, bf16[512,512]{1,0:T(8,128)(2,1)} %copy-done.16, bf16[512,512]{1,0:T(8,128)(2,1)} %collective-permute-done.23.refs_2_, ...), custom_call_target="tpu_custom_call" | custom-call | flops 12884901888 | bytes 29360128 | tf_op jit(solution)/shard_map/density/density/pallas_call | solution.py:499
  186.9 5.9 %all-to-all-done.4.update = bf16[16,64,1024]{2,1,0:T(8,128)(2,1)} async-done(((bf16[16,64,1024]{2,1,0:T(8,128)(2,1)}), bf16[16,64,1024]{2,1,0:T(8,128)(2,1)}, u32[]{:S(2)}, u32[]{:S(2)}) %all-to-all-start.4) | async-done | bytes 2097184 | tf_op jit(solution)/shard_map/transpose_out/all_to_all | solution.py:31
  192.8 4.8 %subtract_update.1 = f32[64,16384]{1,0:T(8,128)} custom-call(f32[64,16384]{1,0:T(8,128)} %orbs.5, bf16[16,64,1024]{2,1,0:T(8,128)(2,1)} %all-to-all-done.4.update), custom_call_target="tpu_custom_call" | custom-call | flops 1048576 | bytes 10485760 | tf_op jit(solution)/shard_map/subtract/subtract_update/pallas_call | solution.py:299
  (115 shorter events, 23.9 us)
Async XLA Ops:
  7.2 63.6 %copy-start = (f32[256,256]{1,0:T(8,128)S(1)}, f32[256,256]{1,0:T(8,128)}, u32[]{:S(2)}) copy-start(f32[256,256]{1,0:T(8,128)} %param.14) | copy-start | bytes 786436
  10.4 34.1 %all-to-all-start = ((bf16[16,96,512]{2,1,0:T(8,128)(2,1)}), bf16[16,96,512]{2,1,0:T(8,128)(2,1)S(1)}, u32[]{:S(2)}, u32[]{:S(2)}) async-start(bf16[16,96,512]{2,1,0:T(8,128)(2,1)} %pack_vectors.1), calls=%async_computation | async-start | bytes 3145728 | tf_op jit(solution)/shard_map/transpose_give/all_to_all | solution.py:31
  20.7 16.7 %copy-start.11 = (f32[64]{0:T(128)S(1)}, f32[64]{0:T(128)}, u32[]{:S(2)}) copy-start(f32[64]{0:T(128)} %param.15) | copy-start | bytes 772
  23.3 4.4 %collective-permute-start = (bf16[80,1024]{1,0:T(8,128)(2,1)S(1)}, bf16[80,1024]{1,0:T(8,128)(2,1)S(1)}, u32[]{:S(2)}, u32[]{:S(2)}) collective-permute-start(bf16[80,1024]{1,0:T(8,128)(2,1)S(1)} %get-tuple-element.138), channel_id=1, source_target_pairs={{0,1},{1,0},{2,3},{3,2},{4,5},{5,4},{6,7},{7,6},{8,9},{9,8},{10,11... | collective-permute-start | bytes 491528 | tf_op jit(solution)/shard_map/window_exchange/ppermute | solution.py:27
  24.4 7.3 %collective-permute-start.1 = (bf16[80,1024]{1,0:T(8,128)(2,1)S(1)}, bf16[80,1024]{1,0:T(8,128)(2,1)S(1)}, u32[]{:S(2)}, u32[]{:S(2)}) collective-permute-start(bf16[80,1024]{1,0:T(8,128)(2,1)S(1)} %get-tuple-element.137), channel_id=1, source_target_pairs={{0,2},{2,0},{1,3},{3,1},{4,6},{6,4},{5,7},{7,5},{8,10},{10,8},{9,1... | collective-permute-start | bytes 491528 | tf_op jit(solution)/shard_map/window_exchange/ppermute | solution.py:27
  27.4 8.3 %collective-permute-start.2 = (bf16[80,1024]{1,0:T(8,128)(2,1)S(1)}, bf16[80,1024]{1,0:T(8,128)(2,1)S(1)}, u32[]{:S(2)}, u32[]{:S(2)}) collective-permute-start(bf16[80,1024]{1,0:T(8,128)(2,1)S(1)} %get-tuple-element.136), channel_id=1, source_target_pairs={{0,3},{1,2},{2,1},{3,0},{4,7},{5,6},{6,5},{7,4},{8,11},{9,10},{10,... | collective-permute-start | bytes 491528 | tf_op jit(solution)/shard_map/window_exchange/ppermute | solution.py:88
  36.1 6.0 %collective-permute-start.3 = (bf16[80,1024]{1,0:T(8,128)(2,1)S(1)}, bf16[80,1024]{1,0:T(8,128)(2,1)}, u32[]{:S(2)}, u32[]{:S(2)}) collective-permute-start(bf16[80,1024]{1,0:T(8,128)(2,1)S(1)} %fusion.29), channel_id=1, source_target_pairs={{0,4},{4,0},{1,5},{5,1},{2,6},{6,2},{3,7},{7,3},{8,12},{12,8},{9,1... | collective-permute-start | bytes 491528 | tf_op jit(solution)/shard_map/window_exchange/ppermute | solution.py:27
  44.5 4.9 %copy-start.5 = (bf16[16,96,512]{2,1,0:T(8,128)(2,1)}, bf16[16,96,512]{2,1,0:T(8,128)(2,1)S(1)}, u32[]{:S(2)}) copy-start(bf16[16,96,512]{2,1,0:T(8,128)(2,1)S(1)} %all-to-all-done) | copy-start | bytes 4718596
  45.7 16.3 %collective-permute-start.4 = (bf16[512,512]{1,0:T(8,128)(2,1)}, bf16[512,512]{1,0:T(8,128)(2,1)}, u32[]{:S(2)}, u32[]{:S(2)}) collective-permute-start(bf16[512,512]{1,0:T(8,128)(2,1)} %bitcast.11), channel_id=1, source_target_pairs={{0,6},{2,4},{4,2},{6,0},{1,7},{3,5},{5,3},{7,1},{8,14},{10,12},{12... | collective-permute-start | bytes 1572872 | tf_op jit(solution)/shard_map/transpose_keep/ppermute | solution.py:107
  49.3 9.6 %collective-permute-start.5 = (bf16[16,16,512]{2,1,0:T(8,128)(2,1)}, bf16[16,16,512]{2,1,0:T(8,128)(2,1)S(1)}, u32[]{:S(2)}, u32[]{:S(2)}) collective-permute-start(bf16[16,16,512]{2,1,0:T(8,128)(2,1)} %get-tuple-element.121), channel_id=1, source_target_pairs={{0,4},{4,0},{1,5},{5,1},{2,6},{6,2},{3,7},{7,3},{8,12},{12,8},{9,1... | collective-permute-start | bytes 786440 | tf_op jit(solution)/shard_map/transpose_keep/ppermute | solution.py:27
  49.3 12.7 %collective-permute-start.6 = (bf16[16,16,512]{2,1,0:T(8,128)(2,1)}, bf16[16,16,512]{2,1,0:T(8,128)(2,1)S(1)}, u32[]{:S(2)}, u32[]{:S(2)}) collective-permute-start(bf16[16,16,512]{2,1,0:T(8,128)(2,1)} %get-tuple-element.120), channel_id=1, source_target_pairs={{0,4},{4,0},{1,5},{5,1},{2,6},{6,2},{3,7},{7,3},{8,12},{12,8},{9,1... | collective-permute-start | bytes 786440 | tf_op jit(solution)/shard_map/transpose_keep/ppermute | solution.py:27
  52.1 24.5 %all-to-all-start.1 = ((bf16[16,80,512]{2,1,0:T(8,128)(2,1)}), bf16[16,80,512]{2,1,0:T(8,128)(2,1)S(1)}, u32[]{:S(2)}, u32[]{:S(2)}) async-start(bf16[16,80,512]{2,1,0:T(8,128)(2,1)} %pack_weights.1), calls=%async_computation.1 | async-start | bytes 2621440 | tf_op jit(solution)/shard_map/transpose_keep/all_to_all | solution.py:31
  58.8 104.8 %all-gather.3.cloned.1.call-start = ((), (), s32[]{:S(2)}) async-start(), calls=%async_computation.5 | async-start | bytes 5570560 | tf_op jit(solution)/shard_map/transpose_keep/all_gather | solution.py:138
  58.8 14.9 %collective-permute-start.8 = (bf16[512,512]{1,0:T(8,128)(2,1)}, bf16[512,512]{1,0:T(8,128)(2,1)S(1)}, u32[]{:S(2)}, u32[]{:S(2)}) collective-permute-start(bf16[512,512]{1,0:T(8,128)(2,1)} %bitcast.12), channel_id=1, source_target_pairs={{0,6},{2,4},{4,2},{6,0},{1,7},{3,5},{5,3},{7,1},{8,14},{10,12},{12... | collective-permute-start | bytes 1572872 | tf_op jit(solution)/shard_map/transpose_keep/ppermute | solution.py:108
  62.9 11.5 %collective-permute-start.7 = (bf16[512,512]{1,0:T(8,128)(2,1)S(1)}, bf16[512,512]{1,0:T(8,128)(2,1)S(1)}, u32[]{:S(2)}, u32[]{:S(2)}) collective-permute-start(bf16[512,512]{1,0:T(8,128)(2,1)S(1)} %get-tuple-element.125), channel_id=1, source_target_pairs={{0,4},{4,0},{1,5},{5,1},{2,6},{6,2},{3,7},{7,3},{8,12},{12,8},{9,1... | collective-permute-start | bytes 1572872 | tf_op jit(solution)/shard_map/transpose_keep/ppermute | solution.py:27
  65.5 4.1 %copy-start.8 = (bf16[512,512]{1,0:T(8,128)(2,1)}, bf16[512,512]{1,0:T(8,128)(2,1)S(1)}, u32[]{:S(2)}) copy-start(bf16[512,512]{1,0:T(8,128)(2,1)S(1)} %get-tuple-element.95.refs_6_) | copy-start | bytes 1572868
  65.5 9.9 %collective-permute-start.9 = (bf16[512,512]{1,0:T(8,128)(2,1)S(1)}, bf16[512,512]{1,0:T(8,128)(2,1)}, u32[]{:S(2)}, u32[]{:S(2)}) collective-permute-start(bf16[512,512]{1,0:T(8,128)(2,1)S(1)} %get-tuple-element.95.refs_6_), channel_id=1, source_target_pairs={{0,1},{1,0},{2,3},{3,2},{4,5},{5,4},{6,7},{7,6},{8,9},{9,8},{10,11... | collective-permute-start | bytes 1572872 | tf_op jit(solution)/shard_map/transpose_keep/ppermute | solution.py:27
  67.5 2.0 copy-start.10
  72.1 4.6 %copy-start.3 = (bf16[2,256,512]{2,1,0:T(8,128)(2,1)S(1)}, bf16[2,256,512]{2,1,0:T(8,128)(2,1)}, u32[]{:S(2)}) copy-start(bf16[2,256,512]{2,1,0:T(8,128)(2,1)} %fusion.4.vec_two) | copy-start | bytes 1572868
  76.7 1.2 copy-start.2
  77.9 3.5 %copy-start.4 = (s32[2]{0:T(128)}, s32[2]{0:T(128)S(1)}, u32[]{:S(2)}) copy-start(s32[2]{0:T(128)S(1)} %pad_add_fusion.place) | copy-start | bytes 28
  81.5 5.4 %collective-permute-start.10 = (bf16[16,32,640]{2,1,0:T(8,128)(2,1)S(1)}, bf16[16,32,640]{2,1,0:T(8,128)(2,1)S(1)}, u32[]{:S(2)}, u32[]{:S(2)}) collective-permute-start(bf16[16,32,640]{2,1,0:T(8,128)(2,1)S(1)} %get-tuple-element.73), channel_id=1, source_target_pairs={{0,1},{1,0},{2,3},{3,2},{4,5},{5,4},{6,7},{7,6},{8,9},{9,8},{10,11... | collective-permute-start | bytes 1966088 | tf_op jit(solution)/shard_map/project/ppermute | solution.py:27
  85.8 26.9 %collective-permute-start.11 = (bf16[1024,512]{1,0:T(8,128)(2,1)}, bf16[1024,512]{1,0:T(8,128)(2,1)}, u32[]{:S(2)}, u32[]{:S(2)}) collective-permute-start(bf16[1024,512]{1,0:T(8,128)(2,1)} %bitcast.23.refs_10_), channel_id=1, source_target_pairs={{0,2},{2,0},{1,3},{3,1},{4,6},{6,4},{5,7},{7,5},{8,10},{10,8},{9,1... | collective-permute-start | bytes 3145736 | tf_op jit(solution)/shard_map/project/ppermute | solution.py:27
  87.9 32.1 %copy-start.6 = (f32[512,512]{1,0:T(8,128)S(1)}, f32[512,512]{1,0:T(8,128)}, u32[]{:S(2)}) copy-start(f32[512,512]{1,0:T(8,128)} %convolution_add_fusion) | copy-start | bytes 3145732
  87.9 24.8 %all-to-all-start.2 = ((bf16[16,32,640]{2,1,0:T(8,128)(2,1)}), bf16[16,32,640]{2,1,0:T(8,128)(2,1)S(1)}, u32[]{:S(2)}, u32[]{:S(2)}) async-start(bf16[16,32,640]{2,1,0:T(8,128)(2,1)} %add_convert_fusion), calls=%async_computation.2 | async-start | bytes 1310720 | tf_op jit(solution)/shard_map/project/all_to_all | solution.py:31
  93.8 33.2 %collective-permute-start.17 = (bf16[512,512]{1,0:T(8,128)(2,1)}, bf16[512,512]{1,0:T(8,128)(2,1)}, u32[]{:S(2)}, u32[]{:S(2)}) collective-permute-start(bf16[512,512]{1,0:T(8,128)(2,1)} %collective-permute-done.4.refs_17_), channel_id=1, source_target_pairs={{0,1},{1,0},{2,3},{3,2},{4,5},{5,4},{6,7},{7,6},{8,9},{9,8},{10,11... | collective-permute-start | bytes 1572872 | tf_op jit(solution)/shard_map/coefficients/ppermute | solution.py:27
  94.5 36.3 %collective-permute-start.14 = (bf16[1024,512]{1,0:T(8,128)(2,1)}, bf16[1024,512]{1,0:T(8,128)(2,1)}, u32[]{:S(2)}, u32[]{:S(2)}) collective-permute-start(bf16[1024,512]{1,0:T(8,128)(2,1)} %bitcast.23.refs_10_), channel_id=1, source_target_pairs={{0,1},{1,0},{2,3},{3,2},{4,5},{5,4},{6,7},{7,6},{8,9},{9,8},{10,11... | collective-permute-start | bytes 3145736 | tf_op jit(solution)/shard_map/coefficients/ppermute | solution.py:27
  94.6 17.1 %collective-permute-start.12 = (bf16[16,16,128]{2,1,0:T(8,128)(2,1)S(1)}, bf16[16,16,128]{2,1,0:T(8,128)(2,1)S(1)}, u32[]{:S(2)}, u32[]{:S(2)}) collective-permute-start(bf16[16,16,128]{2,1,0:T(8,128)(2,1)S(1)} %slice.115), channel_id=1, source_target_pairs={{0,4},{4,0},{1,5},{5,1},{2,6},{6,2},{3,7},{7,3},{8,12},{12,8},{9,1... | collective-permute-start | bytes 196616 | tf_op jit(solution)/shard_map/project/ppermute | solution.py:27
  95.2 32.4 %collective-permute-start.16 = (bf16[512,512]{1,0:T(8,128)(2,1)}, bf16[512,512]{1,0:T(8,128)(2,1)}, u32[]{:S(2)}, u32[]{:S(2)}) collective-permute-start(bf16[512,512]{1,0:T(8,128)(2,1)} %copy-done.14), channel_id=1, source_target_pairs={{0,1},{1,0},{2,3},{3,2},{4,5},{5,4},{6,7},{7,6},{8,9},{9,8},{10,11... | collective-permute-start | bytes 1572872 | tf_op jit(solution)/shard_map/coefficients/ppermute | solution.py:27
  111.7 19.2 %collective-permute-start.18 = (bf16[512,512]{1,0:T(8,128)(2,1)}, bf16[512,512]{1,0:T(8,128)(2,1)}, u32[]{:S(2)}, u32[]{:S(2)}) collective-permute-start(bf16[512,512]{1,0:T(8,128)(2,1)} %copy-done.13), channel_id=1, source_target_pairs={{0,1},{1,0},{2,3},{3,2},{4,5},{5,4},{6,7},{7,6},{8,9},{9,8},{10,11... | collective-permute-start | bytes 1572872 | tf_op jit(solution)/shard_map/coefficients/ppermute | solution.py:27
  112.8 4.9 %collective-permute-start.13 = (f32[32,640]{1,0:T(8,128)S(1)}, f32[32,640]{1,0:T(8,128)S(1)}, u32[]{:S(2)}, u32[]{:S(2)}) collective-permute-start(f32[32,640]{1,0:T(8,128)S(1)} %convert_reduce_fusion), channel_id=1, source_target_pairs={{0,2},{2,0},{1,3},{3,1},{4,6},{6,4},{5,7},{7,5},{8,10},{10,8},{9,1... | collective-permute-start | bytes 245768 | tf_op jit(solution)/shard_map/project/ppermute | solution.py:27
  117.7 28.6 %collective-permute-start.15 = (bf16[1024,512]{1,0:T(8,128)(2,1)}, bf16[1024,512]{1,0:T(8,128)(2,1)}, u32[]{:S(2)}, u32[]{:S(2)}) collective-permute-start(bf16[1024,512]{1,0:T(8,128)(2,1)} %collective-permute-done.11.refs_16_), channel_id=1, source_target_pairs={{0,1},{1,0},{2,3},{3,2},{4,5},{5,4},{6,7},{7,6},{8,9},{9,8},{10,11... | collective-permute-start | bytes 3145736 | tf_op jit(solution)/shard_map/coefficients/ppermute | solution.py:27
  120.8 6.3 %copy-start.9 = (bf16[512,512]{1,0:T(8,128)(2,1)S(1)}, bf16[512,512]{1,0:T(8,128)(2,1)}, u32[]{:S(2)}) copy-start(bf16[512,512]{1,0:T(8,128)(2,1)} %get-tuple-element.82) | copy-start | bytes 1572868
  121.7 24.7 %all-to-all-start.3 = ((bf16[16,32,640]{2,1,0:T(8,128)(2,1)}), bf16[16,32,640]{2,1,0:T(8,128)(2,1)S(1)}, u32[]{:S(2)}, u32[]{:S(2)}) async-start(bf16[16,32,640]{2,1,0:T(8,128)(2,1)} %broadcast_in_dim.6), calls=%async_computation.3 | async-start | bytes 1310720 | tf_op jit(solution)/shard_map/coefficients/all_to_all | solution.py:31
  127.0 13.3 %collective-permute-start.19 = (bf16[512,512]{1,0:T(8,128)(2,1)S(1)}, bf16[512,512]{1,0:T(8,128)(2,1)S(1)}, u32[]{:S(2)}, u32[]{:S(2)}) collective-permute-start(bf16[512,512]{1,0:T(8,128)(2,1)S(1)} %copy-done.9), channel_id=1, source_target_pairs={{0,4},{4,0},{1,5},{5,1},{2,6},{6,2},{3,7},{7,3},{8,12},{12,8},{9,1... | collective-permute-start | bytes 1572872 | tf_op jit(solution)/shard_map/coefficients/ppermute | solution.py:27
  127.6 14.4 %collective-permute-start.20 = (bf16[512,512]{1,0:T(8,128)(2,1)}, bf16[512,512]{1,0:T(8,128)(2,1)}, u32[]{:S(2)}, u32[]{:S(2)}) collective-permute-start(bf16[512,512]{1,0:T(8,128)(2,1)} %get-tuple-element.83), channel_id=1, source_target_pairs={{0,6},{2,4},{4,2},{6,0},{1,7},{3,5},{5,3},{7,1},{8,14},{10,12},{12... | collective-permute-start | bytes 1572872 | tf_op jit(solution)/shard_map/coefficients/ppermute | solution.py:167
  140.4 19.8 %copy-start.15 = (bf16[512,512]{1,0:T(8,128)(2,1)}, bf16[512,512]{1,0:T(8,128)(2,1)S(1)}, u32[]{:S(2)}) copy-start(bf16[512,512]{1,0:T(8,128)(2,1)S(1)} %collective-permute-done.19.refs_12_) | copy-start | bytes 1572868
  146.4 2.9 %copy-start.7 = (bf16[16,32,640]{2,1,0:T(8,128)(2,1)}, bf16[16,32,640]{2,1,0:T(8,128)(2,1)S(1)}, u32[]{:S(2)}) copy-start(bf16[16,32,640]{2,1,0:T(8,128)(2,1)S(1)} %all-to-all-done.3.mine) | copy-start | bytes 1966084
  146.4 2.9 %collective-permute-start.21 = (bf16[16,32,640]{2,1,0:T(8,128)(2,1)S(1)}, bf16[16,32,640]{2,1,0:T(8,128)(2,1)S(1)}, u32[]{:S(2)}, u32[]{:S(2)}) collective-permute-start(bf16[16,32,640]{2,1,0:T(8,128)(2,1)S(1)} %all-to-all-done.3.mine), channel_id=1, source_target_pairs={{0,1},{1,0},{2,3},{3,2},{4,5},{5,4},{6,7},{7,6},{8,9},{9,8},{10,11... | collective-permute-start | bytes 1966088 | tf_op jit(solution)/shard_map/coefficients/ppermute | solution.py:27
  147.5 13.6 %collective-permute-start.22 = (bf16[512,512]{1,0:T(8,128)(2,1)S(1)}, bf16[512,512]{1,0:T(8,128)(2,1)S(1)}, u32[]{:S(2)}, u32[]{:S(2)}) collective-permute-start(bf16[512,512]{1,0:T(8,128)(2,1)S(1)} %bitcast.58), channel_id=1, source_target_pairs={{0,4},{4,0},{1,5},{5,1},{2,6},{6,2},{3,7},{7,3},{8,12},{12,8},{9,1... | collective-permute-start | bytes 1572872 | tf_op jit(solution)/shard_map/coefficients/ppermute | solution.py:27
  149.2 0.8 copy-start.12
  155.2 37.6 %all-to-all-start.4 = ((bf16[16,64,1024]{2,1,0:T(8,128)(2,1)}), bf16[16,64,1024]{2,1,0:T(8,128)(2,1)}, u32[]{:S(2)}, u32[]{:S(2)}) async-start(bf16[16,64,1024]{2,1,0:T(8,128)(2,1)} %get-tuple-element.89), calls=%async_computation.4 | async-start | bytes 4194304 | tf_op jit(solution)/shard_map/transpose_out/all_to_all | solution.py:31
  159.7 2.3 %collective-permute-start.24 = (bf16[512,512]{1,0:T(8,128)(2,1)}, bf16[512,512]{1,0:T(8,128)(2,1)S(1)}, u32[]{:S(2)}, u32[]{:S(2)}) collective-permute-start(bf16[512,512]{1,0:T(8,128)(2,1)} %collective-permute-done.20.refs_8_), channel_id=1, source_target_pairs={{0,1},{1,0},{2,3},{3,2},{4,5},{5,4},{6,7},{7,6},{8,9},{9,8},{10,11... | collective-permute-start | bytes 1572872 | tf_op jit(solution)/shard_map/density/ppermute | solution.py:27
  160.2 2.3 %collective-permute-start.25 = (bf16[512,512]{1,0:T(8,128)(2,1)S(1)}, bf16[512,512]{1,0:T(8,128)(2,1)S(1)}, u32[]{:S(2)}, u32[]{:S(2)}) collective-permute-start(bf16[512,512]{1,0:T(8,128)(2,1)S(1)} %collective-permute-done.19.refs_12_), channel_id=1, source_target_pairs={{0,1},{1,0},{2,3},{3,2},{4,5},{5,4},{6,7},{7,6},{8,9},{9,8},{10,11... | collective-permute-start | bytes 1572872 | tf_op jit(solution)/shard_map/density/ppermute | solution.py:27
  161.2 2.5 %copy-start.16 = (bf16[512,512]{1,0:T(8,128)(2,1)}, bf16[512,512]{1,0:T(8,128)(2,1)S(1)}, u32[]{:S(2)}) copy-start(bf16[512,512]{1,0:T(8,128)(2,1)S(1)} %collective-permute-done.22.refs_1_) | copy-start | bytes 1572868
  161.2 2.5 %collective-permute-start.23 = (bf16[512,512]{1,0:T(8,128)(2,1)S(1)}, bf16[512,512]{1,0:T(8,128)(2,1)}, u32[]{:S(2)}, u32[]{:S(2)}) collective-permute-start(bf16[512,512]{1,0:T(8,128)(2,1)S(1)} %collective-permute-done.22.refs_1_), channel_id=1, source_target_pairs={{0,1},{1,0},{2,3},{3,2},{4,5},{5,4},{6,7},{7,6},{8,9},{9,8},{10,11... | collective-permute-start | bytes 1572872 | tf_op jit(solution)/shard_map/density/ppermute | solution.py:27
  162.0 1.7 copy-start.17
  192.8 4.8 %copy-start.1 = (f32[256,256]{1,0:T(8,128)S(1)}, f32[256,256]{1,0:T(8,128)}, u32[]{:S(2)}) copy-start(f32[256,256]{1,0:T(8,128)} %param.14) | copy-start | bytes 786436
  (3 other events, 2.4 us)
Sparse Core Ops, SparseCore 0:
  76.7 69.4 all-gather.2
